TPU v7x, 256 devices: a whole 4x4x8 slice. The times are simulated.
256 devices in a mesh: fsdp: 32 (over x, y, core), tensor: 8 (over z).
Axes of the slice: x: 4, y: 4, z: 8, core: 2. Of those that a mesh axis runs over, the one named last changes fastest.
Arguments:
- momentum: float32 [8192, 28672], P('fsdp', 'tensor'), may hold values from -250 to 250
- gradient: bfloat16 [8192, 28672], P('fsdp', 'tensor'), may hold values from -3 to 3
- weight: bfloat16 [8192, 28672], P('fsdp', 'tensor'), may hold values from -6 to 6
- basis: float32 [28672, 256], P(('tensor', 'fsdp')), may hold values from -6 to 6
Outputs:
- new_momentum: float32 [8192, 28672], P('fsdp', 'tensor')
- new_weight: bfloat16 [8192, 28672], P('fsdp', 'tensor')
- new_basis: float32 [28672, 256], P(('tensor', 'fsdp'))
All inputs are finite; a program needn't handle non-finite values.
Results may differ from a plain program's by a relative error of at most 0.001.
Values sent between devices are 32-bit elements; how exact they have to be, the bound alone decides.
No kernel may reach another device: no remote copies, remote signals or barrier semaphores. Data moves between devices by JAX's collectives and lax.ppermute only.
A program may use at most 64 MiB of HBM per device.

v0:
```python
import math

import jax
import jax.numpy as jnp
from jax import lax
from jax.sharding import PartitionSpec as P

keep_rate = 0.95
step_size = 0.25
decay_rate = 0.1


def orthonormalize(proj, gram):
    lower = jnp.linalg.cholesky(gram)
    return lax.linalg.triangular_solve(lower, proj, left_side=False, lower=True, transpose_a=True)


def gram_of(proj):
    return jnp.dot(proj.T, proj, precision=lax.Precision.HIGHEST)


def per_device(momentum, gradient, weight, basis):
    highest = lax.Precision.HIGHEST
    buffer = momentum + gradient.astype(jnp.float32)
    rows_local = buffer.shape[0]
    cols_local = buffer.shape[1]
    partial_value = jnp.dot(
        buffer, lax.all_gather(basis, "fsdp", axis=0, tiled=True), precision=highest
    )
    proj = lax.psum(partial_value, "tensor")
    gram = lax.psum(gram_of(proj), "fsdp")
    ortho = orthonormalize(proj, gram)
    total_cols = cols_local * lax.axis_size("tensor")
    contract = (((0,), (0,)), ((), ()))
    local_back = lax.dot_general(buffer, ortho, contract, precision=highest)
    back = lax.psum(local_back, "fsdp")
    sums = lax.psum(jnp.sum(back * back, axis=0), "tensor")
    rms = jnp.sqrt(sums / total_cols + 1e-06)
    count = cols_local // lax.axis_size("fsdp")
    own = lax.dynamic_slice_in_dim(back, lax.axis_index("fsdp") * count, count, 0)
    new_basis = own / rms
    new_momentum = buffer - (1.0 - keep_rate) * jnp.dot(ortho, back.T, precision=highest)
    columns = back / rms
    update = jnp.dot(ortho, columns.T, precision=highest)
    scale = step_size * math.sqrt(total_cols / (rows_local * lax.axis_size("fsdp")))
    new_weight = (
        (1.0 - step_size * decay_rate) * weight.astype(jnp.float32) - scale * update
    ).astype(jnp.bfloat16)
    return (new_momentum, new_weight, new_basis)


def solution(mesh):
    in_specs = (
        P("fsdp", "tensor"),
        P("fsdp", "tensor"),
        P("fsdp", "tensor"),
        P(("tensor", "fsdp"), None),
    )
    out_specs = (P("fsdp", "tensor"), P("fsdp", "tensor"), P(("tensor", "fsdp"), None))
    return jax.shard_map(
        per_device, mesh=mesh, in_specs=in_specs, out_specs=out_specs, check_vma=False
    )
```

profile of v0, /device:TPU:1, one launch (start us, length us, event | category | flops | bytes accessed | tf_op | source)
XLA Modules:
  0.0 494.8 jit_solution(3055728820711789288)
XLA Ops:
  7.2 0.0 all-gather.2.cloned.1.call-start
  7.2 0.7 all-gather.2.cloned.1.call-update
  7.9 0.0 all-reduce.5.cloned.1.call-start
  7.9 57.5 %all-gather.2.cloned.1.call-done = f32[3584,256]{1,0:T(8,128)} async-done(((f32[112,256]{1,0:T(8,128)}), f32[3584,256]{1,0:T(8,128)}) %all-gather.2.cloned.1.call-update) | async-done | bytes 3670032 | tf_op jit(solution)/shard_map/all_gather | solution.py:28
  65.4 7.8 %fusion.6 = f32[256,256]{1,0:T(8,128)} fusion(f32[3584,256]{1,0:T(8,128)} %all-gather.2.cloned.1.call-done, f32[256,3584]{1,0:T(8,128)} %param.4, bf16[256,3584]{1,0:T(8,128)(2,1)} %param.5), kind=kOutput, calls=%fused_computation.12 | convolution fusion | flops 2820407296 | bytes 9437184 | tf_op jit(solution)/shard_map/dot_general | solution.py:27
  73.2 0.0 copy-start
  73.2 0.0 all-reduce.5.cloned.1.call-update
  73.2 0.0 all-reduce.7.cloned.1.call-start
  73.3 67.1 %all-reduce.5.cloned.1.call-done = f32[256,256]{1,0:T(8,128)} async-done(((f32[256,256]{1,0:T(8,128)}), f32[256,256]{1,0:T(8,128)}) %all-reduce.5.cloned.1.call-update) | async-done | bytes 262160 | tf_op jit(solution)/shard_map/psum | solution.py:30
  140.4 0.0 copy-start.2
  140.4 2.4 fusion.19
  142.7 0.0 all-reduce.7.cloned.1.call-update
  142.8 0.2 all-reduce.9.cloned.1.call-start
  143.0 115.8 %all-reduce.7.cloned.1.call-done = f32[256,256]{0,1:T(8,128)} async-done(((f32[256,256]{0,1:T(8,128)}), f32[256,256]{0,1:T(8,128)}) %all-reduce.7.cloned.1.call-update) | async-done | bytes 262160 | tf_op jit(solution)/shard_map/psum | solution.py:31
  258.8 1.1 copy.8
  259.9 1.0 fusion.7
  260.9 11.7 %cholesky.50 = f32[128,128]{1,0:T(8,128)S(1)} custom-call(f32[128,128]{1,0:T(8,128)S(1)} %cholesky.118), custom_call_target="Cholesky" | custom-call | tf_op jit(solution)/shard_map/jit(cholesky)/cholesky | solution.py:14
  272.7 9.8 %custom-call.14 = f32[1,128,128]{1,2,0:T(8,128)S(1)} custom-call(f32[1,128,128]{2,1,0:T(8,128)S(1)} %get-tuple-element.24), custom_call_target="InvertDiagBlocksLowerTriangular" | custom-call | tf_op jit(solution)/shard_map/jit(cholesky)/cholesky | solution.py:14
  282.5 0.2 constant_dynamic-update-slice_fusion
  282.7 0.3 convolution_subtract_fusion.1
  283.0 11.7 %cholesky.105 = f32[128,128]{1,0:T(8,128)S(1)} custom-call(f32[128,128]{1,0:T(8,128)S(1)} %convolution_subtract_fusion.1), custom_call_target="Cholesky" | custom-call | tf_op jit(solution)/shard_map/jit(cholesky)/cholesky | solution.py:14
  294.7 0.6 compare_reduce_fusion
  296.7 0.1 triangular_solve.58
  296.8 4.2 while.1
  297.0 0.6 fusion.29
  297.5 1.4 bitcast_dynamic-update-slice_fusion.2
  299.0 0.6 fusion.29
  299.5 1.4 bitcast_dynamic-update-slice_fusion.2
  300.9 19.7 %custom-call.15 = f32[2,128,128]{1,2,0:T(8,128)S(1)} custom-call(f32[2,128,128]{2,1,0:T(8,128)S(1)} %get-tuple-element.10), custom_call_target="InvertDiagBlocksLowerTriangular" | custom-call | tf_op jit(solution)/shard_map/triangular_solve | solution.py:15
  320.6 0.0 copy-done.2
  320.6 0.3 fusion.8
  321.0 0.4 convolution_subtract_fusion
  321.3 0.3 fusion.10
  321.7 0.0 copy-done
  321.7 9.8 %fusion.5 = f32[3584,256]{1,0:T(8,128)} fusion(f32[256,3584]{1,0:T(8,128)} %param.4, bf16[256,3584]{1,0:T(8,128)(2,1)S(1)} %copy-done, f32[256,128]{0,1:T(8,128)S(1)} %fusion.10, f32[256,128]{0,1:T(8,128)S(1)} %fusion.8), kind=kOutput, calls=%fused_computation.11 | convolution fusion | flops 2820472832 | bytes 9437184 | tf_op jit(solution)/shard_map/dot_general | solution.py:35
  331.4 0.0 all-reduce.9.cloned.1.call-update
  331.5 120.6 %all-reduce.9.cloned.1.call-done = f32[3584,256]{1,0:T(8,128)} async-done(((f32[3584,256]{1,0:T(8,128)}), f32[3584,256]{1,0:T(8,128)}) %all-reduce.9.cloned.1.call-update) | async-done | bytes 3670032 | tf_op jit(solution)/shard_map/psum | solution.py:36
  452.1 2.5 multiply_reduce_fusion
  454.6 13.7 %psum.31 = f32[256]{0:T(256)S(1)} all-reduce(f32[256]{0:T(256)S(1)} %multiply_reduce_fusion), channel_id=1, replica_groups=mesh['fsdp'=32,'tensor'=8] {'tensor'}, use_global_device_ids=true, to_apply=%region_8.9 | all-reduce | flops 256 | bytes 2048 | tf_op jit(solution)/shard_map/psum | solution.py:37
  468.3 0.0 copy-start.1
  468.3 0.0 copy-start.3
  468.3 12.0 %fusion.1 = f32[256,3584]{1,0:T(8,128)} fusion(f32[3584,256]{1,0:T(8,128)} %all-reduce.9.cloned.1.call-done, f32[256,3584]{1,0:T(8,128)} %param.4, bf16[256,3584]{1,0:T(8,128)(2,1)S(1)} %copy-done, f32[256,128]{0,1:T(8,128)S(1)} %fusion.10, f32[256,128]{0,1:T(8,128)S(1)} %fusion.8), kind=kOutput, calls=%fused_computation.5 | convolution fusion | flops 2822307840 | bytes 13107200 | tf_op jit(solution)/shard_map/dot_general | solution.py:42
  480.4 0.0 copy-done.1
  480.4 0.0 copy-done.3
  480.4 7.2 %fusion.2 = bf16[256,3584]{1,0:T(8,128)(2,1)} fusion(f32[3584,256]{1,0:T(8,128)S(1)} %copy-done.1, bf16[256,3584]{1,0:T(8,128)(2,1)S(1)} %copy-done.3, f32[256]{0:T(256)S(1)} %add_sqrt_fusion, f32[256,128]{0,1:T(8,128)S(1)} %fusion.10, f32[256,128]{0,1:T(8,128)S(1)} %fusion.8), kind=kOutput, calls=%fused_computation.6 | convolution fusion | flops 2824142848 | bytes 7603200 | tf_op jit(solution)/shard_map/dot_general | solution.py:44
  487.6 0.7 dynamic-slice_divide_fusion
  (10 shorter events, 0.2 us)
Async XLA Ops:
  7.2 58.2 %all-gather.2.cloned.1.call-start = ((), (), s32[]{:S(2)}) async-start(), calls=%async_computation | async-start | bytes 3784704 | tf_op jit(solution)/shard_map/all_gather | solution.py:28
  7.9 132.5 %all-reduce.5.cloned.1.call-start = ((), (), s32[]{:S(2)}) async-start(), calls=%async_computation.1 | async-start | bytes 524288 | tf_op jit(solution)/shard_map/psum | solution.py:30
  73.2 248.5 %copy-start = (bf16[256,3584]{1,0:T(8,128)(2,1)S(1)}, bf16[256,3584]{1,0:T(8,128)(2,1)}, u32[]{:S(2)}) copy-start(bf16[256,3584]{1,0:T(8,128)(2,1)} %param.5) | copy-start | bytes 5505028
  73.2 185.6 %all-reduce.7.cloned.1.call-start = ((), (), s32[]{:S(2)}) async-start(), calls=%async_computation.2 | async-start | bytes 524288 | tf_op jit(solution)/shard_map/psum | solution.py:31
  140.4 180.3 %copy-start.2 = (f32[256,256]{1,0:T(8,128)S(1)}, f32[256,256]{1,0:T(8,128)}, u32[]{:S(2)}) copy-start(f32[256,256]{1,0:T(8,128)} %all-reduce.5.cloned.1.call-done) | copy-start | bytes 786436
  142.8 309.3 %all-reduce.9.cloned.1.call-start = ((), (), s32[]{:S(2)}) async-start(), calls=%async_computation.3 | async-start | bytes 7340032 | tf_op jit(solution)/shard_map/psum | solution.py:36
  468.3 12.0 %copy-start.1 = (f32[3584,256]{1,0:T(8,128)S(1)}, f32[3584,256]{1,0:T(8,128)}, u32[]{:S(2)}) copy-start(f32[3584,256]{1,0:T(8,128)} %all-reduce.9.cloned.1.call-done) | copy-start | bytes 11010052
  468.3 12.0 %copy-start.3 = (bf16[256,3584]{1,0:T(8,128)(2,1)S(1)}, bf16[256,3584]{1,0:T(8,128)(2,1)}, u32[]{:S(2)}) copy-start(bf16[256,3584]{1,0:T(8,128)(2,1)} %param.6) | copy-start | bytes 5505028
Sparse Core Ops, SparseCore 0:
  10.5 54.8 all-gather.1
  73.3 66.9 all-reduce.4
  144.5 114.2 all-reduce.6
  331.6 120.4 all-reduce.8
where the time goes:
time: 499 us; the launch traced here: 495 us
  waiting for transfers between devices  362 us (73%)
  other arithmetic  57.8 us (12%)
  matrix products  40.6 us (8%)
  between operations  15.2 us (3%)
  blocking collectives  13.7 us (3%)
  local copies, waits for them, and re-layouts  5.14 us (1%)
    psum x1, waiting for transfers between devices, per_device(): back = lax.psum(local_back, 'fsdp')  121 us
    psum x1, waiting for transfers between devices, per_device(): gram = lax.psum(gram_of(proj), 'fsdp')  116 us
    psum x1, waiting for transfers between devices, per_device(): proj = lax.psum(partial_value, 'tensor')  67.1 us
    all_gather x1, waiting for transfers between devices, per_device(): lax.all_gather(basis, 'fsdp', axis=0, tiled=True)  57.5 us
    another operation x6, other arithmetic, orthonormalize(): lower = jnp.linalg.cholesky(gram)  33.9 us
    another operation x3, other arithmetic, orthonormalize(): lax.linalg.triangular_solve(lower, proj, left_side=False, lower=True, tra...  19.7 us
    psum x1, blocking collectives, per_device(): sums = lax.psum(jnp.sum(back * back, axis=0), 'tensor')  13.7 us
    dot_general x1, matrix products, per_device(): jnp.dot(ortho, back.T, precision=highest)  12 us
  transfers between devices with their start and end apart: 4, of which 4 were waited for; matrix products, arithmetic and copies ran while one was open for 0% of the time, Pallas kernels for 0%

commit v1 on v0

v1 whole, which is shorter than its diff:
```python
import math

import jax
import jax.numpy as jnp
from jax import lax
from jax.experimental import pallas as pl
from jax.experimental.pallas import tpu as pltpu
from jax.sharding import Mesh, PartitionSpec as P

keep_rate = 0.95
step_size = 0.25
decay_rate = 0.1

F32 = jnp.float32
BF16 = jnp.bfloat16
HIGH = lax.Precision.HIGH
HIGHEST = lax.Precision.HIGHEST
VMEM = pltpu.VMEM


def split(x):
    hi = x.astype(BF16)
    lo = (x - hi.astype(F32)).astype(BF16)
    return hi, lo


def nt(a, b):
    return lax.dot_general(a, b, (((1,), (1,)), ((), ())), preferred_element_type=F32)


def sort_columns_kernel(core_ref, mom_ref, grad_ref, keep_ref, send_ref, *, count):
    buffer = mom_ref[...] + grad_ref[...].astype(F32)
    chunks = buffer.shape[1] // count
    parts = [
        jnp.concatenate(
            [buffer[:, i * count : (i + 1) * count] for i in range(first, chunks, 2)], axis=1
        )
        for first in range(2)
    ]

    @pl.when(core_ref[0] == 0)
    def _():
        keep_ref[...] = parts[0]
        send_ref[...] = parts[1]

    @pl.when(core_ref[0] == 1)
    def _():
        keep_ref[...] = parts[1]
        send_ref[...] = parts[0]


def sort_columns(core, momentum, gradient, count):
    rows, cols = momentum.shape
    tile = 64
    spec = pl.BlockSpec((tile, cols), lambda i: (i, 0))
    half = pl.BlockSpec((tile, cols // 2), lambda i: (i, 0))
    out = jax.ShapeDtypeStruct((rows, cols // 2), F32)
    return pl.pallas_call(
        lambda *refs: sort_columns_kernel(*refs, count=count),
        grid=(rows // tile,),
        in_specs=[pl.BlockSpec(memory_space=pltpu.SMEM), spec, spec],
        out_specs=[half, half],
        out_shape=[out, out],
        compiler_params=pltpu.CompilerParams(vmem_limit_bytes=40 * 2**20),
        cost_estimate=pl.CostEstimate(flops=rows * cols, bytes_accessed=rows * cols * 10, transcendentals=0),
    )(core, momentum, gradient)


def bc(x):
    return jnp.broadcast_to(x, (8, 128))


def inverse_factor_kernel(g_ref, x_ref, a, w):
    n = g_ref.shape[0]
    a[...] = g_ref[...]
    w[...] = (
        lax.broadcasted_iota(jnp.int32, (n, n), 0) == lax.broadcasted_iota(jnp.int32, (n, n), 1)
    ).astype(F32)
    outer = 128
    for r0 in range(0, n, outer):
        tiles = [(a, t) for t in range(r0, n, 128)] + [(w, t) for t in range(0, r0 + outer, 128)]
        for s in range(outer // 8):
            top = r0 + 8 * s
            below = range(top + 8, r0 + outer, 8)
            cols = [[bc(a[i : i + 8, top + m : top + m + 1]) for m in range(8)] for i in below]
            own = [bc(a[top : top + 8, top + m : top + m + 1]) for m in range(8)]
            e = [[bc(own[j][i : i + 1, :]) if i >= j else None for j in range(8)] for i in range(8)]
            inv = [None] * 8
            for j in range(8):
                inv[j] = lax.rsqrt(e[j][j])
                for i in range(j + 1, 8):
                    e[i][j] = e[i][j] * inv[j]
                for k in range(j + 1, 8):
                    for i in range(k, 8):
                        e[i][k] = e[i][k] - e[i][j] * e[k][j]
            xs = [[None] * 8 for _ in range(8)]
            for i in range(8):
                xs[i][i] = inv[i]
                for j in range(i):
                    total = e[i][j] * xs[j][j]
                    for k in range(j + 1, i):
                        total = total + e[i][k] * xs[k][j]
                    xs[i][j] = -total * inv[i]
            for ref, t in tiles:
                rows = [bc(ref[top + k : top + k + 1, t : t + 128]) for k in range(8)]
                made = []
                for i in range(8):
                    total = xs[i][0] * rows[0]
                    for k in range(1, i + 1):
                        total = total + xs[i][k] * rows[k]
                    made.append(total)
                if len(below):
                    back = []
                    for m in range(8):
                        total = xs[m][m] * made[m]
                        for i in range(m + 1, 8):
                            total = total + xs[i][m] * made[i]
                        back.append(total)
                    for n_at, i in enumerate(below):
                        value = ref[i : i + 8, t : t + 128]
                        for m in range(8):
                            value = value - cols[n_at][m] * back[m]
                        ref[i : i + 8, t : t + 128] = value
                sub = lax.broadcasted_iota(jnp.int32, (8, 128), 0)
                row = made[0]
                for i in range(1, 8):
                    row = jnp.where(sub == i, made[i], row)
                ref[top : top + 8, t : t + 128] = row
        if r0 + outer < n:
            end = r0 + outer
            u = a[r0:end, end:n]
            for ref, lo, hi in ((a, end, n), (w, 0, end)):
                ref[end:n, lo:hi] -= lax.dot_general(
                    u, ref[r0:end, lo:hi], (((0,), (0,)), ((), ())),
                    precision=HIGHEST, preferred_element_type=F32,
                )
    x_ref[...] = w[...]


def inverse_factor(gram):
    n = gram.shape[0]
    return pl.pallas_call(
        inverse_factor_kernel,
        out_shape=jax.ShapeDtypeStruct((n, n), F32),
        in_specs=[pl.BlockSpec(memory_space=VMEM)],
        out_specs=pl.BlockSpec(memory_space=VMEM),
        scratch_shapes=[VMEM((n, n), F32), VMEM((n, n), F32)],
        compiler_params=pltpu.CompilerParams(vmem_limit_bytes=16 * 2**20),
        cost_estimate=pl.CostEstimate(flops=n**3, bytes_accessed=8 * n * n, transcendentals=0),
    )(gram)


def update_kernel(core_ref, mom_ref, grad_ref, weight_ref, m1_ref, m2_ref, own_ref, other_ref,
                  new_mom_ref, new_weight_ref, s_ref, *, count):
    pairs = s_ref.shape[0] // (2 * count)
    for i in range(pairs):
        first = pl.multiple_of((2 * i + core_ref[0]) * count, 8)
        second = pl.multiple_of((2 * i + 1 - core_ref[0]) * count, 8)
        s_ref[pl.ds(first, count), :] = own_ref[i]
        s_ref[pl.ds(second, count), :] = other_ref[i]
    s_hi, s_lo = split(s_ref[...])
    m2_hi, m2_lo = split(m2_ref[...])
    m1_hi = m1_ref[...].astype(BF16)
    buffer = mom_ref[...] + grad_ref[...].astype(F32)
    new_mom_ref[...] = buffer - nt(m1_hi, s_hi)
    update = nt(m2_hi, s_hi) + nt(m2_hi, s_lo) + nt(m2_lo, s_hi)
    new_weight_ref[...] = (
        (1.0 - step_size * decay_rate) * weight_ref[...].astype(F32) - update
    ).astype(BF16)


def updates(core, momentum, gradient, weight, m1, m2, own, other):
    rows, cols = momentum.shape
    chunks, count, rank = own.shape
    tiles = 4
    per = chunks // tiles
    spec = pl.BlockSpec((rows, cols // tiles), lambda i: (0, i))
    whole = pl.BlockSpec((rows, rank), lambda i: (0, 0))
    part = pl.BlockSpec((per, count, rank), lambda i: (i, 0, 0))
    return pl.pallas_call(
        lambda *refs: update_kernel(*refs, count=count),
        grid=(tiles,),
        in_specs=[pl.BlockSpec(memory_space=pltpu.SMEM), spec, spec, spec, whole, whole, part, part],
        out_specs=[spec, spec],
        out_shape=[jax.ShapeDtypeStruct((rows, cols), F32), jax.ShapeDtypeStruct((rows, cols), BF16)],
        scratch_shapes=[VMEM((2 * per * count, rank), F32)],
        compiler_params=pltpu.CompilerParams(vmem_limit_bytes=40 * 2**20),
        cost_estimate=pl.CostEstimate(
            flops=8 * rows * cols * rank, bytes_accessed=rows * cols * 16, transcendentals=0
        ),
    )(core, momentum, gradient, weight, m1, m2, own, other)


def tn(a, b):
    return lax.dot_general(a, b, (((0,), (0,)), ((), ())), precision=HIGH, preferred_element_type=F32)


def across_cores(x):
    return lax.ppermute(x, "c", [(0, 1), (1, 0)])


def gather(x, axes, n):
    spread = jnp.broadcast_to(x[None], (n,) + x.shape)
    return lax.all_to_all(spread, axes, 0, 0)


def per_device(momentum, gradient, weight, basis):
    chips = lax.axis_size("x") * lax.axis_size("y")
    cores = lax.axis_size("c")
    depth = lax.axis_size("z")
    plane = ("x", "y")
    rows, cols = momentum.shape
    count, rank = basis.shape
    total_cols = cols * depth
    total_rows = rows * chips * cores
    core = lax.axis_index("c").astype(jnp.int32).reshape(1)

    keep, send = sort_columns(core, momentum, gradient, count)
    recv = across_cores(send)
    right = gather(basis, plane, chips).reshape(chips * count, rank)

    mine = jnp.dot(keep, right, precision=HIGH)
    theirs = jnp.dot(recv, right, precision=HIGH)
    partial = mine + across_cores(theirs)
    share = rows // depth
    piece = jnp.sum(lax.all_to_all(partial.reshape(depth, share, rank), "z", 0, 0), axis=0)
    proj = gather(piece, "z", depth).reshape(rows, rank)
    proj_other = across_cores(proj)

    raw = tn(keep, proj) + tn(recv, proj_other)
    gram_part = tn(proj, proj) + tn(proj_other, proj_other)
    gram_share = rank // chips
    packed = jnp.concatenate(
        [raw.reshape(chips, count, rank), gram_part.reshape(chips, gram_share, rank)], axis=1
    )
    summed = jnp.sum(lax.all_to_all(packed, plane, 0, 0), axis=0)
    everything = gather(summed, plane, chips)
    half = everything[:, :count]
    gram = everything[:, count:].reshape(rank, rank)
    half_other = across_cores(half)

    inverse = inverse_factor(gram)
    back = lax.dot_general(
        half.reshape(chips * count, rank), inverse, (((1,), (1,)), ((), ())), precision=HIGH
    )
    sums = jnp.sum(back * back, axis=0)
    sums = jnp.sum(
        gather(jnp.broadcast_to(sums[None], (8, rank)), ("c", "z"), cores * depth), axis=0
    )[0]
    rms = jnp.sqrt(sums / total_cols + 1e-06)

    own_back = lax.dot_general(
        summed[:count], inverse, (((1,), (1,)), ((), ())), precision=HIGH
    )
    new_basis = own_back / rms
    ortho = lax.dot_general(proj, inverse, (((1,), (1,)), ((), ())), precision=HIGH)
    scale = step_size * math.sqrt(total_cols / total_rows)
    m1 = jnp.dot((1.0 - keep_rate) * ortho, inverse, precision=HIGH)
    m2 = jnp.dot(scale * ortho / rms, inverse, precision=HIGH)
    new_momentum, new_weight = updates(
        core, momentum, gradient, weight, m1, m2, half, half_other
    )
    return new_momentum, new_weight, new_basis


def solution(mesh):
    fsdp, depth = mesh.devices.shape
    grid = Mesh(mesh.devices.reshape(4, 4, 2, depth), ("x", "y", "c", "z"))
    block = P(("x", "y", "c"), "z")
    rows = P(("z", "x", "y", "c"), None)
    return jax.shard_map(
        per_device, mesh=grid, in_specs=(block, block, block, rows),
        out_specs=(block, block, rows), check_vma=False,
    )
```

time: 499 us -> 181 us (0.36)
  waiting for transfers between devices: 362 us -> 6.79 us
  blocking collectives: 13.7 us -> 121 us
  other arithmetic: 57.8 us -> 0.39 us
  matrix products: 40.6 us -> 8.92 us
  Pallas kernels: 0 us -> 17.7 us
  starting transfers between devices: 0.34 us -> 15.2 us
  between operations: 15.2 us -> 0.85 us
    psum x3 -> x0, waiting for transfers between devices: 303 us -> none  [the longest x1 121 us: per_device(): back = lax.psum(local_back, 'fsdp')]
    all_to_all x0 -> x5, blocking collectives: none -> 121 us  [the longest x3 71.6 us: gather(): return lax.all_to_all(spread, axes, 0, 0)]
    all_gather x1 -> x0, waiting for transfers between devices: 57.5 us -> none  [per_device(): lax.all_gather(basis, 'fsdp', axis=0, tiled=True)]
    another operation x9 -> x0, other arithmetic: 53.7 us -> none  [the longest x6 33.9 us: orthonormalize(): lower = jnp.linalg.cholesky(gram)]
    dot_general x5 -> x11, matrix products: 39.2 us -> 8.92 us  [the longest x4 4.08 us: tn(): lax.dot_general(a, b, (((0,), (0,)), ((), ())), precision=HIGH, preferred...]
    pallas_call x0 -> x3, Pallas kernels: none -> 17.7 us  [the longest x1 9.94 us: inverse_factor(): pl.pallas_call(inverse_factor_kernel, out_shape=jax.ShapeDtypeStruct((n,...]
    psum x1 -> x0, blocking collectives: 13.7 us -> none  [per_device(): sums = lax.psum(jnp.sum(back * back, axis=0), 'tensor')]
    ppermute x0 -> x4, starting transfers between devices: none -> 11.8 us  [across_cores(): return lax.ppermute(x, 'c', [(0, 1), (1, 0)])]
  transfers between devices with their start and end apart: 4 -> 5, of which waited for: 4 -> 2; matrix products, arithmetic and copies ran while one was open for 0% -> 4% of each run, Pallas kernels for 0% -> 6%
where the time goes in v1:
time: 181 us
  blocking collectives  121 us (67%)
  Pallas kernels  17.7 us (10%)
  starting transfers between devices  15.2 us (8%)
  local copies, waits for them, and re-layouts  9.97 us (6%)
  matrix products  8.92 us (5%)
  waiting for transfers between devices  6.79 us (4%)
    all_to_all x3, blocking collectives, gather(): return lax.all_to_all(spread, axes, 0, 0)  71.6 us
    all_to_all x1, blocking collectives, per_device(): summed = jnp.sum(lax.all_to_all(packed, plane, 0, 0), axis=0)  30.1 us
    all_to_all x1, blocking collectives, per_device(): lax.all_to_all(partial.reshape(depth, share, rank), 'z', 0, 0)  19.1 us
    ppermute x4, starting transfers between devices, across_cores(): return lax.ppermute(x, 'c', [(0, 1), (1, 0)])  11.8 us
    pallas_call x1, Pallas kernels, inverse_factor(): pl.pallas_call(inverse_factor_kernel, out_shape=jax.ShapeDtypeStruct((n,...  9.94 us
    unnamed x16, local copies, waits for them, and re-layouts  8.78 us
    all_to_all x1, waiting for transfers between devices, gather(): return lax.all_to_all(spread, axes, 0, 0)  6.66 us
    pallas_call x1, Pallas kernels, updates(): pl.pallas_call(lambda *refs: update_kernel(*refs, count=count), grid=(til...  5.82 us
  transfers between devices with their start and end apart: 5, of which 2 were waited for; matrix products, arithmetic and copies ran while one was open for 4% of the time, Pallas kernels for 6%

profile of v1, /device:TPU:1, one launch (start us, length us, event | category | flops | bytes accessed | tf_op | source)
XLA Modules:
  0.0 180.6 jit_solution(12420624219759531238)
XLA Ops:
  0.6 0.0 copy-start
  0.6 2.0 %copy-done = f32[256,3584]{1,0:T(8,128)S(1)} copy-done((f32[256,3584]{1,0:T(8,128)S(1)}, f32[256,3584]{1,0:T(8,128)}, u32[]{:S(2)}) %copy-start) | copy-done | bytes 3670040
  2.7 0.0 copy-start.2
  2.7 1.5 copy-done.2
  4.2 0.0 copy-start.7
  4.2 1.9 %shard_map.67 = (f32[256,1792]{1,0:T(8,128)S(1)}, f32[256,1792]{1,0:T(8,128)S(1)}) custom-call(s32[1]{0:T(128)} %bitcast.refs_0_, f32[256,3584]{1,0:T(8,128)S(1)} %copy-done, bf16[256,3584]{1,0:T(8,128)(2,1)S(1)} %copy-done.2), custom_call_target="tpu_custom_call" | custom-call | flops 917504 | bytes 9175040 | tf_op jit(solution)/shard_map/pallas_call | solution.py:58
  6.1 3.3 %collective-permute-start = (f32[256,1792]{1,0:T(8,128)S(1)}, f32[256,1792]{1,0:T(8,128)S(1)}, u32[]{:S(2)}, u32[]{:S(2)}) collective-permute-start(f32[256,1792]{1,0:T(8,128)S(1)} %get-tuple-element.8), channel_id=1, source_target_pairs={{0,8},{8,0},{1,9},{9,1},{2,10},{10,2},{3,11},{11,3},{4,12},{12,4},... | collective-permute-start | bytes 5505032 | tf_op jit(solution)/shard_map/ppermute | solution.py:199
  9.4 0.0 copy-done.7
  9.4 0.2 broadcast_in_dim.6
  9.6 29.5 %all_to_all.30 = f32[16,112,256]{2,1,0:T(8,128)S(1)} all-to-all(f32[16,112,256]{2,1,0:T(8,128)S(1)} %broadcast_in_dim.6), channel_id=1, replica_groups=mesh['x'=4,'y'=4,'c'=2,'z'=8] {'x','y'}, dimensions={0} | all-to-all | bytes 3670016 | tf_op jit(solution)/shard_map/all_to_all | solution.py:204
  39.1 0.0 collective-permute-done
  39.1 0.0 copy-start.5
  39.1 1.0 fusion.15
  40.1 0.2 copy-done.5
  40.3 1.6 collective-permute-start.1
  41.9 1.0 fusion.14
  43.0 0.1 collective-permute-done.1
  43.1 19.1 %all_to_all.31 = f32[8,32,256]{2,1,0:T(8,128)S(1)} all-to-all(f32[8,32,256]{2,1,0:T(8,128)S(1)} %bitcast.38), channel_id=1, replica_groups=mesh['x'=4,'y'=4,'c'=2,'z'=8] {'z'}, dimensions={0} | all-to-all | bytes 524288 | tf_op jit(solution)/shard_map/all_to_all | solution.py:226
  62.2 12.1 %all_to_all.32 = f32[8,32,256]{2,1,0:T(8,128)S(1)} all-to-all(f32[8,32,256]{2,1,0:T(8,128)S(1)} %broadcast_in_dim.7), channel_id=1, replica_groups=mesh['x'=4,'y'=4,'c'=2,'z'=8] {'z'}, dimensions={0} | all-to-all | bytes 524288 | tf_op jit(solution)/shard_map/all_to_all | solution.py:204
  74.3 3.2 %collective-permute-start.2 = (f32[256,256]{1,0:T(8,128)S(1)}, f32[256,256]{1,0:T(8,128)S(1)}, u32[]{:S(2)}, u32[]{:S(2)}) collective-permute-start(f32[256,256]{1,0:T(8,128)S(1)} %bitcast.35), channel_id=1, source_target_pairs={{0,8},{8,0},{1,9},{9,1},{2,10},{10,2},{3,11},{11,3},{4,12},{12,4},... | collective-permute-start | bytes 786440 | tf_op jit(solution)/shard_map/ppermute | solution.py:199
  77.5 0.4 convolution_bitcast_fusion
  77.9 0.0 copy-start.6
  77.9 1.6 fusion.16
  79.5 0.0 collective-permute-done.2
  79.5 0.0 copy-done.6
  79.6 1.7 convolution_add_fusion
  81.2 0.4 convolution_add_fusion.1
  81.6 0.2 pad_maximum_fusion
  81.8 30.1 %all_to_all.33 = f32[16,128,256]{2,1,0:T(8,128)S(1)} all-to-all(f32[16,128,256]{2,1,0:T(8,128)S(1)} %pad_maximum_fusion), channel_id=1, replica_groups=mesh['x'=4,'y'=4,'c'=2,'z'=8] {'x','y'}, dimensions={0} | all-to-all | bytes 4194304 | tf_op jit(solution)/shard_map/all_to_all | solution.py:236
  112.0 0.1 reduce_sum.37
  112.1 0.2 broadcast_in_dim.8
  112.3 30.0 %all_to_all.34 = f32[16,128,256]{2,1,0:T(8,128)S(1)} all-to-all(f32[16,128,256]{2,1,0:T(8,128)S(1)} %broadcast_in_dim.8), channel_id=1, replica_groups=mesh['x'=4,'y'=4,'c'=2,'z'=8] {'x','y'}, dimensions={0} | all-to-all | bytes 4194304 | tf_op jit(solution)/shard_map/all_to_all | solution.py:204
  142.3 0.1 slice.17.refs_6_
  142.5 3.7 %collective-permute-start.3 = (f32[16,112,256]{2,1,0:T(8,128)S(1)}, f32[16,112,256]{2,1,0:T(8,128)}, u32[]{:S(2)}, u32[]{:S(2)}) collective-permute-start(f32[16,112,256]{2,1,0:T(8,128)S(1)} %slice.17.refs_6_), channel_id=1, source_target_pairs={{0,8},{8,0},{1,9},{9,1},{2,10},{10,2},{3,11},{11,3},{4,12},{12,4},... | collective-permute-start | bytes 5505032 | tf_op jit(solution)/shard_map/ppermute | solution.py:199
  146.2 9.9 %shard_map.68 = f32[256,256]{1,0:T(8,128)S(1)} custom-call(f32[256,256]{1,0:T(8,128)S(1)} %bitcast.31), custom_call_target="tpu_custom_call" | custom-call | flops 16777216 | bytes 524288 | tf_op jit(solution)/shard_map/pallas_call | solution.py:142
  156.1 0.9 fusion
  157.1 0.7 broadcast_in_dim_broadcast_in_dim_broadcast_in_dim.2
  157.7 3.4 %all-to-all-start.5 = ((f32[16,8,256]{2,1,0:T(8,128)}), f32[16,8,256]{2,1,0:T(8,128)S(1)}, u32[]{:S(2)}, u32[]{:S(2)}) async-start(f32[16,8,256]{2,1,0:T(8,128)} %broadcast_in_dim_broadcast_in_dim_broadcast_in_dim.2), calls=%async_computation.5 | async-start | bytes 262144 | tf_op jit(solution)/shard_map/all_to_all | solution.py:204
  161.2 0.3 fusion.17
  161.5 0.3 fusion.4.refs_4_
  161.8 6.7 %all-to-all-done.5 = f32[16,8,256]{2,1,0:T(8,128)S(1)} async-done(((f32[16,8,256]{2,1,0:T(8,128)}), f32[16,8,256]{2,1,0:T(8,128)S(1)}, u32[]{:S(2)}, u32[]{:S(2)}) %all-to-all-start.5) | async-done | bytes 131104 | tf_op jit(solution)/shard_map/all_to_all | solution.py:204
  168.5 0.9 convolution_divide_fusion
  169.5 0.3 fusion.1.refs_5_
  169.7 0.0 collective-permute-done.3.refs_7_
  169.8 0.0 copy-start.1
  169.8 2.0 %copy-done.1 = f32[256,3584]{1,0:T(8,128)S(1)} copy-done((f32[256,3584]{1,0:T(8,128)S(1)}, f32[256,3584]{1,0:T(8,128)}, u32[]{:S(2)}) %copy-start.1) | copy-done | bytes 3670040
  171.8 0.0 copy-start.3
  171.8 1.5 copy-done.3
  173.3 0.0 copy-start.4
  173.3 1.5 copy-done.4
  174.8 5.8 %shard_map.69 = (f32[256,3584]{1,0:T(8,128)}, bf16[256,3584]{1,0:T(8,128)(2,1)}) custom-call(s32[1]{0:T(128)} %bitcast.refs_0_, f32[256,3584]{1,0:T(8,128)S(1)} %copy-done.1, bf16[256,3584]{1,0:T(8,128)(2,1)S(1)} %copy-done.3, bf16[256,3584]{1,0:T(8,128)(2,1)S(1)} %copy-done.4, f32[256,256]{1,0:T(8,128)S(1)} %fusion.4.refs_4_, ...), custom_call_target="tpu_custom_call" | custom-call | flops 1879048192 | bytes 14680064 | tf_op jit(solution)/shard_map/pallas_call | solution.py:180
  (6 shorter events, 0.1 us)
Async XLA Ops:
  0.6 2.0 %copy-start = (f32[256,3584]{1,0:T(8,128)S(1)}, f32[256,3584]{1,0:T(8,128)}, u32[]{:S(2)}) copy-start(f32[256,3584]{1,0:T(8,128)} %refs_1_.3) | copy-start | bytes 11010052
  2.7 1.5 copy-start.2
  4.2 5.2 %copy-start.7 = (f32[112,256]{1,0:T(8,128)S(1)}, f32[112,256]{1,0:T(8,128)}, u32[]{:S(2)}) copy-start(f32[112,256]{1,0:T(8,128)} %param.7) | copy-start | bytes 344068
  6.1 33.0 %collective-permute-start = (f32[256,1792]{1,0:T(8,128)S(1)}, f32[256,1792]{1,0:T(8,128)S(1)}, u32[]{:S(2)}, u32[]{:S(2)}) collective-permute-start(f32[256,1792]{1,0:T(8,128)S(1)} %get-tuple-element.8), channel_id=1, source_target_pairs={{0,8},{8,0},{1,9},{9,1},{2,10},{10,2},{3,11},{11,3},{4,12},{12,4},... | collective-permute-start | bytes 5505032 | tf_op jit(solution)/shard_map/ppermute | solution.py:199
  39.1 1.2 copy-start.5
  40.3 2.8 %collective-permute-start.1 = (f32[256,256]{1,0:T(8,128)S(1)}, f32[256,256]{1,0:T(8,128)S(1)}, u32[]{:S(2)}, u32[]{:S(2)}) collective-permute-start(f32[256,256]{1,0:T(8,128)S(1)} %fusion.15), channel_id=1, source_target_pairs={{0,8},{8,0},{1,9},{9,1},{2,10},{10,2},{3,11},{11,3},{4,12},{12,4},... | collective-permute-start | bytes 786440 | tf_op jit(solution)/shard_map/ppermute | solution.py:199
  74.3 5.2 %collective-permute-start.2 = (f32[256,256]{1,0:T(8,128)S(1)}, f32[256,256]{1,0:T(8,128)S(1)}, u32[]{:S(2)}, u32[]{:S(2)}) collective-permute-start(f32[256,256]{1,0:T(8,128)S(1)} %bitcast.35), channel_id=1, source_target_pairs={{0,8},{8,0},{1,9},{9,1},{2,10},{10,2},{3,11},{11,3},{4,12},{12,4},... | collective-permute-start | bytes 786440 | tf_op jit(solution)/shard_map/ppermute | solution.py:199
  77.9 1.7 copy-start.6
  142.5 27.3 %collective-permute-start.3 = (f32[16,112,256]{2,1,0:T(8,128)S(1)}, f32[16,112,256]{2,1,0:T(8,128)}, u32[]{:S(2)}, u32[]{:S(2)}) collective-permute-start(f32[16,112,256]{2,1,0:T(8,128)S(1)} %slice.17.refs_6_), channel_id=1, source_target_pairs={{0,8},{8,0},{1,9},{9,1},{2,10},{10,2},{3,11},{11,3},{4,12},{12,4},... | collective-permute-start | bytes 5505032 | tf_op jit(solution)/shard_map/ppermute | solution.py:199
  157.7 10.7 %all-to-all-start.5 = ((f32[16,8,256]{2,1,0:T(8,128)}), f32[16,8,256]{2,1,0:T(8,128)S(1)}, u32[]{:S(2)}, u32[]{:S(2)}) async-start(f32[16,8,256]{2,1,0:T(8,128)} %broadcast_in_dim_broadcast_in_dim_broadcast_in_dim.2), calls=%async_computation.5 | async-start | bytes 262144 | tf_op jit(solution)/shard_map/all_to_all | solution.py:204
  169.8 2.0 %copy-start.1 = (f32[256,3584]{1,0:T(8,128)S(1)}, f32[256,3584]{1,0:T(8,128)}, u32[]{:S(2)}) copy-start(f32[256,3584]{1,0:T(8,128)} %refs_1_.3) | copy-start | bytes 11010052
  171.8 1.5 copy-start.3
  173.3 1.5 copy-start.4

commit v2 on v1

--- a/solution.py
+++ b/solution.py
@@ -1,3 +1,4 @@
+import functools
 import math
 
 import jax
@@ -28,40 +29,59 @@
     return lax.dot_general(a, b, (((1,), (1,)), ((), ())), preferred_element_type=F32)
 
 
-def sort_columns_kernel(core_ref, mom_ref, grad_ref, keep_ref, send_ref, *, count):
-    buffer = mom_ref[...] + grad_ref[...].astype(F32)
-    chunks = buffer.shape[1] // count
-    parts = [
-        jnp.concatenate(
-            [buffer[:, i * count : (i + 1) * count] for i in range(first, chunks, 2)], axis=1
+def sort_columns_kernel(core_ref, mom_ref, grad_ref, keep_ref, send_ref, mom, grad, sems, *, count):
+    steps, tile, cols = mom.shape
+    loads = []
+    for t in range(steps):
+        rows = pl.ds(t * tile, tile)
+        pair = (
+            pltpu.make_async_copy(mom_ref.at[rows, :], mom.at[t], sems.at[0, t]),
+            pltpu.make_async_copy(grad_ref.at[rows, :], grad.at[t], sems.at[1, t]),
         )
-        for first in range(2)
-    ]
-
-    @pl.when(core_ref[0] == 0)
-    def _():
-        keep_ref[...] = parts[0]
-        send_ref[...] = parts[1]
-
-    @pl.when(core_ref[0] == 1)
-    def _():
-        keep_ref[...] = parts[1]
-        send_ref[...] = parts[0]
+        for load in pair:
+            load.start()
+        loads.append(pair)
+    for t in range(steps):
+        for load in loads[t]:
+            load.wait()
+        buffer = mom[t] + grad[t].astype(F32)
+        parts = [
+            jnp.concatenate(
+                [buffer[:, i * count : (i + 1) * count] for i in range(first, cols // count, 2)],
+                axis=1,
+            )
+            for first in range(2)
+        ]
+        rows = pl.ds(t * tile, tile)
+
+        @pl.when(core_ref[0] == 0)
+        def _():
+            keep_ref[rows, :] = parts[0]
+            send_ref[rows, :] = parts[1]
+
+        @pl.when(core_ref[0] == 1)
+        def _():
+            keep_ref[rows, :] = parts[1]
+            send_ref[rows, :] = parts[0]
 
 
 def sort_columns(core, momentum, gradient, count):
     rows, cols = momentum.shape
-    tile = 64
-    spec = pl.BlockSpec((tile, cols), lambda i: (i, 0))
-    half = pl.BlockSpec((tile, cols // 2), lambda i: (i, 0))
+    steps = 8
     out = jax.ShapeDtypeStruct((rows, cols // 2), F32)
+    hbm = pl.BlockSpec(memory_space=pltpu.HBM)
+    vmem = pl.BlockSpec(memory_space=VMEM)
     return pl.pallas_call(
         lambda *refs: sort_columns_kernel(*refs, count=count),
-        grid=(rows // tile,),
-        in_specs=[pl.BlockSpec(memory_space=pltpu.SMEM), spec, spec],
-        out_specs=[half, half],
+        in_specs=[pl.BlockSpec(memory_space=pltpu.SMEM), hbm, hbm],
+        out_specs=[vmem, vmem],
         out_shape=[out, out],
-        compiler_params=pltpu.CompilerParams(vmem_limit_bytes=40 * 2**20),
+        scratch_shapes=[
+            VMEM((steps, rows // steps, cols), F32),
+            VMEM((steps, rows // steps, cols), BF16),
+            pltpu.SemaphoreType.DMA((2, steps)),
+        ],
+        compiler_params=pltpu.CompilerParams(vmem_limit_bytes=53 * 2**20),
         cost_estimate=pl.CostEstimate(flops=rows * cols, bytes_accessed=rows * cols * 10, transcendentals=0),
     )(core, momentum, gradient)
 
@@ -70,9 +90,24 @@
     return jnp.broadcast_to(x, (8, 128))
 
 
-def inverse_factor_kernel(g_ref, x_ref, a, w):
-    n = g_ref.shape[0]
-    a[...] = g_ref[...]
+def dot3(dims, a, b):
+    a_hi, a_lo = split(a)
+    b_hi, b_lo = split(b)
+    dot = functools.partial(
+        lax.dot_general, dimension_numbers=(dims, ((), ())), preferred_element_type=F32
+    )
+    return dot(a_hi, b_hi) + dot(a_hi, b_lo) + dot(a_lo, b_hi)
+
+
+NT = ((1,), (1,))
+NN = ((1,), (0,))
+
+
+def factor_kernel(got_ref, proj_ref, own_ref, x_ref, ortho_ref, m1_ref, back_ref, sums_ref, a, w):
+    chips, packed, n = got_ref.shape
+    count, share = own_ref.shape[0], n // chips
+    for i in range(chips):
+        a[i * share : (i + 1) * share, :] = got_ref[i, count:, :]
     w[...] = (
         lax.broadcasted_iota(jnp.int32, (n, n), 0) == lax.broadcasted_iota(jnp.int32, (n, n), 1)
     ).astype(F32)
@@ -134,61 +169,179 @@
                     u, ref[r0:end, lo:hi], (((0,), (0,)), ((), ())),
                     precision=HIGHEST, preferred_element_type=F32,
                 )
-    x_ref[...] = w[...]
-
-
-def inverse_factor(gram):
-    n = gram.shape[0]
+    inverse = w[...]
+    x_ref[...] = inverse
+    total = jnp.zeros((1, n), F32)
+    for i in range(0, chips, 4):
+        rows = jnp.concatenate([got_ref[i + k, :count, :] for k in range(4)], axis=0)
+        back = dot3(NT, rows, inverse)
+        total = total + jnp.sum(back * back, axis=0, keepdims=True)
+    sums_ref[...] = jnp.broadcast_to(total[None], sums_ref.shape)
+    ortho = dot3(NT, proj_ref[...], inverse)
+    ortho_ref[...] = ortho
+    m1_ref[...] = dot3(NN, (1.0 - keep_rate) * ortho, inverse)
+    back_ref[...] = dot3(NT, own_ref[...], inverse)
+
+
+def factor(got, proj, own, copies):
+    n = got.shape[2]
+    rows = proj.shape[0]
+    vmem = pl.BlockSpec(memory_space=VMEM)
     return pl.pallas_call(
-        inverse_factor_kernel,
-        out_shape=jax.ShapeDtypeStruct((n, n), F32),
-        in_specs=[pl.BlockSpec(memory_space=VMEM)],
-        out_specs=pl.BlockSpec(memory_space=VMEM),
+        factor_kernel,
+        out_shape=[
+            jax.ShapeDtypeStruct((n, n), F32),
+            jax.ShapeDtypeStruct((rows, n), F32),
+            jax.ShapeDtypeStruct((rows, n), F32),
+            jax.ShapeDtypeStruct(own.shape, F32),
+            jax.ShapeDtypeStruct((copies, 8, n), F32),
+        ],
+        in_specs=[vmem] * 3,
+        out_specs=[vmem] * 5,
         scratch_shapes=[VMEM((n, n), F32), VMEM((n, n), F32)],
         compiler_params=pltpu.CompilerParams(vmem_limit_bytes=16 * 2**20),
-        cost_estimate=pl.CostEstimate(flops=n**3, bytes_accessed=8 * n * n, transcendentals=0),
-    )(gram)
-
-
-def update_kernel(core_ref, mom_ref, grad_ref, weight_ref, m1_ref, m2_ref, own_ref, other_ref,
-                  new_mom_ref, new_weight_ref, s_ref, *, count):
-    pairs = s_ref.shape[0] // (2 * count)
-    for i in range(pairs):
-        first = pl.multiple_of((2 * i + core_ref[0]) * count, 8)
-        second = pl.multiple_of((2 * i + 1 - core_ref[0]) * count, 8)
-        s_ref[pl.ds(first, count), :] = own_ref[i]
-        s_ref[pl.ds(second, count), :] = other_ref[i]
-    s_hi, s_lo = split(s_ref[...])
-    m2_hi, m2_lo = split(m2_ref[...])
-    m1_hi = m1_ref[...].astype(BF16)
-    buffer = mom_ref[...] + grad_ref[...].astype(F32)
-    new_mom_ref[...] = buffer - nt(m1_hi, s_hi)
-    update = nt(m2_hi, s_hi) + nt(m2_hi, s_lo) + nt(m2_lo, s_hi)
-    new_weight_ref[...] = (
-        (1.0 - step_size * decay_rate) * weight_ref[...].astype(F32) - update
-    ).astype(BF16)
-
-
-def updates(core, momentum, gradient, weight, m1, m2, own, other):
+        cost_estimate=pl.CostEstimate(flops=40 * n**3, bytes_accessed=16 * n * n, transcendentals=0),
+    )(got, proj, own)
+
+
+TILES = 4
+HBM = pl.BlockSpec(memory_space=pltpu.HBM)
+IN_VMEM = pl.BlockSpec(memory_space=VMEM)
+IN_SMEM = pl.BlockSpec(memory_space=pltpu.SMEM)
+
+
+def copies_of(pairs, sems):
+    return [pltpu.make_async_copy(src, dst, sems.at[i]) for i, (src, dst) in enumerate(pairs)]
+
+
+def momentum_kernel(core_ref, mom_ref, grad_ref, m1_ref, own_ref, other_ref,
+                    out_ref, hi_ref, lo_ref,
+                    mom, grad, own, other, out, hi, lo, load_sems, store_sems):
+    tiles, rows, width = mom.shape
+    chunks, count, _ = own.shape
+    per = chunks // tiles
+    loads, stores = [], []
+    for t in range(tiles):
+        cols, part = pl.ds(t * width, width), pl.ds(t * per, per)
+        loads.append(copies_of(
+            [
+                (own_ref.at[part], own.at[part]), (other_ref.at[part], other.at[part]),
+                (mom_ref.at[:, cols], mom.at[t]), (grad_ref.at[:, cols], grad.at[t]),
+            ],
+            load_sems.at[t],
+        ))
+        stores.append(copies_of(
+            [
+                (hi.at[cols], hi_ref.at[cols]), (lo.at[cols], lo_ref.at[cols]),
+                (out.at[t], out_ref.at[:, cols]),
+            ],
+            store_sems.at[t],
+        ))
+        for load in loads[t]:
+            load.start()
+    m1 = m1_ref[...].astype(BF16)
+    for t in range(tiles):
+        loads[t][0].wait()
+        loads[t][1].wait()
+        for i in range(t * per, (t + 1) * per):
+            mine = pl.ds(pl.multiple_of((2 * i + core_ref[0]) * count, 16), count)
+            theirs = pl.ds(pl.multiple_of((2 * i + 1 - core_ref[0]) * count, 16), count)
+            hi[mine, :], lo[mine, :] = split(own[i])
+            hi[theirs, :], lo[theirs, :] = split(other[i])
+        stores[t][0].start()
+        stores[t][1].start()
+        change = nt(m1, hi[t * width : (t + 1) * width, :])
+        loads[t][2].wait()
+        loads[t][3].wait()
+        out[t] = mom[t] + grad[t].astype(F32) - change
+        stores[t][2].start()
+    for group in stores:
+        for store in group:
+            store.wait()
+
+
+def update_momentum(core, momentum, gradient, m1, own, other):
     rows, cols = momentum.shape
-    chunks, count, rank = own.shape
-    tiles = 4
-    per = chunks // tiles
-    spec = pl.BlockSpec((rows, cols // tiles), lambda i: (0, i))
-    whole = pl.BlockSpec((rows, rank), lambda i: (0, 0))
-    part = pl.BlockSpec((per, count, rank), lambda i: (i, 0, 0))
+    rank = own.shape[2]
+    factor_part = jax.ShapeDtypeStruct((cols, rank), BF16)
+    tile = (TILES, rows, cols // TILES)
     return pl.pallas_call(
-        lambda *refs: update_kernel(*refs, count=count),
-        grid=(tiles,),
-        in_specs=[pl.BlockSpec(memory_space=pltpu.SMEM), spec, spec, spec, whole, whole, part, part],
-        out_specs=[spec, spec],
-        out_shape=[jax.ShapeDtypeStruct((rows, cols), F32), jax.ShapeDtypeStruct((rows, cols), BF16)],
-        scratch_shapes=[VMEM((2 * per * count, rank), F32)],
-        compiler_params=pltpu.CompilerParams(vmem_limit_bytes=40 * 2**20),
+        momentum_kernel,
+        in_specs=[IN_SMEM, HBM, HBM, IN_VMEM, HBM, HBM],
+        out_specs=[HBM] * 3,
+        out_shape=[jax.ShapeDtypeStruct((rows, cols), F32), factor_part, factor_part],
+        scratch_shapes=[
+            VMEM(tile, F32), VMEM(tile, BF16), VMEM(own.shape, F32), VMEM(own.shape, F32),
+            VMEM(tile, F32), VMEM((cols, rank), BF16), VMEM((cols, rank), BF16),
+            pltpu.SemaphoreType.DMA((TILES, 4)), pltpu.SemaphoreType.DMA((TILES, 3)),
+        ],
+        compiler_params=pltpu.CompilerParams(vmem_limit_bytes=53 * 2**20),
         cost_estimate=pl.CostEstimate(
-            flops=8 * rows * cols * rank, bytes_accessed=rows * cols * 16, transcendentals=0
+            flops=2 * rows * cols * rank, bytes_accessed=rows * cols * 18, transcendentals=0
         ),
-    )(core, momentum, gradient, weight, m1, m2, own, other)
+    )(core, momentum, gradient, m1, own, other)
+
+
+def weight_kernel(weight_ref, got_ref, ortho_ref, x_ref, back_ref, hi_ref, lo_ref,
+                  out_ref, basis_ref,
+                  weight, hi, lo, out, load_sems, store_sems, *, scale, total_cols):
+    tiles, rows, width = out.shape
+    loads, stores = [], []
+    for t in range(tiles):
+        cols = pl.ds(t * width, width)
+        loads.append(copies_of(
+            [
+                (hi_ref.at[cols], hi.at[cols]), (lo_ref.at[cols], lo.at[cols]),
+                (weight_ref.at[:, cols], weight.at[t]),
+            ],
+            load_sems.at[t],
+        ))
+        stores.append(
+            pltpu.make_async_copy(out.at[t], out_ref.at[:, cols], store_sems.at[t])
+        )
+        for load in loads[t]:
+            load.start()
+    sums = got_ref[0, 0:1, :]
+    for i in range(1, got_ref.shape[0]):
+        sums = sums + got_ref[i, 0:1, :]
+    rms = jnp.sqrt(sums / total_cols + 1e-06)
+    basis_ref[...] = back_ref[...] / rms
+    left_hi, left_lo = split(dot3(NN, scale * ortho_ref[...] / rms, x_ref[...]))
+    for t in range(tiles):
+        for load in loads[t]:
+            load.wait()
+        right_hi = hi[t * width : (t + 1) * width, :]
+        right_lo = lo[t * width : (t + 1) * width, :]
+        change = nt(left_hi, right_hi) + nt(left_hi, right_lo) + nt(left_lo, right_hi)
+        out[t] = (
+            (1.0 - step_size * decay_rate) * weight[t].astype(F32) - change
+        ).astype(BF16)
+        stores[t].start()
+    for store in stores:
+        store.wait()
+
+
+def update_weight(weight, got, ortho, inverse, back, hi, lo, scale, total_cols):
+    rows, cols = weight.shape
+    count, rank = back.shape
+    tile = (TILES, rows, cols // TILES)
+    return pl.pallas_call(
+        functools.partial(weight_kernel, scale=scale, total_cols=total_cols),
+        in_specs=[HBM] + [IN_VMEM] * 4 + [HBM] * 2,
+        out_specs=[HBM, IN_VMEM],
+        out_shape=[
+            jax.ShapeDtypeStruct((rows, cols), BF16), jax.ShapeDtypeStruct((count, rank), F32)
+        ],
+        scratch_shapes=[
+            VMEM(tile, BF16), VMEM((cols, rank), BF16), VMEM((cols, rank), BF16),
+            VMEM(tile, BF16),
+            pltpu.SemaphoreType.DMA((TILES, 3)), pltpu.SemaphoreType.DMA((TILES,)),
+        ],
+        compiler_params=pltpu.CompilerParams(vmem_limit_bytes=53 * 2**20),
+        cost_estimate=pl.CostEstimate(
+            flops=6 * rows * cols * rank, bytes_accessed=rows * cols * 8, transcendentals=0
+        ),
+    )(weight, got, ortho, inverse, back, hi, lo)
 
 
 def tn(a, b):
@@ -236,29 +389,14 @@
     summed = jnp.sum(lax.all_to_all(packed, plane, 0, 0), axis=0)
     everything = gather(summed, plane, chips)
     half = everything[:, :count]
-    gram = everything[:, count:].reshape(rank, rank)
     half_other = across_cores(half)
-
-    inverse = inverse_factor(gram)
-    back = lax.dot_general(
-        half.reshape(chips * count, rank), inverse, (((1,), (1,)), ((), ())), precision=HIGH
-    )
-    sums = jnp.sum(back * back, axis=0)
-    sums = jnp.sum(
-        gather(jnp.broadcast_to(sums[None], (8, rank)), ("c", "z"), cores * depth), axis=0
-    )[0]
-    rms = jnp.sqrt(sums / total_cols + 1e-06)
-
-    own_back = lax.dot_general(
-        summed[:count], inverse, (((1,), (1,)), ((), ())), precision=HIGH
-    )
-    new_basis = own_back / rms
-    ortho = lax.dot_general(proj, inverse, (((1,), (1,)), ((), ())), precision=HIGH)
+    inverse, ortho, m1, back, sums = factor(everything, proj, summed[:count], cores * depth)
+    sums = lax.all_to_all(sums, ("c", "z"), 0, 0)
+    new_momentum, hi, lo = update_momentum(core, momentum, gradient, m1, half, half_other)
+    sums, hi, lo = lax.optimization_barrier((sums, hi, lo))
     scale = step_size * math.sqrt(total_cols / total_rows)
-    m1 = jnp.dot((1.0 - keep_rate) * ortho, inverse, precision=HIGH)
-    m2 = jnp.dot(scale * ortho / rms, inverse, precision=HIGH)
-    new_momentum, new_weight = updates(
-        core, momentum, gradient, weight, m1, m2, half, half_other
+    new_weight, new_basis = update_weight(
+        weight, sums, ortho, inverse, back, hi, lo, scale, total_cols
     )
     return new_momentum, new_weight, new_basis
 

time: 181 us -> 178 us (0.983)
  Pallas kernels: 17.7 us -> 30.9 us
  local copies, waits for them, and re-layouts: 9.97 us -> 0.58 us
  waiting for transfers between devices: 6.79 us -> 0.72 us
    pallas_call x3 -> x4, Pallas kernels: 17.7 us -> 30.9 us  [the longest x1 12.3 us: factor(): pl.pallas_call(factor_kernel, out_shape=[jax.ShapeDtypeStruct((n, n), F32...]
    unnamed x16 -> x6, local copies, waits for them, and re-layouts: 8.78 us -> 0.01 us
    all_to_all x1, waiting for transfers between devices: 6.66 us -> 0.57 us  [per_device(): sums = lax.all_to_all(sums, ('c', 'z'), 0, 0)]
    dot_general x5 -> x0, matrix products: 2.8 us -> none  [the longest x1 0.94 us: per_device(): lax.dot_general(summed[:count], inverse, (((1,), (1,)), ((), ())), precis...]
  transfers between devices with their start and end apart: 5 -> 5, of which waited for: 2 -> 2; matrix products, arithmetic and copies ran while one was open for 4% -> 3% of each run, Pallas kernels for 6% -> 11%
where the time goes in v2:
time: 178 us; the launch traced here: 177 us
  blocking collectives  121 us (68%)
  Pallas kernels  30.9 us (17%)
  starting transfers between devices  15.5 us (9%)
  matrix products  7.64 us (4%)
    all_to_all x3, blocking collectives, gather(): return lax.all_to_all(spread, axes, 0, 0)  71.6 us
    all_to_all x1, blocking collectives, per_device(): summed = jnp.sum(lax.all_to_all(packed, plane, 0, 0), axis=0)  30.1 us
    all_to_all x1, blocking collectives, per_device(): lax.all_to_all(partial.reshape(depth, share, rank), 'z', 0, 0)  19.1 us
    pallas_call x1, Pallas kernels, factor(): pl.pallas_call(factor_kernel, out_shape=[jax.ShapeDtypeStruct((n, n), F32...  12.3 us
    ppermute x4, starting transfers between devices, across_cores(): return lax.ppermute(x, 'c', [(0, 1), (1, 0)])  11.9 us
    pallas_call x1, Pallas kernels, update_weight(): pl.pallas_call(functools.partial(weight_kernel, scale=scale, total_cols=t...  6.79 us
    pallas_call x1, Pallas kernels, update_momentum(): pl.pallas_call(momentum_kernel, in_specs=[IN_SMEM, HBM, HBM, IN_VMEM, HBM...  6.54 us
    dot_general x4, matrix products, tn(): lax.dot_general(a, b, (((0,), (0,)), ((), ())), precision=HIGH, preferred...  5.6 us
  transfers between devices with their start and end apart: 5, of which 2 were waited for; matrix products, arithmetic and copies ran while one was open for 3% of the time, Pallas kernels for 11%

profile of v2, /device:TPU:1, one launch (start us, length us, event | category | flops | bytes accessed | tf_op | source)
XLA Modules:
  0.0 177.4 jit_solution(1841274336260897875)
XLA Ops:
  0.6 0.0 copy-start.2
  0.6 5.2 %shard_map.67 = (f32[256,1792]{1,0:T(8,128)}, f32[256,1792]{1,0:T(8,128)}) custom-call(s32[1]{0:T(128)} %bitcast.refs_0_.core_ref, f32[256,3584]{1,0:T(8,128)} %mom_ref.1, bf16[256,3584]{1,0:T(8,128)(2,1)} %grad_ref.1), custom_call_target="tpu_custom_call" | custom-call | flops 917504 | bytes 9175040 | tf_op jit(solution)/shard_map/pallas_call | solution.py:74
  5.9 3.2 %collective-permute-start = (f32[256,1792]{1,0:T(8,128)}, f32[256,1792]{1,0:T(8,128)S(1)}, u32[]{:S(2)}, u32[]{:S(2)}) collective-permute-start(f32[256,1792]{1,0:T(8,128)} %get-tuple-element.19), channel_id=1, source_target_pairs={{0,8},{8,0},{1,9},{9,1},{2,10},{10,2},{3,11},{11,3},{4,12},{12,4},... | collective-permute-start | bytes 5505032 | tf_op jit(solution)/shard_map/ppermute | solution.py:352
  9.1 0.0 copy-done.2
  9.1 0.2 broadcast_in_dim.6
  9.3 29.5 %all_to_all.30 = f32[16,112,256]{2,1,0:T(8,128)S(1)} all-to-all(f32[16,112,256]{2,1,0:T(8,128)S(1)} %broadcast_in_dim.6), channel_id=1, replica_groups=mesh['x'=4,'y'=4,'c'=2,'z'=8] {'x','y'}, dimensions={0} | all-to-all | bytes 3670016 | tf_op jit(solution)/shard_map/all_to_all | solution.py:357
  38.8 0.0 collective-permute-done
  38.8 0.0 copy-start.1
  38.8 1.0 fusion.1
  39.8 1.7 collective-permute-start.1
  41.6 0.0 copy-done.1
  41.6 1.0 fusion
  42.6 0.1 collective-permute-done.1
  42.8 19.1 %all_to_all.31 = f32[8,32,256]{2,1,0:T(8,128)S(1)} all-to-all(f32[8,32,256]{2,1,0:T(8,128)S(1)} %bitcast.26), channel_id=1, replica_groups=mesh['x'=4,'y'=4,'c'=2,'z'=8] {'z'}, dimensions={0} | all-to-all | bytes 524288 | tf_op jit(solution)/shard_map/all_to_all | solution.py:379
  61.9 12.1 %all_to_all.32 = f32[8,32,256]{2,1,0:T(8,128)S(1)} all-to-all(f32[8,32,256]{2,1,0:T(8,128)S(1)} %broadcast_in_dim.7), channel_id=1, replica_groups=mesh['x'=4,'y'=4,'c'=2,'z'=8] {'z'}, dimensions={0} | all-to-all | bytes 524288 | tf_op jit(solution)/shard_map/all_to_all | solution.py:357
  74.0 3.2 %collective-permute-start.2 = (f32[256,256]{1,0:T(8,128)S(1)}, f32[256,256]{1,0:T(8,128)S(1)}, u32[]{:S(2)}, u32[]{:S(2)}) collective-permute-start(f32[256,256]{1,0:T(8,128)S(1)} %bitcast.20), channel_id=1, source_target_pairs={{0,8},{8,0},{1,9},{9,1},{2,10},{10,2},{3,11},{11,3},{4,12},{12,4},... | collective-permute-start | bytes 786440 | tf_op jit(solution)/shard_map/ppermute | solution.py:352
  77.1 0.4 convolution_bitcast_fusion
  77.5 3.1 %fusion.2 = f32[1792,256]{1,0:T(8,128)S(1)} fusion(f32[256,1792]{1,0:T(8,128)} %get-tuple-element.18, f32[256,256]{1,0:T(8,128)S(1)} %bitcast.21), kind=kOutput, calls=%fused_computation.6 | convolution fusion | flops 704643072 | bytes 3932160 | tf_op jit(solution)/shard_map/dot_general | solution.py:348
  80.7 0.0 collective-permute-done.2
  80.7 1.7 convolution_add_fusion
  82.4 0.4 convolution_add_fusion.1
  82.8 0.2 pad_maximum_fusion
  83.0 30.1 %all_to_all.33 = f32[16,128,256]{2,1,0:T(8,128)S(1)} all-to-all(f32[16,128,256]{2,1,0:T(8,128)S(1)} %pad_maximum_fusion), channel_id=1, replica_groups=mesh['x'=4,'y'=4,'c'=2,'z'=8] {'x','y'}, dimensions={0} | all-to-all | bytes 4194304 | tf_op jit(solution)/shard_map/all_to_all | solution.py:389
  113.1 0.1 reduce_sum.19
  113.2 0.2 broadcast_in_dim.8
  113.4 30.0 %all_to_all.34.got_ref = f32[16,128,256]{2,1,0:T(8,128)S(1)} all-to-all(f32[16,128,256]{2,1,0:T(8,128)S(1)} %broadcast_in_dim.8), channel_id=1, replica_groups=mesh['x'=4,'y'=4,'c'=2,'z'=8] {'x','y'}, dimensions={0} | all-to-all | bytes 4194304 | tf_op jit(solution)/shard_map/all_to_all | solution.py:357
  143.5 0.2 slice.9.own_ref
  143.6 0.0 copy-start
  143.7 3.7 %collective-permute-start.3 = (f32[16,112,256]{2,1,0:T(8,128)S(1)}, f32[16,112,256]{2,1,0:T(8,128)}, u32[]{:S(2)}, u32[]{:S(2)}) collective-permute-start(f32[16,112,256]{2,1,0:T(8,128)S(1)} %slice.9.own_ref), channel_id=1, source_target_pairs={{0,8},{8,0},{1,9},{9,1},{2,10},{10,2},{3,11},{11,3},{4,12},{12,4},... | collective-permute-start | bytes 5505032 | tf_op jit(solution)/shard_map/ppermute | solution.py:352
  147.4 12.3 %shard_map.68 = (f32[256,256]{1,0:T(8,128)S(1)}, f32[256,256]{1,0:T(8,128)S(1)}, f32[256,256]{1,0:T(8,128)S(1)}, f32[112,256]{1,0:T(8,128)S(1)}, f32[16,8,256]{2,1,0:T(8,128)}) custom-call(f32[16,128,256]{2,1,0:T(8,128)S(1)} %all_to_all.34.got_ref, f32[256,256]{1,0:T(8,128)S(1)} %bitcast.22, f32[112,256]{1,0:T(8,128)S(1)} %slice.8.own_ref), custom_call_target="tpu_custom_call" | custom-call | flops 671088640 | bytes 1048576 | tf_op jit(solution)/shard_map/pallas_call | solution.py:190
  159.7 3.6 %all-to-all-start.5 = ((f32[16,8,256]{2,1,0:T(8,128)}), f32[16,8,256]{2,1,0:T(8,128)S(1)}, u32[]{:S(2)}, u32[]{:S(2)}) async-start(f32[16,8,256]{2,1,0:T(8,128)} %get-tuple-element.22), calls=%async_computation.5 | async-start | bytes 262144 | tf_op jit(solution)/shard_map/all_to_all | solution.py:394
  163.3 0.0 collective-permute-done.3.other_ref
  163.3 0.0 copy-done
  163.3 6.5 %shard_map.69 = (f32[256,3584]{1,0:T(8,128)}, bf16[3584,256]{1,0:T(8,128)(2,1)}, bf16[3584,256]{1,0:T(8,128)(2,1)}) custom-call(s32[1]{0:T(128)} %bitcast.refs_0_.core_ref, f32[256,3584]{1,0:T(8,128)} %mom_ref.1, bf16[256,3584]{1,0:T(8,128)(2,1)} %grad_ref.1, f32[256,256]{1,0:T(8,128)S(1)} %get-tuple-element.20.m1_ref, f32[16,112,256]{2,1,0:T(8,128)} %copy-done, ...), custom_call_target="tpu_custom_call" | custom-call | flops 469762048 | bytes 16515072 | tf_op jit(solution)/shard_map/pallas_call | solution.py:268
  169.9 0.6 all-to-all-done.5.got_ref
  170.5 6.8 %shard_map.70 = (bf16[256,3584]{1,0:T(8,128)(2,1)}, f32[112,256]{1,0:T(8,128)}) custom-call(bf16[256,3584]{1,0:T(8,128)(2,1)} %weight_ref.1, f32[16,8,256]{2,1,0:T(8,128)S(1)} %all-to-all-done.5.got_ref, f32[256,256]{1,0:T(8,128)S(1)} %get-tuple-element.26.ortho_ref, f32[256,256]{1,0:T(8,128)S(1)} %get-tuple-element.27.x_ref, ...), custom_call_target="tpu_custom_call" | custom-call | flops 1409286144 | bytes 7340032 | tf_op jit(solution)/shard_map/pallas_call | solution.py:328
  (4 shorter events, 0.1 us)
Async XLA Ops:
  0.6 8.5 %copy-start.2 = (f32[112,256]{1,0:T(8,128)S(1)}, f32[112,256]{1,0:T(8,128)}, u32[]{:S(2)}) copy-start(f32[112,256]{1,0:T(8,128)} %param.7) | copy-start | bytes 344068
  5.9 32.9 %collective-permute-start = (f32[256,1792]{1,0:T(8,128)}, f32[256,1792]{1,0:T(8,128)S(1)}, u32[]{:S(2)}, u32[]{:S(2)}) collective-permute-start(f32[256,1792]{1,0:T(8,128)} %get-tuple-element.19), channel_id=1, source_target_pairs={{0,8},{8,0},{1,9},{9,1},{2,10},{10,2},{3,11},{11,3},{4,12},{12,4},... | collective-permute-start | bytes 5505032 | tf_op jit(solution)/shard_map/ppermute | solution.py:352
  38.8 2.8 %copy-start.1 = (f32[256,1792]{1,0:T(8,128)S(1)}, f32[256,1792]{1,0:T(8,128)}, u32[]{:S(2)}) copy-start(f32[256,1792]{1,0:T(8,128)} %get-tuple-element.18) | copy-start | bytes 5505028
  39.8 2.9 %collective-permute-start.1 = (f32[256,256]{1,0:T(8,128)S(1)}, f32[256,256]{1,0:T(8,128)S(1)}, u32[]{:S(2)}, u32[]{:S(2)}) collective-permute-start(f32[256,256]{1,0:T(8,128)S(1)} %fusion.1), channel_id=1, source_target_pairs={{0,8},{8,0},{1,9},{9,1},{2,10},{10,2},{3,11},{11,3},{4,12},{12,4},... | collective-permute-start | bytes 786440 | tf_op jit(solution)/shard_map/ppermute | solution.py:352
  74.0 6.7 %collective-permute-start.2 = (f32[256,256]{1,0:T(8,128)S(1)}, f32[256,256]{1,0:T(8,128)S(1)}, u32[]{:S(2)}, u32[]{:S(2)}) collective-permute-start(f32[256,256]{1,0:T(8,128)S(1)} %bitcast.20), channel_id=1, source_target_pairs={{0,8},{8,0},{1,9},{9,1},{2,10},{10,2},{3,11},{11,3},{4,12},{12,4},... | collective-permute-start | bytes 786440 | tf_op jit(solution)/shard_map/ppermute | solution.py:352
  143.6 19.7 %copy-start = (f32[16,112,256]{2,1,0:T(8,128)}, f32[16,112,256]{2,1,0:T(8,128)S(1)}, u32[]{:S(2)}) copy-start(f32[16,112,256]{2,1,0:T(8,128)S(1)} %slice.9.own_ref) | copy-start | bytes 5505028
  143.7 19.7 %collective-permute-start.3 = (f32[16,112,256]{2,1,0:T(8,128)S(1)}, f32[16,112,256]{2,1,0:T(8,128)}, u32[]{:S(2)}, u32[]{:S(2)}) collective-permute-start(f32[16,112,256]{2,1,0:T(8,128)S(1)} %slice.9.own_ref), channel_id=1, source_target_pairs={{0,8},{8,0},{1,9},{9,1},{2,10},{10,2},{3,11},{11,3},{4,12},{12,4},... | collective-permute-start | bytes 5505032 | tf_op jit(solution)/shard_map/ppermute | solution.py:352
  159.7 10.8 %all-to-all-start.5 = ((f32[16,8,256]{2,1,0:T(8,128)}), f32[16,8,256]{2,1,0:T(8,128)S(1)}, u32[]{:S(2)}, u32[]{:S(2)}) async-start(f32[16,8,256]{2,1,0:T(8,128)} %get-tuple-element.22), calls=%async_computation.5 | async-start | bytes 262144 | tf_op jit(solution)/shard_map/all_to_all | solution.py:394

commit v3 on v0

v3 whole, which is shorter than its diff:
```python
import functools
import math

import jax
import jax.numpy as jnp
from jax import lax
from jax.experimental import pallas as pl
from jax.experimental.pallas import tpu as pltpu
from jax.sharding import Mesh, PartitionSpec as P

keep_rate = 0.95
step_size = 0.25
decay_rate = 0.1

F32 = jnp.float32
BF16 = jnp.bfloat16
HIGH = lax.Precision.HIGH
HIGHEST = lax.Precision.HIGHEST
VMEM = pltpu.VMEM
TILES = 4
HBM = pl.BlockSpec(memory_space=pltpu.HBM)
IN_VMEM = pl.BlockSpec(memory_space=VMEM)
IN_SMEM = pl.BlockSpec(memory_space=pltpu.SMEM)


def split(x):
    hi = x.astype(BF16)
    lo = (x - hi.astype(F32)).astype(BF16)
    return hi, lo


def nt(a, b):
    return lax.dot_general(a, b, (((1,), (1,)), ((), ())), preferred_element_type=F32)


def copies_of(pairs, sems):
    return [pltpu.make_async_copy(src, dst, sems.at[i]) for i, (src, dst) in enumerate(pairs)]


def sort_columns_kernel(core_ref, mom_ref, grad_ref, keep_ref, send_ref,
                        mom, grad, keep, send, load_sems, store_sems, *, count):
    steps, tile, cols = mom.shape
    loads, stores = [], []
    for t in range(steps):
        rows = pl.ds(t * tile, tile)
        loads.append(copies_of(
            [(mom_ref.at[rows, :], mom.at[t]), (grad_ref.at[rows, :], grad.at[t])],
            load_sems.at[t],
        ))
        stores.append(copies_of(
            [(send.at[t], send_ref.at[rows, :]), (keep.at[t], keep_ref.at[rows, :])],
            store_sems.at[t],
        ))
        for load in loads[t]:
            load.start()
    for t in range(steps):
        for load in loads[t]:
            load.wait()
        buffer = mom[t] + grad[t].astype(F32)
        parts = [
            jnp.concatenate(
                [buffer[:, i * count : (i + 1) * count] for i in range(first, cols // count, 2)],
                axis=1,
            )
            for first in range(2)
        ]

        @pl.when(core_ref[0] == 0)
        def _():
            keep[t] = parts[0]
            send[t] = parts[1]

        @pl.when(core_ref[0] == 1)
        def _():
            keep[t] = parts[1]
            send[t] = parts[0]

        for store in stores[t]:
            store.start()
    for group in stores:
        for store in group:
            store.wait()


def sort_columns(core, momentum, gradient, count):
    rows, cols = momentum.shape
    steps = 8
    tile = rows // steps
    out = jax.ShapeDtypeStruct((rows, cols // 2), F32)
    return pl.pallas_call(
        lambda *refs: sort_columns_kernel(*refs, count=count),
        in_specs=[IN_SMEM, HBM, HBM],
        out_specs=[HBM, HBM],
        out_shape=[out, out],
        scratch_shapes=[
            VMEM((steps, tile, cols), F32), VMEM((steps, tile, cols), BF16),
            VMEM((steps, tile, cols // 2), F32), VMEM((steps, tile, cols // 2), F32),
            pltpu.SemaphoreType.DMA((steps, 2)), pltpu.SemaphoreType.DMA((steps, 2)),
        ],
        compiler_params=pltpu.CompilerParams(vmem_limit_bytes=53 * 2**20),
        cost_estimate=pl.CostEstimate(
            flops=rows * cols, bytes_accessed=rows * cols * 10, transcendentals=0
        ),
    )(core, momentum, gradient)


def bc(x):
    return jnp.broadcast_to(x, (8, 128))


def split3(x):
    hi = x.astype(BF16)
    rest = x - hi.astype(F32)
    mid = rest.astype(BF16)
    return hi, mid, (rest - mid.astype(F32)).astype(BF16)


def dot3(dims, a, b):
    a_hi, a_lo = split(a)
    b_hi, b_lo = split(b)
    dot = functools.partial(
        lax.dot_general, dimension_numbers=(dims, ((), ())), preferred_element_type=F32
    )
    return dot(a_hi, b_hi) + dot(a_hi, b_lo) + dot(a_lo, b_hi)


NT = ((1,), (1,))


def eliminate(top, below, tiles, a):
    cols = [[bc(a[i : i + 8, top + m : top + m + 1]) for m in range(8)] for i in below]
    own = [bc(a[top : top + 8, top + m : top + m + 1]) for m in range(8)]
    e = [[bc(own[j][i : i + 1, :]) if i >= j else None for j in range(8)] for i in range(8)]
    inv = [None] * 8
    for j in range(8):
        inv[j] = lax.rsqrt(e[j][j])
        for i in range(j + 1, 8):
            e[i][j] = e[i][j] * inv[j]
        for k in range(j + 1, 8):
            for i in range(k, 8):
                e[i][k] = e[i][k] - e[i][j] * e[k][j]
    xs = [[None] * 8 for _ in range(8)]
    for i in range(8):
        xs[i][i] = inv[i]
        for j in range(i):
            total = e[i][j] * xs[j][j]
            for k in range(j + 1, i):
                total = total + e[i][k] * xs[k][j]
            xs[i][j] = -total * inv[i]
    sub = lax.broadcasted_iota(jnp.int32, (8, 128), 0)
    for ref, t in tiles:
        rows = [bc(ref[top + k : top + k + 1, t : t + 128]) for k in range(8)]
        made = []
        for i in range(8):
            total = xs[i][0] * rows[0]
            for k in range(1, i + 1):
                total = total + xs[i][k] * rows[k]
            made.append(total)
        if below:
            back = []
            for m in range(8):
                total = xs[m][m] * made[m]
                for i in range(m + 1, 8):
                    total = total + xs[i][m] * made[i]
                back.append(total)
            for n_at, i in enumerate(below):
                value = ref[i : i + 8, t : t + 128]
                for m in range(8):
                    value = value - cols[n_at][m] * back[m]
                ref[i : i + 8, t : t + 128] = value
        row = made[0]
        for i in range(1, 8):
            row = jnp.where(sub == i, made[i], row)
        ref[top : top + 8, t : t + 128] = row


def factor_kernel(got_ref, proj_ref, back_ref, ortho_ref, sums_ref, a, w):
    chips, packed, n = got_ref.shape
    share = n // chips
    count = packed - share
    panel = 32
    for i in range(chips):
        a[i * share : (i + 1) * share, :] = got_ref[i, count:, :]
    w[...] = (
        lax.broadcasted_iota(jnp.int32, (n, n), 0) == lax.broadcasted_iota(jnp.int32, (n, n), 1)
    ).astype(F32)
    for r0 in range(0, n, panel):
        end = r0 + panel
        tiles = [(a, t) for t in range(r0 // 128 * 128, n, 128)]
        tiles += [(w, t) for t in range(0, end, 128)]
        for top in range(r0, end, 8):
            eliminate(top, list(range(top + 8, end, 8)), tiles, a)
        if end < n:
            lo, width = end // 128 * 128, -(-end // 128) * 128
            u = a[r0:end, lo:]
            v = jnp.concatenate([u, w[r0:end, :width]], axis=1)
            uh, um, ul = split3(u)
            vh, vm, vl = split3(v)
            change = lax.dot_general(
                jnp.concatenate([uh, uh, um, uh, ul, um], axis=0),
                jnp.concatenate([vh, vm, vh, vl, vh, vm], axis=0),
                (((0,), (0,)), ((), ())), preferred_element_type=F32,
            )
            a[end:n, lo:] -= change[end - lo :, : n - lo]
            w[end:n, :width] -= change[end - lo :, n - lo :]
    inverse = w[...]
    total = jnp.zeros((1, n), F32)
    group = 4
    for i in range(0, chips, group):
        rows = jnp.concatenate([got_ref[i + k, :count, :] for k in range(group)], axis=0)
        back = dot3(NT, rows, inverse)
        for k in range(group):
            back_ref[i + k] = back[k * count : (k + 1) * count]
        total = total + jnp.sum(back * back, axis=0, keepdims=True)
    sums_ref[...] = jnp.broadcast_to(total[None], sums_ref.shape)
    ortho_ref[...] = dot3(NT, proj_ref[...], inverse)


def factor(got, proj, copies):
    chips, packed, n = got.shape
    rows = proj.shape[0]
    return pl.pallas_call(
        factor_kernel,
        out_shape=[
            jax.ShapeDtypeStruct((chips, packed - n // chips, n), F32),
            jax.ShapeDtypeStruct((rows, n), F32),
            jax.ShapeDtypeStruct((copies, 8, n), F32),
        ],
        in_specs=[IN_VMEM] * 2,
        out_specs=[IN_VMEM] * 3,
        scratch_shapes=[VMEM((n, n), F32), VMEM((n, n), F32)],
        compiler_params=pltpu.CompilerParams(vmem_limit_bytes=16 * 2**20),
        cost_estimate=pl.CostEstimate(flops=40 * n**3, bytes_accessed=16 * n * n, transcendentals=0),
    )(got, proj)


def place(core, count, per, own, other, hi, lo, t):
    for i in range(t * per, (t + 1) * per):
        mine = pl.ds(pl.multiple_of((2 * i + core) * count, 16), count)
        theirs = pl.ds(pl.multiple_of((2 * i + 1 - core) * count, 16), count)
        for rows, value in ((mine, own[i]), (theirs, other[i])):
            hi[rows, :] = value.astype(BF16)
            if lo is not None:
                lo[rows, :] = (value - value.astype(BF16).astype(F32)).astype(BF16)


def early_kernel(core_ref, mom_ref, grad_ref, ortho_ref, own_ref, other_ref, out_ref,
                 mom, grad, own, other, out, hi, load_sems, store_sems):
    tiles, rows, width = mom.shape
    chunks, count, _ = own.shape
    per = chunks // tiles
    loads, stores = [], []
    for t in range(tiles):
        cols, part = pl.ds(t * width, width), pl.ds(t * per, per)
        loads.append(copies_of(
            [
                (own_ref.at[part], own.at[part]), (other_ref.at[part], other.at[part]),
                (mom_ref.at[:, cols], mom.at[t]), (grad_ref.at[:, cols], grad.at[t]),
            ],
            load_sems.at[t],
        ))
        stores.append(pltpu.make_async_copy(out.at[t], out_ref.at[:, cols], store_sems.at[t]))
        for load in loads[t]:
            load.start()
    left = ((1.0 - keep_rate) * ortho_ref[...]).astype(BF16)
    for t in range(tiles):
        for load in loads[t]:
            load.wait()
        place(core_ref[0], count, per, own, other, hi, None, t)
        change = nt(left, hi[t * width : (t + 1) * width, :])
        out[t] = mom[t] + grad[t].astype(F32) - change
        stores[t].start()
    for store in stores:
        store.wait()


def update_early(core, momentum, gradient, ortho, own, other, tiles):
    rows, cols = momentum.shape
    chunks, count, rank = own.shape
    width = cols // TILES
    tile = (tiles, rows, width)
    part = (chunks // TILES * tiles, count, rank)
    return pl.pallas_call(
        early_kernel,
        in_specs=[IN_SMEM, HBM, HBM, IN_VMEM, HBM, HBM],
        out_specs=HBM,
        out_shape=jax.ShapeDtypeStruct((rows, cols), F32),
        scratch_shapes=[
            VMEM(tile, F32), VMEM(tile, BF16), VMEM(part, F32), VMEM(part, F32),
            VMEM(tile, F32), VMEM((tiles * width, rank), BF16),
            pltpu.SemaphoreType.DMA((tiles, 4)), pltpu.SemaphoreType.DMA((tiles,)),
        ],
        compiler_params=pltpu.CompilerParams(vmem_limit_bytes=53 * 2**20),
        cost_estimate=pl.CostEstimate(
            flops=2 * rows * cols * rank, bytes_accessed=rows * cols * 18, transcendentals=0
        ),
    )(core, momentum, gradient, ortho, own, other)


def late_kernel(place_ref, mom_ref, grad_ref, weight_ref, got_ref, ortho_ref, own_ref, other_ref,
                begun_ref, new_mom_ref, new_weight_ref, basis_ref,
                mom, grad, weight, own, other, new_mom, new_weight, hi, lo,
                load_sems, store_sems, *, early, scale, total_cols):
    tiles, rows, width = weight.shape
    chunks, count, _ = own.shape
    per = chunks // tiles
    loads, stores = [], []
    order = list(range(early, tiles)) + list(range(early))
    for t in order:
        cols, part = pl.ds(t * width, width), pl.ds(t * per, per)
        pairs = [
            (own_ref.at[part], own.at[part]), (other_ref.at[part], other.at[part]),
            (weight_ref.at[:, cols], weight.at[t]),
        ]
        results = [(new_weight.at[t], new_weight_ref.at[:, cols])]
        if t >= early:
            pairs += [
                (mom_ref.at[:, cols], mom.at[t - early]),
                (grad_ref.at[:, cols], grad.at[t - early]),
            ]
            results.append((new_mom.at[t - early], new_mom_ref.at[:, cols]))
        loads.append(copies_of(pairs, load_sems.at[t]))
        stores.append(copies_of(results, store_sems.at[t]))
        for load in loads[-1]:
            load.start()
    sums = got_ref[0, 0:1, :]
    for i in range(1, got_ref.shape[0]):
        sums = sums + got_ref[i, 0:1, :]
    rms = jnp.sqrt(sums / total_cols + 1e-06)
    ortho = ortho_ref[...]
    first = ((1.0 - keep_rate) * ortho).astype(BF16)
    left_hi, left_lo = split(scale * ortho / rms)
    for t, load_group, store_group in zip(order, loads, stores):
        for load in load_group:
            load.wait()
        place(place_ref[0], count, per, own, other, hi, lo, t)
        right_hi = hi[t * width : (t + 1) * width, :]
        right_lo = lo[t * width : (t + 1) * width, :]
        if t >= early:
            new_mom[t - early] = (
                mom[t - early] + grad[t - early].astype(F32) - nt(first, right_hi)
            )
        change = nt(left_hi, right_hi) + nt(left_hi, right_lo) + nt(left_lo, right_hi)
        new_weight[t] = (
            (1.0 - step_size * decay_rate) * weight[t].astype(F32) - change
        ).astype(BF16)
        for store in store_group:
            store.start()
    basis_ref[...] = own[place_ref[1]] / rms
    for group in stores:
        for store in group:
            store.wait()


def update_late(where, momentum, gradient, weight, got, ortho, own, other, begun, early, scale,
                total_cols):
    rows, cols = weight.shape
    chunks, count, rank = own.shape
    tile = (TILES, rows, cols // TILES)
    rest = (TILES - early, rows, cols // TILES)
    return pl.pallas_call(
        functools.partial(late_kernel, early=early, scale=scale, total_cols=total_cols),
        in_specs=[IN_SMEM, HBM, HBM, HBM, IN_VMEM, IN_VMEM, HBM, HBM, HBM],
        out_specs=[HBM, HBM, IN_VMEM],
        out_shape=[
            jax.ShapeDtypeStruct((rows, cols), F32), jax.ShapeDtypeStruct((rows, cols), BF16),
            jax.ShapeDtypeStruct((count, rank), F32),
        ],
        scratch_shapes=[
            VMEM(rest, F32), VMEM(rest, BF16), VMEM(tile, BF16),
            VMEM(own.shape, F32), VMEM(own.shape, F32), VMEM(rest, F32), VMEM(tile, BF16),
            VMEM((cols, rank), BF16), VMEM((cols, rank), BF16),
            pltpu.SemaphoreType.DMA((TILES, 5)), pltpu.SemaphoreType.DMA((TILES, 2)),
        ],
        input_output_aliases={8: 0},
        compiler_params=pltpu.CompilerParams(vmem_limit_bytes=53 * 2**20),
        cost_estimate=pl.CostEstimate(
            flops=8 * rows * cols * rank, bytes_accessed=rows * cols * 18, transcendentals=0
        ),
    )(where, momentum, gradient, weight, got, ortho, own, other, begun)


def tn(a, b):
    return lax.dot_general(a, b, (((0,), (0,)), ((), ())), precision=HIGH, preferred_element_type=F32)


def across_cores(x):
    return lax.ppermute(x, "c", [(0, 1), (1, 0)])


def gather(x, axes, n):
    spread = jnp.broadcast_to(x[None], (n,) + x.shape)
    return lax.all_to_all(spread, axes, 0, 0)


def per_device(momentum, gradient, weight, basis):
    chips = lax.axis_size("x") * lax.axis_size("y")
    cores = lax.axis_size("c")
    depth = lax.axis_size("z")
    plane = ("x", "y")
    rows, cols = momentum.shape
    count, rank = basis.shape
    total_cols = cols * depth
    total_rows = rows * chips * cores
    core = lax.axis_index("c").astype(jnp.int32).reshape(1)

    keep, send = sort_columns(core, momentum, gradient, count)
    recv = across_cores(send)
    right = gather(basis, plane, chips).reshape(chips * count, rank)

    mine = jnp.dot(keep, right, precision=HIGH)
    theirs = jnp.dot(recv, right, precision=HIGH)
    partial = mine + across_cores(theirs)
    share = rows // depth
    piece = jnp.sum(lax.all_to_all(partial.reshape(depth, share, rank), "z", 0, 0), axis=0)
    proj = gather(piece, "z", depth).reshape(rows, rank)
    proj_other = across_cores(proj)

    raw = tn(keep, proj) + tn(recv, proj_other)
    gram_part = tn(proj, proj) + tn(proj_other, proj_other)
    gram_share = rank // chips
    packed = jnp.concatenate(
        [raw.reshape(chips, count, rank), gram_part.reshape(chips, gram_share, rank)], axis=1
    )
    summed = jnp.sum(lax.all_to_all(packed, plane, 0, 0), axis=0)
    everything = gather(summed, plane, chips)
    back, ortho, sums = factor(everything, proj, cores * depth)
    back_other = across_cores(back)
    sums = lax.all_to_all(sums, ("c", "z"), 0, 0)
    early = 2
    begun = update_early(core, momentum, gradient, ortho, back, back_other, early)
    sums, begun = lax.optimization_barrier((sums, begun))
    chip = (lax.axis_index("x") * lax.axis_size("y") + lax.axis_index("y")).astype(jnp.int32)
    where = jnp.concatenate([core, chip.reshape(1)])
    scale = step_size * math.sqrt(total_cols / total_rows)
    new_momentum, new_weight, new_basis = update_late(
        where, momentum, gradient, weight, sums, ortho, back, back_other, begun, early, scale,
        total_cols,
    )
    return new_momentum, new_weight, new_basis


def solution(mesh):
    fsdp, depth = mesh.devices.shape
    grid = Mesh(mesh.devices.reshape(4, 4, 2, depth), ("x", "y", "c", "z"))
    block = P(("x", "y", "c"), "z")
    rows = P(("z", "x", "y", "c"), None)
    return jax.shard_map(
        per_device, mesh=grid, in_specs=(block, block, block, rows),
        out_specs=(block, block, rows), check_vma=False,
    )
```

time: 499 us -> 175 us (0.35)
  waiting for transfers between devices: 362 us -> 3.69 us
  blocking collectives: 13.7 us -> 121 us
  other arithmetic: 57.8 us -> 0.44 us
  matrix products: 40.6 us -> 7.62 us
  Pallas kernels: 0 us -> 25.6 us
  starting transfers between devices: 0.34 us -> 15.2 us
  between operations: 15.2 us -> 0.94 us
    psum x3 -> x0, waiting for transfers between devices: 303 us -> none  [the longest x1 121 us: per_device(): back = lax.psum(local_back, 'fsdp')]
    all_to_all x0 -> x5, blocking collectives: none -> 121 us  [the longest x3 71.6 us: gather(): return lax.all_to_all(spread, axes, 0, 0)]
    all_gather x1 -> x0, waiting for transfers between devices: 57.5 us -> none  [per_device(): lax.all_gather(basis, 'fsdp', axis=0, tiled=True)]
    another operation x9 -> x0, other arithmetic: 53.7 us -> none  [the longest x6 33.9 us: orthonormalize(): lower = jnp.linalg.cholesky(gram)]
    dot_general x5 -> x6, matrix products: 39.2 us -> 7.62 us  [the longest x4 5.58 us: tn(): lax.dot_general(a, b, (((0,), (0,)), ((), ())), precision=HIGH, preferred...]
    pallas_call x0 -> x4, Pallas kernels: none -> 25.6 us  [the longest x1 10.5 us: factor(): pl.pallas_call(factor_kernel, out_shape=[jax.ShapeDtypeStruct((chips, pac...]
    psum x1 -> x0, blocking collectives: 13.7 us -> none  [per_device(): sums = lax.psum(jnp.sum(back * back, axis=0), 'tensor')]
    ppermute x0 -> x4, starting transfers between devices: none -> 11.8 us  [across_cores(): return lax.ppermute(x, 'c', [(0, 1), (1, 0)])]
  transfers between devices with their start and end apart: 4 -> 5, of which waited for: 4 -> 2; matrix products, arithmetic and copies ran while one was open for 0% -> 3% of each run, Pallas kernels for 0% -> 2%
where the time goes in v3:
time: 175 us
  blocking collectives  121 us (69%)
  Pallas kernels  25.6 us (15%)
  starting transfers between devices  15.2 us (9%)
  matrix products  7.62 us (4%)
  waiting for transfers between devices  3.69 us (2%)
    all_to_all x3, blocking collectives, gather(): return lax.all_to_all(spread, axes, 0, 0)  71.6 us
    all_to_all x1, blocking collectives, per_device(): summed = jnp.sum(lax.all_to_all(packed, plane, 0, 0), axis=0)  30.1 us
    all_to_all x1, blocking collectives, per_device(): lax.all_to_all(partial.reshape(depth, share, rank), 'z', 0, 0)  19.1 us
    ppermute x4, starting transfers between devices, across_cores(): return lax.ppermute(x, 'c', [(0, 1), (1, 0)])  11.8 us
    pallas_call x1, Pallas kernels, factor(): pl.pallas_call(factor_kernel, out_shape=[jax.ShapeDtypeStruct((chips, pac...  10.5 us
    pallas_call x1, Pallas kernels, update_late(): pl.pallas_call(functools.partial(late_kernel, early=early, scale=scale, t...  7.05 us
    dot_general x4, matrix products, tn(): lax.dot_general(a, b, (((0,), (0,)), ((), ())), precision=HIGH, preferred...  5.58 us
    pallas_call x1, Pallas kernels, sort_columns(): pl.pallas_call(lambda *refs: sort_columns_kernel(*refs, count=count), in_...  4.43 us
  transfers between devices with their start and end apart: 5, of which 2 were waited for; matrix products, arithmetic and copies ran while one was open for 3% of the time, Pallas kernels for 2%

profile of v3, /device:TPU:1, one launch (start us, length us, event | category | flops | bytes accessed | tf_op | source)
XLA Modules:
  0.0 174.6 jit_solution(18186679270055671701)
XLA Ops:
  0.6 0.0 copy-start.2
  0.6 4.4 %shard_map.67 = (f32[256,1792]{1,0:T(8,128)}, f32[256,1792]{1,0:T(8,128)}) custom-call(s32[1]{0:T(128)} %bitcast.refs_0_.core_ref, f32[256,3584]{1,0:T(8,128)} %mom_ref.3, bf16[256,3584]{1,0:T(8,128)(2,1)} %grad_ref.3), custom_call_target="tpu_custom_call" | custom-call | flops 917504 | bytes 9175040 | tf_op jit(solution)/shard_map/pallas_call | solution.py:90
  5.1 3.4 %collective-permute-start = (f32[256,1792]{1,0:T(8,128)}, f32[256,1792]{1,0:T(8,128)S(1)}, u32[]{:S(2)}, u32[]{:S(2)}) collective-permute-start(f32[256,1792]{1,0:T(8,128)} %get-tuple-element.11), channel_id=1, source_target_pairs={{0,8},{8,0},{1,9},{9,1},{2,10},{10,2},{3,11},{11,3},{4,12},{12,4},... | collective-permute-start | bytes 5505032 | tf_op jit(solution)/shard_map/ppermute | solution.py:388
  8.5 0.0 copy-done.2
  8.5 0.2 broadcast_in_dim.6
  8.7 29.5 %all_to_all.30 = f32[16,112,256]{2,1,0:T(8,128)S(1)} all-to-all(f32[16,112,256]{2,1,0:T(8,128)S(1)} %broadcast_in_dim.6), channel_id=1, replica_groups=mesh['x'=4,'y'=4,'c'=2,'z'=8] {'x','y'}, dimensions={0} | all-to-all | bytes 3670016 | tf_op jit(solution)/shard_map/all_to_all | solution.py:393
  38.2 0.0 collective-permute-done
  38.2 0.0 copy-start.1
  38.2 1.0 fusion.1
  39.2 1.7 collective-permute-start.1
  40.9 0.0 copy-done.1
  40.9 1.0 fusion
  42.0 0.1 collective-permute-done.1
  42.1 19.1 %all_to_all.31 = f32[8,32,256]{2,1,0:T(8,128)S(1)} all-to-all(f32[8,32,256]{2,1,0:T(8,128)S(1)} %bitcast.27), channel_id=1, replica_groups=mesh['x'=4,'y'=4,'c'=2,'z'=8] {'z'}, dimensions={0} | all-to-all | bytes 524288 | tf_op jit(solution)/shard_map/all_to_all | solution.py:415
  61.3 12.1 %all_to_all.32 = f32[8,32,256]{2,1,0:T(8,128)S(1)} all-to-all(f32[8,32,256]{2,1,0:T(8,128)S(1)} %broadcast_in_dim.7), channel_id=1, replica_groups=mesh['x'=4,'y'=4,'c'=2,'z'=8] {'z'}, dimensions={0} | all-to-all | bytes 524288 | tf_op jit(solution)/shard_map/all_to_all | solution.py:393
  73.3 3.2 %collective-permute-start.2 = (f32[256,256]{1,0:T(8,128)S(1)}, f32[256,256]{1,0:T(8,128)S(1)}, u32[]{:S(2)}, u32[]{:S(2)}) collective-permute-start(f32[256,256]{1,0:T(8,128)S(1)} %bitcast.21), channel_id=1, source_target_pairs={{0,8},{8,0},{1,9},{9,1},{2,10},{10,2},{3,11},{11,3},{4,12},{12,4},... | collective-permute-start | bytes 786440 | tf_op jit(solution)/shard_map/ppermute | solution.py:388
  76.5 0.4 convolution_bitcast_fusion
  76.9 3.1 %fusion.2 = f32[1792,256]{1,0:T(8,128)S(1)} fusion(f32[256,1792]{1,0:T(8,128)} %get-tuple-element.10, f32[256,256]{1,0:T(8,128)S(1)} %bitcast.22), kind=kOutput, calls=%fused_computation.7 | convolution fusion | flops 704643072 | bytes 3932160 | tf_op jit(solution)/shard_map/dot_general | solution.py:384
  80.0 0.0 collective-permute-done.2
  80.0 1.7 convolution_add_fusion
  81.7 0.4 convolution_add_fusion.1
  82.1 0.2 pad_maximum_fusion
  82.3 30.1 %all_to_all.33 = f32[16,128,256]{2,1,0:T(8,128)S(1)} all-to-all(f32[16,128,256]{2,1,0:T(8,128)S(1)} %pad_maximum_fusion), channel_id=1, replica_groups=mesh['x'=4,'y'=4,'c'=2,'z'=8] {'x','y'}, dimensions={0} | all-to-all | bytes 4194304 | tf_op jit(solution)/shard_map/all_to_all | solution.py:425
  112.4 0.1 reduce_sum.19
  112.6 0.2 broadcast_in_dim.8
  112.8 30.0 %all_to_all.34.got_ref = f32[16,128,256]{2,1,0:T(8,128)S(1)} all-to-all(f32[16,128,256]{2,1,0:T(8,128)S(1)} %broadcast_in_dim.8), channel_id=1, replica_groups=mesh['x'=4,'y'=4,'c'=2,'z'=8] {'x','y'}, dimensions={0} | all-to-all | bytes 4194304 | tf_op jit(solution)/shard_map/all_to_all | solution.py:393
  142.8 10.5 %shard_map.68 = (f32[16,112,256]{2,1,0:T(8,128)S(1)}, f32[256,256]{1,0:T(8,128)S(1)}, f32[16,8,256]{2,1,0:T(8,128)}) custom-call(f32[16,128,256]{2,1,0:T(8,128)S(1)} %all_to_all.34.got_ref, f32[256,256]{1,0:T(8,128)S(1)} %bitcast.23), custom_call_target="tpu_custom_call" | custom-call | flops 671088640 | bytes 1048576 | tf_op jit(solution)/shard_map/pallas_call | solution.py:222
  153.3 0.0 copy-start
  153.3 3.4 %collective-permute-start.3 = (f32[16,112,256]{2,1,0:T(8,128)S(1)}, f32[16,112,256]{2,1,0:T(8,128)}, u32[]{:S(2)}, u32[]{:S(2)}) collective-permute-start(f32[16,112,256]{2,1,0:T(8,128)S(1)} %get-tuple-element.14.own_ref), channel_id=1, source_target_pairs={{0,8},{8,0},{1,9},{9,1},{2,10},{10,2},{3,11},{11,3},{4,12},{12,4},... | collective-permute-start | bytes 5505032 | tf_op jit(solution)/shard_map/ppermute | solution.py:388
  156.7 3.4 %all-to-all-start.5 = ((f32[16,8,256]{2,1,0:T(8,128)}), f32[16,8,256]{2,1,0:T(8,128)S(1)}, u32[]{:S(2)}, u32[]{:S(2)}) async-start(f32[16,8,256]{2,1,0:T(8,128)} %get-tuple-element.12), calls=%async_computation.5 | async-start | bytes 262144 | tf_op jit(solution)/shard_map/all_to_all | solution.py:429
  160.1 0.1 pad_add_fusion.place_ref
  160.2 0.0 collective-permute-done.3.other_ref
  160.3 0.0 copy-done
  160.3 3.7 %shard_map.69.begun_ref = f32[256,3584]{1,0:T(8,128)} custom-call(s32[1]{0:T(128)} %bitcast.refs_0_.core_ref, f32[256,3584]{1,0:T(8,128)} %mom_ref.3, bf16[256,3584]{1,0:T(8,128)(2,1)} %grad_ref.3, f32[256,256]{1,0:T(8,128)S(1)} %get-tuple-element.13.ortho_ref, f32[16,112,256]{2,1,0:T(8,128)} %copy-done, f32[16,112,256]{2,1,0:T(8,128)} %collective-permute-done.3.other_ref), custom_call_target="tpu_custom_call" | custom-call | flops 469762048 | bytes 16515072 | tf_op jit(solution)/shard_map/pallas_call | solution.py:283
  163.9 3.5 %all-to-all-done.5.got_ref = f32[16,8,256]{2,1,0:T(8,128)S(1)} async-done(((f32[16,8,256]{2,1,0:T(8,128)}), f32[16,8,256]{2,1,0:T(8,128)S(1)}, u32[]{:S(2)}, u32[]{:S(2)}) %all-to-all-start.5) | async-done | bytes 131104 | tf_op jit(solution)/shard_map/all_to_all | solution.py:429
  167.4 7.0 %shard_map.70 = (f32[256,3584]{1,0:T(8,128)}, bf16[256,3584]{1,0:T(8,128)(2,1)}, f32[112,256]{1,0:T(8,128)}) custom-call(s32[2]{0:T(128)S(1)} %pad_add_fusion.place_ref, f32[256,3584]{1,0:T(8,128)} %mom_ref.3, bf16[256,3584]{1,0:T(8,128)(2,1)} %grad_ref.3, bf16[256,3584]{1,0:T(8,128)(2,1)} %weight_ref.1, ...), custom_call_target="tpu_custom_call", output_to_operand_aliasing={{0}: (8, {})} | custom-call | flops 1879048192 | bytes 16515072 | tf_op jit(solution)/shard_map/pallas_call | solution.py:361
  (3 shorter events, 0.1 us)
Async XLA Ops:
  0.6 7.9 %copy-start.2 = (f32[112,256]{1,0:T(8,128)S(1)}, f32[112,256]{1,0:T(8,128)}, u32[]{:S(2)}) copy-start(f32[112,256]{1,0:T(8,128)} %param.7) | copy-start | bytes 344068
  5.1 33.1 %collective-permute-start = (f32[256,1792]{1,0:T(8,128)}, f32[256,1792]{1,0:T(8,128)S(1)}, u32[]{:S(2)}, u32[]{:S(2)}) collective-permute-start(f32[256,1792]{1,0:T(8,128)} %get-tuple-element.11), channel_id=1, source_target_pairs={{0,8},{8,0},{1,9},{9,1},{2,10},{10,2},{3,11},{11,3},{4,12},{12,4},... | collective-permute-start | bytes 5505032 | tf_op jit(solution)/shard_map/ppermute | solution.py:388
  38.2 2.8 %copy-start.1 = (f32[256,1792]{1,0:T(8,128)S(1)}, f32[256,1792]{1,0:T(8,128)}, u32[]{:S(2)}) copy-start(f32[256,1792]{1,0:T(8,128)} %get-tuple-element.10) | copy-start | bytes 5505028
  39.2 2.9 %collective-permute-start.1 = (f32[256,256]{1,0:T(8,128)S(1)}, f32[256,256]{1,0:T(8,128)S(1)}, u32[]{:S(2)}, u32[]{:S(2)}) collective-permute-start(f32[256,256]{1,0:T(8,128)S(1)} %fusion.1), channel_id=1, source_target_pairs={{0,8},{8,0},{1,9},{9,1},{2,10},{10,2},{3,11},{11,3},{4,12},{12,4},... | collective-permute-start | bytes 786440 | tf_op jit(solution)/shard_map/ppermute | solution.py:388
  73.3 6.7 %collective-permute-start.2 = (f32[256,256]{1,0:T(8,128)S(1)}, f32[256,256]{1,0:T(8,128)S(1)}, u32[]{:S(2)}, u32[]{:S(2)}) collective-permute-start(f32[256,256]{1,0:T(8,128)S(1)} %bitcast.21), channel_id=1, source_target_pairs={{0,8},{8,0},{1,9},{9,1},{2,10},{10,2},{3,11},{11,3},{4,12},{12,4},... | collective-permute-start | bytes 786440 | tf_op jit(solution)/shard_map/ppermute | solution.py:388
  153.3 7.0 %copy-start = (f32[16,112,256]{2,1,0:T(8,128)}, f32[16,112,256]{2,1,0:T(8,128)S(1)}, u32[]{:S(2)}) copy-start(f32[16,112,256]{2,1,0:T(8,128)S(1)} %get-tuple-element.14.own_ref) | copy-start | bytes 5505028
  153.3 7.0 %collective-permute-start.3 = (f32[16,112,256]{2,1,0:T(8,128)S(1)}, f32[16,112,256]{2,1,0:T(8,128)}, u32[]{:S(2)}, u32[]{:S(2)}) collective-permute-start(f32[16,112,256]{2,1,0:T(8,128)S(1)} %get-tuple-element.14.own_ref), channel_id=1, source_target_pairs={{0,8},{8,0},{1,9},{9,1},{2,10},{10,2},{3,11},{11,3},{4,12},{12,4},... | collective-permute-start | bytes 5505032 | tf_op jit(solution)/shard_map/ppermute | solution.py:388
  156.7 10.7 %all-to-all-start.5 = ((f32[16,8,256]{2,1,0:T(8,128)}), f32[16,8,256]{2,1,0:T(8,128)S(1)}, u32[]{:S(2)}, u32[]{:S(2)}) async-start(f32[16,8,256]{2,1,0:T(8,128)} %get-tuple-element.12), calls=%async_computation.5 | async-start | bytes 262144 | tf_op jit(solution)/shard_map/all_to_all | solution.py:429

commit v4 on v3

--- a/solution.py
+++ b/solution.py
@@ -31,6 +31,10 @@
 
 def nt(a, b):
     return lax.dot_general(a, b, (((1,), (1,)), ((), ())), preferred_element_type=F32)
+
+
+def nn(a, b):
+    return lax.dot_general(a, b, (((1,), (0,)), ((), ())), preferred_element_type=F32)
 
 
 def copies_of(pairs, sems):
@@ -357,7 +361,7 @@
     rows, cols = weight.shape
     chunks, count, rank = own.shape
     tile = (TILES, rows, cols // TILES)
-    rest = (TILES - early, rows, cols // TILES)
+    rest = (max(TILES - early, 1), rows, cols // TILES)
     return pl.pallas_call(
         functools.partial(late_kernel, early=early, scale=scale, total_cols=total_cols),
         in_specs=[IN_SMEM, HBM, HBM, HBM, IN_VMEM, IN_VMEM, HBM, HBM, HBM],
@@ -380,8 +384,42 @@
     )(where, momentum, gradient, weight, got, ortho, own, other, begun)
 
 
-def tn(a, b):
-    return lax.dot_general(a, b, (((0,), (0,)), ((), ())), precision=HIGH, preferred_element_type=F32)
+def project_back_kernel(keep_ref, recv_ref, proj_ref, other_ref, out_ref):
+    chips, packed, rank = out_ref.shape
+    share = rank // chips
+    count = packed - share
+    proj = jnp.concatenate([proj_ref[...], other_ref[...]], axis=0)
+    left_hi, left_lo = split(proj.T)
+    per = 8
+    width = per * count
+
+    def product(right):
+        hi, lo = split(right)
+        return nn(left_hi, hi) + nn(left_hi, lo) + nn(left_lo, hi)
+
+    gram = product(proj)
+    for i in range(chips):
+        out_ref[i, count:, :] = gram[i * share : (i + 1) * share, :]
+    for t in range(chips // per):
+        cols = slice(t * width, (t + 1) * width)
+        raw = product(jnp.concatenate([keep_ref[:, cols], recv_ref[:, cols]], axis=0)).T
+        for i in range(per):
+            out_ref[t * per + i, :count, :] = raw[i * count : (i + 1) * count, :]
+
+
+def project_back(keep, recv, proj, other, chips):
+    rows, cols = keep.shape
+    rank = proj.shape[1]
+    return pl.pallas_call(
+        project_back_kernel,
+        in_specs=[IN_VMEM] * 4,
+        out_specs=IN_VMEM,
+        out_shape=jax.ShapeDtypeStruct((chips, cols // chips + rank // chips, rank), F32),
+        compiler_params=pltpu.CompilerParams(vmem_limit_bytes=24 * 2**20),
+        cost_estimate=pl.CostEstimate(
+            flops=12 * rows * cols * rank, bytes_accessed=rows * cols * 8, transcendentals=0
+        ),
+    )(keep, recv, proj, other)
 
 
 def across_cores(x):
@@ -405,7 +443,8 @@
     core = lax.axis_index("c").astype(jnp.int32).reshape(1)
 
     keep, send = sort_columns(core, momentum, gradient, count)
-    recv = across_cores(send)
+    pieces = 4
+    recv = jnp.concatenate([across_cores(piece) for piece in jnp.split(send, pieces, axis=0)])
     right = gather(basis, plane, chips).reshape(chips * count, rank)
 
     mine = jnp.dot(keep, right, precision=HIGH)
@@ -416,18 +455,13 @@
     proj = gather(piece, "z", depth).reshape(rows, rank)
     proj_other = across_cores(proj)
 
-    raw = tn(keep, proj) + tn(recv, proj_other)
-    gram_part = tn(proj, proj) + tn(proj_other, proj_other)
-    gram_share = rank // chips
-    packed = jnp.concatenate(
-        [raw.reshape(chips, count, rank), gram_part.reshape(chips, gram_share, rank)], axis=1
-    )
+    packed = project_back(keep, recv, proj, proj_other, chips)
     summed = jnp.sum(lax.all_to_all(packed, plane, 0, 0), axis=0)
     everything = gather(summed, plane, chips)
     back, ortho, sums = factor(everything, proj, cores * depth)
     back_other = across_cores(back)
     sums = lax.all_to_all(sums, ("c", "z"), 0, 0)
-    early = 2
+    early = TILES
     begun = update_early(core, momentum, gradient, ortho, back, back_other, early)
     sums, begun = lax.optimization_barrier((sums, begun))
     chip = (lax.axis_index("x") * lax.axis_size("y") + lax.axis_index("y")).astype(jnp.int32)

time: 175 us -> 176 us (level)
  blocking collectives: 121 us -> 95.1 us
  waiting for transfers between devices: 3.69 us -> 18.6 us
  starting transfers between devices: 15.2 us -> 20.8 us
  local copies, waits for them, and re-layouts: 0.4 us -> 5.74 us
  Pallas kernels: 25.6 us -> 29.1 us
  matrix products: 7.62 us -> 5.03 us
    all_to_all x3 -> x2, blocking collectives: 71.6 us -> 44.2 us  [gather(): return lax.all_to_all(spread, axes, 0, 0)]
    all_to_all x0 -> x1, waiting for transfers between devices: none -> 13.3 us  [gather(): return lax.all_to_all(spread, axes, 0, 0)]
    all_to_all x0 -> x1, starting transfers between devices: none -> 7.63 us  [gather(): return lax.all_to_all(spread, axes, 0, 0)]
    dot_general x4 -> x0, matrix products: 5.58 us -> none  [tn(): lax.dot_general(a, b, (((0,), (0,)), ((), ())), precision=HIGH, preferred...]
    ppermute x4 -> x7, waiting for transfers between devices: 0.19 us -> 3.94 us  [across_cores(): return lax.ppermute(x, 'c', [(0, 1), (1, 0)])]
    pallas_call x0 -> x1, Pallas kernels: none -> 2.16 us  [project_back(): pl.pallas_call(project_back_kernel, in_specs=[IN_VMEM] * 4, out_specs=IN_...]
    broadcast_in_dim x3, local copies, waits for them, and re-layouts: 0.38 us -> 2.53 us  [gather(): spread = jnp.broadcast_to(x[None], (n,) + x.shape)]
    all_to_all x1, waiting for transfers between devices: 3.5 us -> 1.41 us  [per_device(): sums = lax.all_to_all(sums, ('c', 'z'), 0, 0)]
  transfers between devices with their start and end apart: 5 -> 9, of which waited for: 2 -> 6; matrix products, arithmetic and copies ran while one was open for 3% -> 2% of each run, Pallas kernels for 2% -> 6%
where the time goes in v4:
time: 176 us
  blocking collectives  95.1 us (54%)
  Pallas kernels  29.1 us (17%)
  starting transfers between devices  20.8 us (12%)
  waiting for transfers between devices  18.6 us (11%)
  local copies, waits for them, and re-layouts  5.74 us (3%)
  matrix products  5.03 us (3%)
    all_to_all x2, blocking collectives, gather(): return lax.all_to_all(spread, axes, 0, 0)  44.2 us
    all_to_all x1, blocking collectives, per_device(): summed = jnp.sum(lax.all_to_all(packed, plane, 0, 0), axis=0)  30.5 us
    all_to_all x1, blocking collectives, per_device(): lax.all_to_all(partial.reshape(depth, share, rank), 'z', 0, 0)  20.4 us
    all_to_all x1, waiting for transfers between devices, gather(): return lax.all_to_all(spread, axes, 0, 0)  13.3 us
    pallas_call x1, Pallas kernels, factor(): pl.pallas_call(factor_kernel, out_shape=[jax.ShapeDtypeStruct((chips, pac...  10.5 us
    ppermute x7, starting transfers between devices, across_cores(): return lax.ppermute(x, 'c', [(0, 1), (1, 0)])  9.81 us
    all_to_all x1, starting transfers between devices, gather(): return lax.all_to_all(spread, axes, 0, 0)  7.63 us
    pallas_call x1, Pallas kernels, update_late(): pl.pallas_call(functools.partial(late_kernel, early=early, scale=scale, t...  6.37 us
  transfers between devices with their start and end apart: 9, of which 6 were waited for; matrix products, arithmetic and copies ran while one was open for 2% of the time, Pallas kernels for 6%

profile of v4, /device:TPU:1, one launch (start us, length us, event | category | flops | bytes accessed | tf_op | source)
XLA Modules:
  0.0 175.7 jit_solution(14307247590841566352)
XLA Ops:
  0.6 2.3 %broadcast_in_dim.6 = f32[16,112,256]{2,1,0:T(8,128)} broadcast(f32[112,256]{1,0:T(8,128)} %param.7), dimensions={1,2} | broadcast | bytes 1949696 | tf_op jit(solution)/shard_map/broadcast_in_dim | solution.py:430
  2.9 7.6 %all-to-all-start = ((f32[16,112,256]{2,1,0:T(8,128)}), f32[16,112,256]{2,1,0:T(8,128)}, u32[]{:S(2)}, u32[]{:S(2)}) async-start(f32[16,112,256]{2,1,0:T(8,128)} %broadcast_in_dim.6), calls=%async_computation | async-start | bytes 3670016 | tf_op jit(solution)/shard_map/all_to_all | solution.py:431
  10.6 4.4 %shard_map.67 = (f32[256,1792]{1,0:T(8,128)}, f32[256,1792]{1,0:T(8,128)}) custom-call(s32[1]{0:T(128)} %bitcast.refs_0_.core_ref, f32[256,3584]{1,0:T(8,128)} %mom_ref.3, bf16[256,3584]{1,0:T(8,128)(2,1)} %grad_ref.3), custom_call_target="tpu_custom_call" | custom-call | flops 917504 | bytes 9175040 | tf_op jit(solution)/shard_map/pallas_call | solution.py:94
  15.0 1.6 fusion
  16.6 1.1 collective-permute-start
  17.7 0.1 collective-permute-start.1
  17.8 0.4 collective-permute-start.3
  18.2 0.1 collective-permute-start.2
  18.3 0.8 collective-permute-done
  19.2 0.6 collective-permute-done.1
  19.8 1.3 collective-permute-done.2
  21.2 0.0 collective-permute-done.3
  21.2 13.3 %all-to-all-done = f32[16,112,256]{2,1,0:T(8,128)} async-done(((f32[16,112,256]{2,1,0:T(8,128)}), f32[16,112,256]{2,1,0:T(8,128)}, u32[]{:S(2)}, u32[]{:S(2)}) %all-to-all-start) | async-done | bytes 1835040 | tf_op jit(solution)/shard_map/all_to_all | solution.py:431
  34.5 0.0 copy-start
  34.5 2.6 %fusion.2 = f32[256,256]{1,0:T(8,128)S(1)} fusion(f32[256,1792]{1,0:T(8,128)S(1)} %constant_dynamic-update-slice_fusion.recv_ref, f32[1792,256]{1,0:T(8,128)} %bitcast.2), kind=kOutput, calls=%fused_computation.7 | convolution fusion | flops 704643072 | bytes 3932160 | tf_op jit(solution)/shard_map/dot_general | solution.py:451
  37.1 4.2 %collective-permute-start.4 = (f32[256,256]{1,0:T(8,128)S(1)}, f32[256,256]{1,0:T(8,128)S(1)}, u32[]{:S(2)}, u32[]{:S(2)}) collective-permute-start(f32[256,256]{1,0:T(8,128)S(1)} %fusion.2), channel_id=1, source_target_pairs={{0,8},{8,0},{1,9},{9,1},{2,10},{10,2},{3,11},{11,3},{4,12},{12,4},... | collective-permute-start | bytes 786440 | tf_op jit(solution)/shard_map/ppermute | solution.py:426
  41.3 0.0 copy-done
  41.3 2.5 %fusion.1 = f32[256,256]{1,0:T(8,128)S(1)} fusion(f32[256,1792]{1,0:T(8,128)S(1)} %copy-done, f32[1792,256]{1,0:T(8,128)} %bitcast.2), kind=kOutput, calls=%fused_computation.6 | convolution fusion | flops 704643072 | bytes 3932160 | tf_op jit(solution)/shard_map/dot_general | solution.py:450
  43.8 0.0 collective-permute-done.4
  43.8 20.4 %all_to_all.30 = f32[8,32,256]{2,1,0:T(8,128)S(1)} all-to-all(f32[8,32,256]{2,1,0:T(8,128)S(1)} %bitcast.12), channel_id=1, replica_groups=mesh['x'=4,'y'=4,'c'=2,'z'=8] {'z'}, dimensions={0} | all-to-all | bytes 524288 | tf_op jit(solution)/shard_map/all_to_all | solution.py:454
  64.2 14.7 %all_to_all.31 = f32[8,32,256]{2,1,0:T(8,128)S(1)} all-to-all(f32[8,32,256]{2,1,0:T(8,128)S(1)} %broadcast_in_dim.7), channel_id=1, replica_groups=mesh['x'=4,'y'=4,'c'=2,'z'=8] {'z'}, dimensions={0} | all-to-all | bytes 524288 | tf_op jit(solution)/shard_map/all_to_all | solution.py:431
  78.9 0.6 collective-permute-start.5
  79.5 1.2 collective-permute-done.5.other_ref
  80.6 0.0 copy-start.1
  80.6 1.5 copy-done.1
  82.1 2.2 %shard_map.68 = f32[16,128,256]{2,1,0:T(8,128)S(1)} custom-call(f32[256,1792]{1,0:T(8,128)S(1)} %copy-done.1, f32[256,1792]{1,0:T(8,128)S(1)} %constant_dynamic-update-slice_fusion.recv_ref, f32[256,256]{1,0:T(8,128)S(1)} %bitcast.10, f32[256,256]{1,0:T(8,128)S(1)} %collective-permute-done.5.other_ref), custom_call_target="tpu_custom_call" | custom-call | flops 1409286144 | bytes 3670016 | tf_op jit(solution)/shard_map/pallas_call | solution.py:413
  84.3 30.5 %all_to_all.32 = f32[16,128,256]{2,1,0:T(8,128)S(1)} all-to-all(f32[16,128,256]{2,1,0:T(8,128)S(1)} %shard_map.68), channel_id=1, replica_groups=mesh['x'=4,'y'=4,'c'=2,'z'=8] {'x','y'}, dimensions={0} | all-to-all | bytes 4194304 | tf_op jit(solution)/shard_map/all_to_all | solution.py:459
  114.8 0.1 reduce_sum.19
  115.0 0.2 broadcast_in_dim.8
  115.2 29.6 %all_to_all.33.got_ref = f32[16,128,256]{2,1,0:T(8,128)S(1)} all-to-all(f32[16,128,256]{2,1,0:T(8,128)S(1)} %broadcast_in_dim.8), channel_id=1, replica_groups=mesh['x'=4,'y'=4,'c'=2,'z'=8] {'x','y'}, dimensions={0} | all-to-all | bytes 4194304 | tf_op jit(solution)/shard_map/all_to_all | solution.py:431
  144.7 10.5 %shard_map.69 = (f32[16,112,256]{2,1,0:T(8,128)S(1)}, f32[256,256]{1,0:T(8,128)S(1)}, f32[16,8,256]{2,1,0:T(8,128)}) custom-call(f32[16,128,256]{2,1,0:T(8,128)S(1)} %all_to_all.33.got_ref, f32[256,256]{1,0:T(8,128)S(1)} %bitcast.11), custom_call_target="tpu_custom_call" | custom-call | flops 671088640 | bytes 1048576 | tf_op jit(solution)/shard_map/pallas_call | solution.py:226
  155.2 0.0 copy-start.2
  155.2 3.3 %collective-permute-start.6 = (f32[16,112,256]{2,1,0:T(8,128)S(1)}, f32[16,112,256]{2,1,0:T(8,128)}, u32[]{:S(2)}, u32[]{:S(2)}) collective-permute-start(f32[16,112,256]{2,1,0:T(8,128)S(1)} %get-tuple-element.14.own_ref), channel_id=1, source_target_pairs={{0,8},{8,0},{1,9},{9,1},{2,10},{10,2},{3,11},{11,3},{4,12},{12,4},... | collective-permute-start | bytes 5505032 | tf_op jit(solution)/shard_map/ppermute | solution.py:426
  158.5 3.4 %all-to-all-start.5 = ((f32[16,8,256]{2,1,0:T(8,128)}), f32[16,8,256]{2,1,0:T(8,128)S(1)}, u32[]{:S(2)}, u32[]{:S(2)}) async-start(f32[16,8,256]{2,1,0:T(8,128)} %get-tuple-element.12), calls=%async_computation.5 | async-start | bytes 262144 | tf_op jit(solution)/shard_map/all_to_all | solution.py:463
  161.9 0.1 pad_add_fusion.place_ref
  162.0 0.0 collective-permute-done.6.other_ref
  162.0 0.0 copy-done.2
  162.0 5.7 %shard_map.70.begun_ref = f32[256,3584]{1,0:T(8,128)} custom-call(s32[1]{0:T(128)} %bitcast.refs_0_.core_ref, f32[256,3584]{1,0:T(8,128)} %mom_ref.3, bf16[256,3584]{1,0:T(8,128)(2,1)} %grad_ref.3, f32[256,256]{1,0:T(8,128)S(1)} %get-tuple-element.13.ortho_ref, f32[16,112,256]{2,1,0:T(8,128)} %copy-done.2, f32[16,112,256]{2,1,0:T(8,128)} %collective-permute-done.6.other_ref), custom_call_target="tpu_custom_call" | custom-call | flops 469762048 | bytes 16515072 | tf_op jit(solution)/shard_map/pallas_call | solution.py:287
  167.8 1.4 all-to-all-done.5.got_ref
  169.2 6.4 %shard_map.71 = (f32[256,3584]{1,0:T(8,128)}, bf16[256,3584]{1,0:T(8,128)(2,1)}, f32[112,256]{1,0:T(8,128)}) custom-call(s32[2]{0:T(128)S(1)} %pad_add_fusion.place_ref, f32[256,3584]{1,0:T(8,128)} %mom_ref.3, bf16[256,3584]{1,0:T(8,128)(2,1)} %grad_ref.3, bf16[256,3584]{1,0:T(8,128)(2,1)} %weight_ref.1, ...), custom_call_target="tpu_custom_call", output_to_operand_aliasing={{0}: (8, {})} | custom-call | flops 1879048192 | bytes 16515072 | tf_op jit(solution)/shard_map/pallas_call | solution.py:365
  (7 shorter events, 0.2 us)
Async XLA Ops:
  2.9 31.5 %all-to-all-start = ((f32[16,112,256]{2,1,0:T(8,128)}), f32[16,112,256]{2,1,0:T(8,128)}, u32[]{:S(2)}, u32[]{:S(2)}) async-start(f32[16,112,256]{2,1,0:T(8,128)} %broadcast_in_dim.6), calls=%async_computation | async-start | bytes 3670016 | tf_op jit(solution)/shard_map/all_to_all | solution.py:431
  16.6 2.6 %collective-permute-start = (f32[64,1792]{1,0:T(8,128)S(1)}, f32[64,1792]{1,0:T(8,128)S(1)}, u32[]{:S(2)}, u32[]{:S(2)}) collective-permute-start(f32[64,1792]{1,0:T(8,128)S(1)} %get-tuple-element.20), channel_id=1, source_target_pairs={{0,8},{8,0},{1,9},{9,1},{2,10},{10,2},{3,11},{11,3},{4,12},{12,4},... | collective-permute-start | bytes 1376264 | tf_op jit(solution)/shard_map/ppermute | solution.py:426
  17.7 2.1 %collective-permute-start.1 = (f32[64,1792]{1,0:T(8,128)S(1)}, f32[64,1792]{1,0:T(8,128)S(1)}, u32[]{:S(2)}, u32[]{:S(2)}) collective-permute-start(f32[64,1792]{1,0:T(8,128)S(1)} %get-tuple-element.19), channel_id=1, source_target_pairs={{0,8},{8,0},{1,9},{9,1},{2,10},{10,2},{3,11},{11,3},{4,12},{12,4},... | collective-permute-start | bytes 1376264 | tf_op jit(solution)/shard_map/ppermute | solution.py:426
  17.8 3.3 %collective-permute-start.3 = (f32[64,1792]{1,0:T(8,128)S(1)}, f32[64,1792]{1,0:T(8,128)S(1)}, u32[]{:S(2)}, u32[]{:S(2)}) collective-permute-start(f32[64,1792]{1,0:T(8,128)S(1)} %get-tuple-element.17), channel_id=1, source_target_pairs={{0,8},{8,0},{1,9},{9,1},{2,10},{10,2},{3,11},{11,3},{4,12},{12,4},... | collective-permute-start | bytes 1376264 | tf_op jit(solution)/shard_map/ppermute | solution.py:426
  18.2 2.9 %collective-permute-start.2 = (f32[64,1792]{1,0:T(8,128)S(1)}, f32[64,1792]{1,0:T(8,128)S(1)}, u32[]{:S(2)}, u32[]{:S(2)}) collective-permute-start(f32[64,1792]{1,0:T(8,128)S(1)} %get-tuple-element.18), channel_id=1, source_target_pairs={{0,8},{8,0},{1,9},{9,1},{2,10},{10,2},{3,11},{11,3},{4,12},{12,4},... | collective-permute-start | bytes 1376264 | tf_op jit(solution)/shard_map/ppermute | solution.py:426
  34.5 6.8 %copy-start = (f32[256,1792]{1,0:T(8,128)S(1)}, f32[256,1792]{1,0:T(8,128)}, u32[]{:S(2)}) copy-start(f32[256,1792]{1,0:T(8,128)} %get-tuple-element.10.keep_ref) | copy-start | bytes 5505028
  37.1 6.7 %collective-permute-start.4 = (f32[256,256]{1,0:T(8,128)S(1)}, f32[256,256]{1,0:T(8,128)S(1)}, u32[]{:S(2)}, u32[]{:S(2)}) collective-permute-start(f32[256,256]{1,0:T(8,128)S(1)} %fusion.2), channel_id=1, source_target_pairs={{0,8},{8,0},{1,9},{9,1},{2,10},{10,2},{3,11},{11,3},{4,12},{12,4},... | collective-permute-start | bytes 786440 | tf_op jit(solution)/shard_map/ppermute | solution.py:426
  78.9 1.7 collective-permute-start.5
  80.6 1.5 copy-start.1
  155.2 6.8 %copy-start.2 = (f32[16,112,256]{2,1,0:T(8,128)}, f32[16,112,256]{2,1,0:T(8,128)S(1)}, u32[]{:S(2)}) copy-start(f32[16,112,256]{2,1,0:T(8,128)S(1)} %get-tuple-element.14.own_ref) | copy-start | bytes 5505028
  155.2 6.8 %collective-permute-start.6 = (f32[16,112,256]{2,1,0:T(8,128)S(1)}, f32[16,112,256]{2,1,0:T(8,128)}, u32[]{:S(2)}, u32[]{:S(2)}) collective-permute-start(f32[16,112,256]{2,1,0:T(8,128)S(1)} %get-tuple-element.14.own_ref), channel_id=1, source_target_pairs={{0,8},{8,0},{1,9},{9,1},{2,10},{10,2},{3,11},{11,3},{4,12},{12,4},... | collective-permute-start | bytes 5505032 | tf_op jit(solution)/shard_map/ppermute | solution.py:426
  158.5 10.7 %all-to-all-start.5 = ((f32[16,8,256]{2,1,0:T(8,128)}), f32[16,8,256]{2,1,0:T(8,128)S(1)}, u32[]{:S(2)}, u32[]{:S(2)}) async-start(f32[16,8,256]{2,1,0:T(8,128)} %get-tuple-element.12), calls=%async_computation.5 | async-start | bytes 262144 | tf_op jit(solution)/shard_map/all_to_all | solution.py:463

commit v5 on v4

--- a/solution.py
+++ b/solution.py
@@ -243,13 +243,12 @@
         mine = pl.ds(pl.multiple_of((2 * i + core) * count, 16), count)
         theirs = pl.ds(pl.multiple_of((2 * i + 1 - core) * count, 16), count)
         for rows, value in ((mine, own[i]), (theirs, other[i])):
-            hi[rows, :] = value.astype(BF16)
-            if lo is not None:
-                lo[rows, :] = (value - value.astype(BF16).astype(F32)).astype(BF16)
-
-
-def early_kernel(core_ref, mom_ref, grad_ref, ortho_ref, own_ref, other_ref, out_ref,
-                 mom, grad, own, other, out, hi, load_sems, store_sems):
+            hi[rows, :], lo[rows, :] = split(value)
+
+
+def early_kernel(core_ref, mom_ref, grad_ref, ortho_ref, own_ref, other_ref,
+                 out_ref, hi_ref, lo_ref,
+                 mom, grad, own, other, out, hi, lo, load_sems, store_sems):
     tiles, rows, width = mom.shape
     chunks, count, _ = own.shape
     per = chunks // tiles
@@ -263,36 +262,46 @@
             ],
             load_sems.at[t],
         ))
-        stores.append(pltpu.make_async_copy(out.at[t], out_ref.at[:, cols], store_sems.at[t]))
+        stores.append(copies_of(
+            [
+                (hi.at[cols], hi_ref.at[cols]), (lo.at[cols], lo_ref.at[cols]),
+                (out.at[t], out_ref.at[:, cols]),
+            ],
+            store_sems.at[t],
+        ))
         for load in loads[t]:
             load.start()
     left = ((1.0 - keep_rate) * ortho_ref[...]).astype(BF16)
     for t in range(tiles):
-        for load in loads[t]:
+        for load in loads[t][:2]:
             load.wait()
-        place(core_ref[0], count, per, own, other, hi, None, t)
+        place(core_ref[0], count, per, own, other, hi, lo, t)
+        for store in stores[t][:2]:
+            store.start()
         change = nt(left, hi[t * width : (t + 1) * width, :])
+        for load in loads[t][2:]:
+            load.wait()
         out[t] = mom[t] + grad[t].astype(F32) - change
-        stores[t].start()
-    for store in stores:
-        store.wait()
-
-
-def update_early(core, momentum, gradient, ortho, own, other, tiles):
+        stores[t][2].start()
+    for group in stores:
+        for store in group:
+            store.wait()
+
+
+def update_momentum(core, momentum, gradient, ortho, own, other):
     rows, cols = momentum.shape
-    chunks, count, rank = own.shape
-    width = cols // TILES
-    tile = (tiles, rows, width)
-    part = (chunks // TILES * tiles, count, rank)
+    rank = own.shape[2]
+    tile = (TILES, rows, cols // TILES)
+    part = jax.ShapeDtypeStruct((cols, rank), BF16)
     return pl.pallas_call(
         early_kernel,
         in_specs=[IN_SMEM, HBM, HBM, IN_VMEM, HBM, HBM],
-        out_specs=HBM,
-        out_shape=jax.ShapeDtypeStruct((rows, cols), F32),
+        out_specs=[HBM] * 3,
+        out_shape=[jax.ShapeDtypeStruct((rows, cols), F32), part, part],
         scratch_shapes=[
-            VMEM(tile, F32), VMEM(tile, BF16), VMEM(part, F32), VMEM(part, F32),
-            VMEM(tile, F32), VMEM((tiles * width, rank), BF16),
-            pltpu.SemaphoreType.DMA((tiles, 4)), pltpu.SemaphoreType.DMA((tiles,)),
+            VMEM(tile, F32), VMEM(tile, BF16), VMEM(own.shape, F32), VMEM(own.shape, F32),
+            VMEM(tile, F32), VMEM((cols, rank), BF16), VMEM((cols, rank), BF16),
+            pltpu.SemaphoreType.DMA((TILES, 4)), pltpu.SemaphoreType.DMA((TILES, 3)),
         ],
         compiler_params=pltpu.CompilerParams(vmem_limit_bytes=53 * 2**20),
         cost_estimate=pl.CostEstimate(
@@ -301,97 +310,154 @@
     )(core, momentum, gradient, ortho, own, other)
 
 
-def late_kernel(place_ref, mom_ref, grad_ref, weight_ref, got_ref, ortho_ref, own_ref, other_ref,
-                begun_ref, new_mom_ref, new_weight_ref, basis_ref,
-                mom, grad, weight, own, other, new_mom, new_weight, hi, lo,
-                load_sems, store_sems, *, early, scale, total_cols):
+def late_kernel(chip_ref, weight_ref, got_ref, ortho_ref, back_ref, hi_ref, lo_ref,
+                out_ref, basis_ref,
+                weight, back, hi, lo, out, load_sems, store_sems, back_sem, *, scale, total_cols):
     tiles, rows, width = weight.shape
-    chunks, count, _ = own.shape
-    per = chunks // tiles
     loads, stores = [], []
-    order = list(range(early, tiles)) + list(range(early))
-    for t in order:
-        cols, part = pl.ds(t * width, width), pl.ds(t * per, per)
-        pairs = [
-            (own_ref.at[part], own.at[part]), (other_ref.at[part], other.at[part]),
-            (weight_ref.at[:, cols], weight.at[t]),
-        ]
-        results = [(new_weight.at[t], new_weight_ref.at[:, cols])]
-        if t >= early:
-            pairs += [
-                (mom_ref.at[:, cols], mom.at[t - early]),
-                (grad_ref.at[:, cols], grad.at[t - early]),
-            ]
-            results.append((new_mom.at[t - early], new_mom_ref.at[:, cols]))
-        loads.append(copies_of(pairs, load_sems.at[t]))
-        stores.append(copies_of(results, store_sems.at[t]))
-        for load in loads[-1]:
+    for t in range(tiles):
+        cols = pl.ds(t * width, width)
+        loads.append(copies_of(
+            [
+                (hi_ref.at[cols], hi.at[cols]), (lo_ref.at[cols], lo.at[cols]),
+                (weight_ref.at[:, cols], weight.at[t]),
+            ],
+            load_sems.at[t],
+        ))
+        stores.append(pltpu.make_async_copy(out.at[t], out_ref.at[:, cols], store_sems.at[t]))
+        for load in loads[t]:
             load.start()
+    own = pltpu.make_async_copy(back_ref.at[chip_ref[0]], back, back_sem)
+    own.start()
     sums = got_ref[0, 0:1, :]
     for i in range(1, got_ref.shape[0]):
         sums = sums + got_ref[i, 0:1, :]
     rms = jnp.sqrt(sums / total_cols + 1e-06)
-    ortho = ortho_ref[...]
-    first = ((1.0 - keep_rate) * ortho).astype(BF16)
-    left_hi, left_lo = split(scale * ortho / rms)
-    for t, load_group, store_group in zip(order, loads, stores):
-        for load in load_group:
+    left_hi, left_lo = split(scale * ortho_ref[...] / rms)
+    for t in range(tiles):
+        for load in loads[t]:
             load.wait()
-        place(place_ref[0], count, per, own, other, hi, lo, t)
         right_hi = hi[t * width : (t + 1) * width, :]
         right_lo = lo[t * width : (t + 1) * width, :]
-        if t >= early:
-            new_mom[t - early] = (
-                mom[t - early] + grad[t - early].astype(F32) - nt(first, right_hi)
-            )
         change = nt(left_hi, right_hi) + nt(left_hi, right_lo) + nt(left_lo, right_hi)
-        new_weight[t] = (
+        out[t] = (
             (1.0 - step_size * decay_rate) * weight[t].astype(F32) - change
         ).astype(BF16)
-        for store in store_group:
-            store.start()
-    basis_ref[...] = own[place_ref[1]] / rms
-    for group in stores:
-        for store in group:
-            store.wait()
-
-
-def update_late(where, momentum, gradient, weight, got, ortho, own, other, begun, early, scale,
-                total_cols):
+        stores[t].start()
+    own.wait()
+    basis_ref[...] = back[...] / rms
+    for store in stores:
+        store.wait()
+
+
+def update_weight(chip, weight, got, ortho, back, hi, lo, scale, total_cols):
     rows, cols = weight.shape
-    chunks, count, rank = own.shape
+    chunks, count, rank = back.shape
     tile = (TILES, rows, cols // TILES)
-    rest = (max(TILES - early, 1), rows, cols // TILES)
-    return pl.pallas_call(
-        functools.partial(late_kernel, early=early, scale=scale, total_cols=total_cols),
-        in_specs=[IN_SMEM, HBM, HBM, HBM, IN_VMEM, IN_VMEM, HBM, HBM, HBM],
-        out_specs=[HBM, HBM, IN_VMEM],
+    return pl.pallas_call(
+        functools.partial(late_kernel, scale=scale, total_cols=total_cols),
+        in_specs=[IN_SMEM, HBM, IN_VMEM, IN_VMEM, HBM, HBM, HBM],
+        out_specs=[HBM, IN_VMEM],
         out_shape=[
-            jax.ShapeDtypeStruct((rows, cols), F32), jax.ShapeDtypeStruct((rows, cols), BF16),
-            jax.ShapeDtypeStruct((count, rank), F32),
+            jax.ShapeDtypeStruct((rows, cols), BF16), jax.ShapeDtypeStruct((count, rank), F32)
         ],
         scratch_shapes=[
-            VMEM(rest, F32), VMEM(rest, BF16), VMEM(tile, BF16),
-            VMEM(own.shape, F32), VMEM(own.shape, F32), VMEM(rest, F32), VMEM(tile, BF16),
-            VMEM((cols, rank), BF16), VMEM((cols, rank), BF16),
-            pltpu.SemaphoreType.DMA((TILES, 5)), pltpu.SemaphoreType.DMA((TILES, 2)),
-        ],
-        input_output_aliases={8: 0},
+            VMEM(tile, BF16), VMEM((count, rank), F32),
+            VMEM((cols, rank), BF16), VMEM((cols, rank), BF16), VMEM(tile, BF16),
+            pltpu.SemaphoreType.DMA((TILES, 3)), pltpu.SemaphoreType.DMA((TILES,)),
+            pltpu.SemaphoreType.DMA,
+        ],
         compiler_params=pltpu.CompilerParams(vmem_limit_bytes=53 * 2**20),
         cost_estimate=pl.CostEstimate(
-            flops=8 * rows * cols * rank, bytes_accessed=rows * cols * 18, transcendentals=0
+            flops=6 * rows * cols * rank, bytes_accessed=rows * cols * 8, transcendentals=0
         ),
-    )(where, momentum, gradient, weight, got, ortho, own, other, begun)
-
-
-def project_back_kernel(keep_ref, recv_ref, proj_ref, other_ref, out_ref):
+    )(chip, weight, got, ortho, back, hi, lo)
+
+
+def copies_kernel(x_ref, out_ref, sems):
+    stores = copies_of([(x_ref, out_ref.at[i]) for i in range(out_ref.shape[0])], sems)
+    for store in stores:
+        store.start()
+    for store in stores:
+        store.wait()
+
+
+def copies_in_hbm(x, n):
+    return pl.pallas_call(
+        copies_kernel,
+        in_specs=[IN_VMEM],
+        out_specs=HBM,
+        out_shape=jax.ShapeDtypeStruct((n,) + x.shape, x.dtype),
+        scratch_shapes=[pltpu.SemaphoreType.DMA((n,))],
+        compiler_params=pltpu.CompilerParams(vmem_limit_bytes=8 * 2**20),
+        cost_estimate=pl.CostEstimate(flops=0, bytes_accessed=4 * n * x.size, transcendentals=0),
+    )(x)
+
+
+def project_kernel(left_ref, right_ref, out_ref, left, right, sems):
+    steps, _, width = left.shape
+    loads = []
+    for t in range(steps):
+        part = pl.ds(t * width, width)
+        loads.append(copies_of(
+            [(left_ref.at[:, part], left.at[t]), (right_ref.at[part], right.at[t])], sems.at[t]
+        ))
+        for load in loads[t]:
+            load.start()
+    total = jnp.zeros(out_ref.shape, F32)
+    for t in range(steps):
+        for load in loads[t]:
+            load.wait()
+        a_hi, a_lo = split(left[t])
+        b_hi, b_lo = split(right[t])
+        total = total + (nn(a_hi, b_hi) + nn(a_hi, b_lo) + nn(a_lo, b_hi))
+    out_ref[...] = total
+
+
+def project(left, right):
+    rows, depth = left.shape
+    rank = right.shape[1]
+    steps = 7
+    width = depth // steps
+    return pl.pallas_call(
+        project_kernel,
+        in_specs=[HBM, HBM],
+        out_specs=IN_VMEM,
+        out_shape=jax.ShapeDtypeStruct((rows, rank), F32),
+        scratch_shapes=[
+            VMEM((steps, rows, width), F32), VMEM((steps, width, rank), F32),
+            pltpu.SemaphoreType.DMA((steps, 2)),
+        ],
+        compiler_params=pltpu.CompilerParams(vmem_limit_bytes=53 * 2**20),
+        cost_estimate=pl.CostEstimate(
+            flops=6 * rows * depth * rank, bytes_accessed=8 * rows * depth, transcendentals=0
+        ),
+    )(left, right)
+
+
+def project_back_kernel(keep_ref, recv_ref, proj_ref, other_ref, out_ref,
+                        pair, out, load_sems, store_sems):
     chips, packed, rank = out_ref.shape
+    tiles, rows, width = pair.shape
     share = rank // chips
     count = packed - share
+    per = chips // tiles
+    half = rows // 2
+    loads, stores = [], []
+    for t in range(tiles):
+        cols, part = pl.ds(t * width, width), pl.ds(t * per, per)
+        loads.append(copies_of(
+            [
+                (keep_ref.at[:, cols], pair.at[t, pl.ds(0, half)]),
+                (recv_ref.at[:, cols], pair.at[t, pl.ds(half, half)]),
+            ],
+            load_sems.at[t],
+        ))
+        stores.append(pltpu.make_async_copy(out.at[part], out_ref.at[part], store_sems.at[t]))
+        for load in loads[t]:
+            load.start()
     proj = jnp.concatenate([proj_ref[...], other_ref[...]], axis=0)
     left_hi, left_lo = split(proj.T)
-    per = 8
-    width = per * count
 
     def product(right):
         hi, lo = split(right)
@@ -399,23 +465,33 @@
 
     gram = product(proj)
     for i in range(chips):
-        out_ref[i, count:, :] = gram[i * share : (i + 1) * share, :]
-    for t in range(chips // per):
-        cols = slice(t * width, (t + 1) * width)
-        raw = product(jnp.concatenate([keep_ref[:, cols], recv_ref[:, cols]], axis=0)).T
+        out[i, count:, :] = gram[i * share : (i + 1) * share, :]
+    for t in range(tiles):
+        for load in loads[t]:
+            load.wait()
+        raw = product(pair[t]).T
         for i in range(per):
-            out_ref[t * per + i, :count, :] = raw[i * count : (i + 1) * count, :]
+            out[t * per + i, :count, :] = raw[i * count : (i + 1) * count, :]
+        stores[t].start()
+    for store in stores:
+        store.wait()
 
 
 def project_back(keep, recv, proj, other, chips):
     rows, cols = keep.shape
     rank = proj.shape[1]
+    tiles = 2
+    shape = (chips, cols // chips + rank // chips, rank)
     return pl.pallas_call(
         project_back_kernel,
-        in_specs=[IN_VMEM] * 4,
-        out_specs=IN_VMEM,
-        out_shape=jax.ShapeDtypeStruct((chips, cols // chips + rank // chips, rank), F32),
-        compiler_params=pltpu.CompilerParams(vmem_limit_bytes=24 * 2**20),
+        in_specs=[HBM, HBM, IN_VMEM, IN_VMEM],
+        out_specs=HBM,
+        out_shape=jax.ShapeDtypeStruct(shape, F32),
+        scratch_shapes=[
+            VMEM((tiles, 2 * rows, cols // tiles), F32), VMEM(shape, F32),
+            pltpu.SemaphoreType.DMA((tiles, 2)), pltpu.SemaphoreType.DMA((tiles,)),
+        ],
+        compiler_params=pltpu.CompilerParams(vmem_limit_bytes=53 * 2**20),
         cost_estimate=pl.CostEstimate(
             flops=12 * rows * cols * rank, bytes_accessed=rows * cols * 8, transcendentals=0
         ),
@@ -445,11 +521,10 @@
     keep, send = sort_columns(core, momentum, gradient, count)
     pieces = 4
     recv = jnp.concatenate([across_cores(piece) for piece in jnp.split(send, pieces, axis=0)])
-    right = gather(basis, plane, chips).reshape(chips * count, rank)
-
-    mine = jnp.dot(keep, right, precision=HIGH)
-    theirs = jnp.dot(recv, right, precision=HIGH)
-    partial = mine + across_cores(theirs)
+    right = lax.all_to_all(copies_in_hbm(basis, chips), plane, 0, 0).reshape(chips * count, rank)
+
+    theirs = across_cores(project(recv, right))
+    partial = project(keep, right) + theirs
     share = rows // depth
     piece = jnp.sum(lax.all_to_all(partial.reshape(depth, share, rank), "z", 0, 0), axis=0)
     proj = gather(piece, "z", depth).reshape(rows, rank)
@@ -461,15 +536,12 @@
     back, ortho, sums = factor(everything, proj, cores * depth)
     back_other = across_cores(back)
     sums = lax.all_to_all(sums, ("c", "z"), 0, 0)
-    early = TILES
-    begun = update_early(core, momentum, gradient, ortho, back, back_other, early)
-    sums, begun = lax.optimization_barrier((sums, begun))
+    new_momentum, hi, lo = update_momentum(core, momentum, gradient, ortho, back, back_other)
+    sums, hi, lo = lax.optimization_barrier((sums, hi, lo))
     chip = (lax.axis_index("x") * lax.axis_size("y") + lax.axis_index("y")).astype(jnp.int32)
-    where = jnp.concatenate([core, chip.reshape(1)])
     scale = step_size * math.sqrt(total_cols / total_rows)
-    new_momentum, new_weight, new_basis = update_late(
-        where, momentum, gradient, weight, sums, ortho, back, back_other, begun, early, scale,
-        total_cols,
+    new_weight, new_basis = update_weight(
+        chip.reshape(1), weight, sums, ortho, back, hi, lo, scale, total_cols
     )
     return new_momentum, new_weight, new_basis
 

time: 176 us -> 180 us (1.023)
  Pallas kernels: 29.1 us -> 39.9 us
  matrix products: 5.03 us -> 0 us
  waiting for transfers between devices: 18.6 us -> 14.4 us
    pallas_call x3 -> x6, Pallas kernels: 14.3 us -> 25 us  [the longest x1 6.54 us: update_momentum(): pl.pallas_call(early_kernel, in_specs=[IN_SMEM, HBM, HBM, IN_VMEM, HBM, H...]
    dot_general x2 -> x0, matrix products: 5.03 us -> none  [the longest x1 2.57 us: per_device(): theirs = jnp.dot(recv, right, precision=HIGH)]
    unnamed x9, local copies, waits for them, and re-layouts: 1.6 us -> 4.55 us
    broadcast_in_dim x3 -> x2, local copies, waits for them, and re-layouts: 2.53 us -> 0.21 us  [gather(): spread = jnp.broadcast_to(x[None], (n,) + x.shape)]
  transfers between devices with their start and end apart: 9 -> 9, of which waited for: 6 -> 5; matrix products, arithmetic and copies ran while one was open for 2% -> 3% of each run, Pallas kernels for 6% -> 8%
where the time goes in v5:
time: 180 us
  blocking collectives  95.7 us (53%)
  Pallas kernels  39.9 us (22%)
  starting transfers between devices  21.3 us (12%)
  waiting for transfers between devices  14.4 us (8%)
  local copies, waits for them, and re-layouts  7.16 us (4%)
    all_to_all x2, blocking collectives, gather(): return lax.all_to_all(spread, axes, 0, 0)  44.4 us
    all_to_all x1, blocking collectives, per_device(): summed = jnp.sum(lax.all_to_all(packed, plane, 0, 0), axis=0)  31 us
    all_to_all x1, blocking collectives, per_device(): lax.all_to_all(partial.reshape(depth, share, rank), 'z', 0, 0)  20.3 us
    all_to_all x1, waiting for transfers between devices, per_device(): lax.all_to_all(copies_in_hbm(basis, chips), plane, 0, 0)  11.7 us
    pallas_call x1, Pallas kernels, factor(): pl.pallas_call(factor_kernel, out_shape=[jax.ShapeDtypeStruct((chips, pac...  10.5 us
    ppermute x7, starting transfers between devices, across_cores(): return lax.ppermute(x, 'c', [(0, 1), (1, 0)])  10.1 us
    all_to_all x1, starting transfers between devices, per_device(): lax.all_to_all(copies_in_hbm(basis, chips), plane, 0, 0)  7.6 us
    pallas_call x1, Pallas kernels, update_momentum(): pl.pallas_call(early_kernel, in_specs=[IN_SMEM, HBM, HBM, IN_VMEM, HBM, H...  6.54 us
  transfers between devices with their start and end apart: 9, of which 5 were waited for; matrix products, arithmetic and copies ran while one was open for 3% of the time, Pallas kernels for 8%

profile of v5, /device:TPU:1, one launch (start us, length us, event | category | flops | bytes accessed | tf_op | source)
XLA Modules:
  0.0 179.6 jit_solution(15082948753758681688)
XLA Ops:
  0.6 0.0 copy-start.1
  0.6 0.9 copy-done.1
  1.5 1.4 shard_map.68
  2.9 7.6 %all-to-all-start = ((f32[16,112,256]{2,1,0:T(8,128)}), f32[16,112,256]{2,1,0:T(8,128)S(1)}, u32[]{:S(2)}, u32[]{:S(2)}) async-start(f32[16,112,256]{2,1,0:T(8,128)} %shard_map.68), calls=%async_computation | async-start | bytes 3670016 | tf_op jit(solution)/shard_map/all_to_all | solution.py:524
  10.6 4.4 %shard_map.67 = (f32[256,1792]{1,0:T(8,128)}, f32[256,1792]{1,0:T(8,128)}) custom-call(s32[1]{0:T(128)} %bitcast.refs_0_.core_ref, f32[256,3584]{1,0:T(8,128)} %mom_ref.1, bf16[256,3584]{1,0:T(8,128)(2,1)} %grad_ref.1), custom_call_target="tpu_custom_call" | custom-call | flops 917504 | bytes 9175040 | tf_op jit(solution)/shard_map/pallas_call | solution.py:94
  15.0 1.6 fusion
  16.6 1.1 collective-permute-start
  17.7 0.1 collective-permute-start.1
  17.8 0.4 collective-permute-start.3
  18.2 0.1 collective-permute-start.2
  18.3 0.8 collective-permute-done
  19.1 0.8 constant_dynamic-update-slice_fusion.3
  19.9 0.0 collective-permute-done.1
  19.9 0.8 constant_dynamic-update-slice_fusion.2
  20.7 0.4 collective-permute-done.2
  21.1 0.8 constant_dynamic-update-slice_fusion.1
  21.9 0.0 collective-permute-done.3
  21.9 0.8 constant_dynamic-update-slice_fusion.left_ref.recv_ref
  22.7 11.7 %all-to-all-done = f32[16,112,256]{2,1,0:T(8,128)S(1)} async-done(((f32[16,112,256]{2,1,0:T(8,128)}), f32[16,112,256]{2,1,0:T(8,128)S(1)}, u32[]{:S(2)}, u32[]{:S(2)}) %all-to-all-start) | async-done | bytes 1835040 | tf_op jit(solution)/shard_map/all_to_all | solution.py:524
  34.4 0.0 copy-start.2
  34.4 1.2 copy-done.2
  35.6 3.0 %shard_map.70 = f32[256,256]{1,0:T(8,128)S(1)} custom-call(f32[256,1792]{1,0:T(8,128)} %constant_dynamic-update-slice_fusion.left_ref.recv_ref, f32[1792,256]{1,0:T(8,128)} %bitcast.8), custom_call_target="tpu_custom_call" | custom-call | flops 704643072 | bytes 3670016 | tf_op jit(solution)/shard_map/pallas_call | solution.py:422
  38.6 4.2 %collective-permute-start.4 = (f32[256,256]{1,0:T(8,128)S(1)}, f32[256,256]{1,0:T(8,128)S(1)}, u32[]{:S(2)}, u32[]{:S(2)}) collective-permute-start(f32[256,256]{1,0:T(8,128)S(1)} %shard_map.70), channel_id=1, source_target_pairs={{0,8},{8,0},{1,9},{9,1},{2,10},{10,2},{3,11},{11,3},{4,12},{12,4},... | collective-permute-start | bytes 786440 | tf_op jit(solution)/shard_map/ppermute | solution.py:502
  42.9 3.0 %shard_map.69 = f32[256,256]{1,0:T(8,128)S(1)} custom-call(f32[256,1792]{1,0:T(8,128)} %get-tuple-element.16.left_ref.keep_ref, f32[1792,256]{1,0:T(8,128)} %bitcast.9), custom_call_target="tpu_custom_call" | custom-call | flops 704643072 | bytes 3670016 | tf_op jit(solution)/shard_map/pallas_call | solution.py:422
  45.9 0.0 collective-permute-done.4
  46.0 20.3 %all_to_all.30 = f32[8,32,256]{2,1,0:T(8,128)S(1)} all-to-all(f32[8,32,256]{2,1,0:T(8,128)S(1)} %bitcast.10), channel_id=1, replica_groups=mesh['x'=4,'y'=4,'c'=2,'z'=8] {'z'}, dimensions={0} | all-to-all | bytes 524288 | tf_op jit(solution)/shard_map/all_to_all | solution.py:529
  66.3 14.7 %all_to_all.31 = f32[8,32,256]{2,1,0:T(8,128)S(1)} all-to-all(f32[8,32,256]{2,1,0:T(8,128)S(1)} %broadcast_in_dim.4), channel_id=1, replica_groups=mesh['x'=4,'y'=4,'c'=2,'z'=8] {'z'}, dimensions={0} | all-to-all | bytes 524288 | tf_op jit(solution)/shard_map/all_to_all | solution.py:507
  81.0 0.6 collective-permute-start.5
  81.6 1.2 collective-permute-done.5.other_ref
  82.7 5.8 %shard_map.71 = f32[16,128,256]{2,1,0:T(8,128)} custom-call(f32[256,1792]{1,0:T(8,128)} %get-tuple-element.16.left_ref.keep_ref, f32[256,1792]{1,0:T(8,128)} %constant_dynamic-update-slice_fusion.left_ref.recv_ref, f32[256,256]{1,0:T(8,128)S(1)} %bitcast.6, f32[256,256]{1,0:T(8,128)S(1)} %collective-permute-done.5.other_ref), custom_call_target="tpu_custom_call" | custom-call | flops 1409286144 | bytes 3670016 | tf_op jit(solution)/shard_map/pallas_call | solution.py:485
  88.5 31.0 %all_to_all.32 = f32[16,128,256]{2,1,0:T(8,128)S(1)} all-to-all(f32[16,128,256]{2,1,0:T(8,128)} %shard_map.71), channel_id=1, replica_groups=mesh['x'=4,'y'=4,'c'=2,'z'=8] {'x','y'}, dimensions={0} | all-to-all | bytes 4194304 | tf_op jit(solution)/shard_map/all_to_all | solution.py:534
  119.5 0.1 reduce_sum.19
  119.7 0.2 broadcast_in_dim.5
  119.9 29.8 %all_to_all.33.got_ref = f32[16,128,256]{2,1,0:T(8,128)S(1)} all-to-all(f32[16,128,256]{2,1,0:T(8,128)S(1)} %broadcast_in_dim.5), channel_id=1, replica_groups=mesh['x'=4,'y'=4,'c'=2,'z'=8] {'x','y'}, dimensions={0} | all-to-all | bytes 4194304 | tf_op jit(solution)/shard_map/all_to_all | solution.py:507
  149.6 10.5 %shard_map.72 = (f32[16,112,256]{2,1,0:T(8,128)S(1)}, f32[256,256]{1,0:T(8,128)S(1)}, f32[16,8,256]{2,1,0:T(8,128)}) custom-call(f32[16,128,256]{2,1,0:T(8,128)S(1)} %all_to_all.33.got_ref, f32[256,256]{1,0:T(8,128)S(1)} %bitcast.7), custom_call_target="tpu_custom_call" | custom-call | flops 671088640 | bytes 1048576 | tf_op jit(solution)/shard_map/pallas_call | solution.py:226
  160.1 0.0 copy-start
  160.1 3.5 %collective-permute-start.6 = (f32[16,112,256]{2,1,0:T(8,128)S(1)}, f32[16,112,256]{2,1,0:T(8,128)}, u32[]{:S(2)}, u32[]{:S(2)}) collective-permute-start(f32[16,112,256]{2,1,0:T(8,128)S(1)} %get-tuple-element.19.own_ref.back_ref), channel_id=1, source_target_pairs={{0,8},{8,0},{1,9},{9,1},{2,10},{10,2},{3,11},{11,3},{4,12},{12,4},... | collective-permute-start | bytes 5505032 | tf_op jit(solution)/shard_map/ppermute | solution.py:502
  163.6 3.6 %all-to-all-start.5 = ((f32[16,8,256]{2,1,0:T(8,128)}), f32[16,8,256]{2,1,0:T(8,128)S(1)}, u32[]{:S(2)}, u32[]{:S(2)}) async-start(f32[16,8,256]{2,1,0:T(8,128)} %get-tuple-element.21), calls=%async_computation.5 | async-start | bytes 262144 | tf_op jit(solution)/shard_map/all_to_all | solution.py:538
  167.2 0.0 collective-permute-done.6.other_ref
  167.2 0.0 copy-done
  167.3 6.5 %shard_map.73 = (f32[256,3584]{1,0:T(8,128)}, bf16[3584,256]{1,0:T(8,128)(2,1)}, bf16[3584,256]{1,0:T(8,128)(2,1)}) custom-call(s32[1]{0:T(128)} %bitcast.refs_0_.core_ref, f32[256,3584]{1,0:T(8,128)} %mom_ref.1, bf16[256,3584]{1,0:T(8,128)(2,1)} %grad_ref.1, f32[256,256]{1,0:T(8,128)S(1)} %get-tuple-element.18.ortho_ref, f32[16,112,256]{2,1,0:T(8,128)} %copy-done, ...), custom_call_target="tpu_custom_call" | custom-call | flops 469762048 | bytes 16515072 | tf_op jit(solution)/shard_map/pallas_call | solution.py:296
  173.8 0.4 all-to-all-done.5.got_ref
  174.2 5.3 %shard_map.74 = (bf16[256,3584]{1,0:T(8,128)(2,1)}, f32[112,256]{1,0:T(8,128)}) custom-call(s32[1]{0:T(128)} %bitcast.4.chip_ref, bf16[256,3584]{1,0:T(8,128)(2,1)} %weight_ref.1, f32[16,8,256]{2,1,0:T(8,128)S(1)} %all-to-all-done.5.got_ref, f32[256,256]{1,0:T(8,128)S(1)} %get-tuple-element.18.ortho_ref, f32[16,112,256]{2,1,0:T(8,128)} %copy-done, ...), custom_call_target="tpu_custom_call" | custom-call | flops 1409286144 | bytes 7340032 | tf_op jit(solution)/shard_map/pallas_call | solution.py:357
  (3 shorter events, 0.1 us)
Async XLA Ops:
  0.6 0.9 copy-start.1
  2.9 31.4 %all-to-all-start = ((f32[16,112,256]{2,1,0:T(8,128)}), f32[16,112,256]{2,1,0:T(8,128)S(1)}, u32[]{:S(2)}, u32[]{:S(2)}) async-start(f32[16,112,256]{2,1,0:T(8,128)} %shard_map.68), calls=%async_computation | async-start | bytes 3670016 | tf_op jit(solution)/shard_map/all_to_all | solution.py:524
  16.6 2.6 %collective-permute-start = (f32[64,1792]{1,0:T(8,128)S(1)}, f32[64,1792]{1,0:T(8,128)S(1)}, u32[]{:S(2)}, u32[]{:S(2)}) collective-permute-start(f32[64,1792]{1,0:T(8,128)S(1)} %get-tuple-element.32), channel_id=1, source_target_pairs={{0,8},{8,0},{1,9},{9,1},{2,10},{10,2},{3,11},{11,3},{4,12},{12,4},... | collective-permute-start | bytes 1376264 | tf_op jit(solution)/shard_map/ppermute | solution.py:502
  17.7 2.3 %collective-permute-start.1 = (f32[64,1792]{1,0:T(8,128)S(1)}, f32[64,1792]{1,0:T(8,128)S(1)}, u32[]{:S(2)}, u32[]{:S(2)}) collective-permute-start(f32[64,1792]{1,0:T(8,128)S(1)} %get-tuple-element.31), channel_id=1, source_target_pairs={{0,8},{8,0},{1,9},{9,1},{2,10},{10,2},{3,11},{11,3},{4,12},{12,4},... | collective-permute-start | bytes 1376264 | tf_op jit(solution)/shard_map/ppermute | solution.py:502
  17.8 4.1 %collective-permute-start.3 = (f32[64,1792]{1,0:T(8,128)S(1)}, f32[64,1792]{1,0:T(8,128)S(1)}, u32[]{:S(2)}, u32[]{:S(2)}) collective-permute-start(f32[64,1792]{1,0:T(8,128)S(1)} %get-tuple-element.29), channel_id=1, source_target_pairs={{0,8},{8,0},{1,9},{9,1},{2,10},{10,2},{3,11},{11,3},{4,12},{12,4},... | collective-permute-start | bytes 1376264 | tf_op jit(solution)/shard_map/ppermute | solution.py:502
  18.2 2.9 %collective-permute-start.2 = (f32[64,1792]{1,0:T(8,128)S(1)}, f32[64,1792]{1,0:T(8,128)S(1)}, u32[]{:S(2)}, u32[]{:S(2)}) collective-permute-start(f32[64,1792]{1,0:T(8,128)S(1)} %get-tuple-element.30), channel_id=1, source_target_pairs={{0,8},{8,0},{1,9},{9,1},{2,10},{10,2},{3,11},{11,3},{4,12},{12,4},... | collective-permute-start | bytes 1376264 | tf_op jit(solution)/shard_map/ppermute | solution.py:502
  34.4 1.2 copy-start.2
  38.6 7.3 %collective-permute-start.4 = (f32[256,256]{1,0:T(8,128)S(1)}, f32[256,256]{1,0:T(8,128)S(1)}, u32[]{:S(2)}, u32[]{:S(2)}) collective-permute-start(f32[256,256]{1,0:T(8,128)S(1)} %shard_map.70), channel_id=1, source_target_pairs={{0,8},{8,0},{1,9},{9,1},{2,10},{10,2},{3,11},{11,3},{4,12},{12,4},... | collective-permute-start | bytes 786440 | tf_op jit(solution)/shard_map/ppermute | solution.py:502
  81.0 1.7 collective-permute-start.5
  160.1 7.2 %copy-start = (f32[16,112,256]{2,1,0:T(8,128)}, f32[16,112,256]{2,1,0:T(8,128)S(1)}, u32[]{:S(2)}) copy-start(f32[16,112,256]{2,1,0:T(8,128)S(1)} %get-tuple-element.19.own_ref.back_ref) | copy-start | bytes 5505028
  160.1 7.1 %collective-permute-start.6 = (f32[16,112,256]{2,1,0:T(8,128)S(1)}, f32[16,112,256]{2,1,0:T(8,128)}, u32[]{:S(2)}, u32[]{:S(2)}) collective-permute-start(f32[16,112,256]{2,1,0:T(8,128)S(1)} %get-tuple-element.19.own_ref.back_ref), channel_id=1, source_target_pairs={{0,8},{8,0},{1,9},{9,1},{2,10},{10,2},{3,11},{11,3},{4,12},{12,4},... | collective-permute-start | bytes 5505032 | tf_op jit(solution)/shard_map/ppermute | solution.py:502
  163.6 10.6 %all-to-all-start.5 = ((f32[16,8,256]{2,1,0:T(8,128)}), f32[16,8,256]{2,1,0:T(8,128)S(1)}, u32[]{:S(2)}, u32[]{:S(2)}) async-start(f32[16,8,256]{2,1,0:T(8,128)} %get-tuple-element.21), calls=%async_computation.5 | async-start | bytes 262144 | tf_op jit(solution)/shard_map/all_to_all | solution.py:538

commit v6 on v5

--- a/solution.py
+++ b/solution.py
@@ -41,19 +41,16 @@
     return [pltpu.make_async_copy(src, dst, sems.at[i]) for i, (src, dst) in enumerate(pairs)]
 
 
-def sort_columns_kernel(core_ref, mom_ref, grad_ref, keep_ref, send_ref,
-                        mom, grad, keep, send, load_sems, store_sems, *, count):
+def sort_columns_kernel(core_ref, mom_ref, grad_ref, keep_ref, *rest, count):
+    send_refs, (mom, grad, load_sems) = rest[:-3], rest[-3:]
     steps, tile, cols = mom.shape
-    loads, stores = [], []
+    per = steps // len(send_refs)
+    loads = []
     for t in range(steps):
         rows = pl.ds(t * tile, tile)
         loads.append(copies_of(
             [(mom_ref.at[rows, :], mom.at[t]), (grad_ref.at[rows, :], grad.at[t])],
             load_sems.at[t],
-        ))
-        stores.append(copies_of(
-            [(send.at[t], send_ref.at[rows, :]), (keep.at[t], keep_ref.at[rows, :])],
-            store_sems.at[t],
         ))
         for load in loads[t]:
             load.start()
@@ -68,40 +65,36 @@
             )
             for first in range(2)
         ]
+        send_ref = send_refs[t // per]
+        there = slice(t % per * tile, (t % per + 1) * tile)
+        here = slice(t * tile, (t + 1) * tile)
 
         @pl.when(core_ref[0] == 0)
         def _():
-            keep[t] = parts[0]
-            send[t] = parts[1]
+            keep_ref[here, :] = parts[0]
+            send_ref[there, :] = parts[1]
 
         @pl.when(core_ref[0] == 1)
         def _():
-            keep[t] = parts[1]
-            send[t] = parts[0]
-
-        for store in stores[t]:
-            store.start()
-    for group in stores:
-        for store in group:
-            store.wait()
-
-
-def sort_columns(core, momentum, gradient, count):
+            keep_ref[here, :] = parts[1]
+            send_ref[there, :] = parts[0]
+
+
+def sort_columns(core, momentum, gradient, count, pieces):
     rows, cols = momentum.shape
     steps = 8
     tile = rows // steps
-    out = jax.ShapeDtypeStruct((rows, cols // 2), F32)
-    return pl.pallas_call(
-        lambda *refs: sort_columns_kernel(*refs, count=count),
+    return pl.pallas_call(
+        functools.partial(sort_columns_kernel, count=count),
         in_specs=[IN_SMEM, HBM, HBM],
-        out_specs=[HBM, HBM],
-        out_shape=[out, out],
+        out_specs=[IN_VMEM] * (1 + pieces),
+        out_shape=[jax.ShapeDtypeStruct((rows, cols // 2), F32)]
+        + [jax.ShapeDtypeStruct((rows // pieces, cols // 2), F32)] * pieces,
         scratch_shapes=[
             VMEM((steps, tile, cols), F32), VMEM((steps, tile, cols), BF16),
-            VMEM((steps, tile, cols // 2), F32), VMEM((steps, tile, cols // 2), F32),
-            pltpu.SemaphoreType.DMA((steps, 2)), pltpu.SemaphoreType.DMA((steps, 2)),
+            pltpu.SemaphoreType.DMA((steps, 2)),
         ],
-        compiler_params=pltpu.CompilerParams(vmem_limit_bytes=53 * 2**20),
+        compiler_params=pltpu.CompilerParams(vmem_limit_bytes=16 * 2**20),
         cost_estimate=pl.CostEstimate(
             flops=rows * cols, bytes_accessed=rows * cols * 10, transcendentals=0
         ),
@@ -374,90 +367,39 @@
     )(chip, weight, got, ortho, back, hi, lo)
 
 
-def copies_kernel(x_ref, out_ref, sems):
-    stores = copies_of([(x_ref, out_ref.at[i]) for i in range(out_ref.shape[0])], sems)
-    for store in stores:
-        store.start()
-    for store in stores:
-        store.wait()
-
-
-def copies_in_hbm(x, n):
-    return pl.pallas_call(
-        copies_kernel,
-        in_specs=[IN_VMEM],
-        out_specs=HBM,
-        out_shape=jax.ShapeDtypeStruct((n,) + x.shape, x.dtype),
-        scratch_shapes=[pltpu.SemaphoreType.DMA((n,))],
-        compiler_params=pltpu.CompilerParams(vmem_limit_bytes=8 * 2**20),
-        cost_estimate=pl.CostEstimate(flops=0, bytes_accessed=4 * n * x.size, transcendentals=0),
-    )(x)
-
-
-def project_kernel(left_ref, right_ref, out_ref, left, right, sems):
-    steps, _, width = left.shape
-    loads = []
-    for t in range(steps):
-        part = pl.ds(t * width, width)
-        loads.append(copies_of(
-            [(left_ref.at[:, part], left.at[t]), (right_ref.at[part], right.at[t])], sems.at[t]
-        ))
-        for load in loads[t]:
-            load.start()
-    total = jnp.zeros(out_ref.shape, F32)
-    for t in range(steps):
-        for load in loads[t]:
-            load.wait()
-        a_hi, a_lo = split(left[t])
-        b_hi, b_lo = split(right[t])
-        total = total + (nn(a_hi, b_hi) + nn(a_hi, b_lo) + nn(a_lo, b_hi))
-    out_ref[...] = total
-
-
-def project(left, right):
-    rows, depth = left.shape
-    rank = right.shape[1]
-    steps = 7
-    width = depth // steps
+def project_kernel(right_ref, *refs):
+    left_refs, out_ref = refs[:-1], refs[-1]
+    b_hi, b_lo = split(right_ref[...])
+    rows = left_refs[0].shape[0]
+    for i, left_ref in enumerate(left_refs):
+        a_hi, a_lo = split(left_ref[...])
+        out_ref[i * rows : (i + 1) * rows, :] = nn(a_hi, b_hi) + nn(a_hi, b_lo) + nn(a_lo, b_hi)
+
+
+def project(lefts, right):
+    depth, rank = right.shape
+    rows = sum(left.shape[0] for left in lefts)
     return pl.pallas_call(
         project_kernel,
-        in_specs=[HBM, HBM],
+        in_specs=[IN_VMEM] * (1 + len(lefts)),
         out_specs=IN_VMEM,
         out_shape=jax.ShapeDtypeStruct((rows, rank), F32),
-        scratch_shapes=[
-            VMEM((steps, rows, width), F32), VMEM((steps, width, rank), F32),
-            pltpu.SemaphoreType.DMA((steps, 2)),
-        ],
-        compiler_params=pltpu.CompilerParams(vmem_limit_bytes=53 * 2**20),
+        compiler_params=pltpu.CompilerParams(vmem_limit_bytes=14 * 2**20),
         cost_estimate=pl.CostEstimate(
             flops=6 * rows * depth * rank, bytes_accessed=8 * rows * depth, transcendentals=0
         ),
-    )(left, right)
-
-
-def project_back_kernel(keep_ref, recv_ref, proj_ref, other_ref, out_ref,
-                        pair, out, load_sems, store_sems):
+    )(right, *lefts)
+
+
+def project_back_kernel(proj_ref, other_ref, *refs):
+    left_refs, out_ref = refs[:-1], refs[-1]
     chips, packed, rank = out_ref.shape
-    tiles, rows, width = pair.shape
     share = rank // chips
     count = packed - share
-    per = chips // tiles
-    half = rows // 2
-    loads, stores = [], []
-    for t in range(tiles):
-        cols, part = pl.ds(t * width, width), pl.ds(t * per, per)
-        loads.append(copies_of(
-            [
-                (keep_ref.at[:, cols], pair.at[t, pl.ds(0, half)]),
-                (recv_ref.at[:, cols], pair.at[t, pl.ds(half, half)]),
-            ],
-            load_sems.at[t],
-        ))
-        stores.append(pltpu.make_async_copy(out.at[part], out_ref.at[part], store_sems.at[t]))
-        for load in loads[t]:
-            load.start()
     proj = jnp.concatenate([proj_ref[...], other_ref[...]], axis=0)
     left_hi, left_lo = split(proj.T)
+    per = 8
+    width = per * count
 
     def product(right):
         hi, lo = split(right)
@@ -465,37 +407,27 @@
 
     gram = product(proj)
     for i in range(chips):
-        out[i, count:, :] = gram[i * share : (i + 1) * share, :]
-    for t in range(tiles):
-        for load in loads[t]:
-            load.wait()
-        raw = product(pair[t]).T
+        out_ref[i, count:, :] = gram[i * share : (i + 1) * share, :]
+    for t in range(chips // per):
+        cols = slice(t * width, (t + 1) * width)
+        raw = product(jnp.concatenate([ref[:, cols] for ref in left_refs], axis=0)).T
         for i in range(per):
-            out[t * per + i, :count, :] = raw[i * count : (i + 1) * count, :]
-        stores[t].start()
-    for store in stores:
-        store.wait()
-
-
-def project_back(keep, recv, proj, other, chips):
-    rows, cols = keep.shape
-    rank = proj.shape[1]
-    tiles = 2
-    shape = (chips, cols // chips + rank // chips, rank)
+            out_ref[t * per + i, :count, :] = raw[i * count : (i + 1) * count, :]
+
+
+def project_back(lefts, proj, other, chips):
+    cols = lefts[0].shape[1]
+    rows, rank = proj.shape
     return pl.pallas_call(
         project_back_kernel,
-        in_specs=[HBM, HBM, IN_VMEM, IN_VMEM],
-        out_specs=HBM,
-        out_shape=jax.ShapeDtypeStruct(shape, F32),
-        scratch_shapes=[
-            VMEM((tiles, 2 * rows, cols // tiles), F32), VMEM(shape, F32),
-            pltpu.SemaphoreType.DMA((tiles, 2)), pltpu.SemaphoreType.DMA((tiles,)),
-        ],
-        compiler_params=pltpu.CompilerParams(vmem_limit_bytes=53 * 2**20),
+        in_specs=[IN_VMEM] * (2 + len(lefts)),
+        out_specs=IN_VMEM,
+        out_shape=jax.ShapeDtypeStruct((chips, cols // chips + rank // chips, rank), F32),
+        compiler_params=pltpu.CompilerParams(vmem_limit_bytes=24 * 2**20),
         cost_estimate=pl.CostEstimate(
             flops=12 * rows * cols * rank, bytes_accessed=rows * cols * 8, transcendentals=0
         ),
-    )(keep, recv, proj, other)
+    )(proj, other, *lefts)
 
 
 def across_cores(x):
@@ -518,19 +450,18 @@
     total_rows = rows * chips * cores
     core = lax.axis_index("c").astype(jnp.int32).reshape(1)
 
-    keep, send = sort_columns(core, momentum, gradient, count)
-    pieces = 4
-    recv = jnp.concatenate([across_cores(piece) for piece in jnp.split(send, pieces, axis=0)])
-    right = lax.all_to_all(copies_in_hbm(basis, chips), plane, 0, 0).reshape(chips * count, rank)
+    keep, *send = sort_columns(core, momentum, gradient, count, 4)
+    recv = [across_cores(piece) for piece in send]
+    right = gather(basis, plane, chips).reshape(chips * count, rank)
 
     theirs = across_cores(project(recv, right))
-    partial = project(keep, right) + theirs
+    partial = project([keep], right) + theirs
     share = rows // depth
     piece = jnp.sum(lax.all_to_all(partial.reshape(depth, share, rank), "z", 0, 0), axis=0)
     proj = gather(piece, "z", depth).reshape(rows, rank)
     proj_other = across_cores(proj)
 
-    packed = project_back(keep, recv, proj, proj_other, chips)
+    packed = project_back([keep] + recv, proj, proj_other, chips)
     summed = jnp.sum(lax.all_to_all(packed, plane, 0, 0), axis=0)
     everything = gather(summed, plane, chips)
     back, ortho, sums = factor(everything, proj, cores * depth)

time: 180 us -> 173 us (0.961)
  Pallas kernels: 39.9 us -> 34.2 us
  local copies, waits for them, and re-layouts: 7.16 us -> 10.1 us
  blocking collectives: 95.7 us -> 93.2 us
  waiting for transfers between devices: 14.4 us -> 12.2 us
    pallas_call x5 -> x4, Pallas kernels: 17.6 us -> 11.9 us  [the longest x1 6.82 us: sort_columns(): pl.pallas_call(functools.partial(sort_columns_kernel, count=count), in_sp...]
    all_to_all x1, waiting for transfers between devices: 11.7 us -> 7.18 us  [gather(): return lax.all_to_all(spread, axes, 0, 0)]
    unnamed x9 -> x18, local copies, waits for them, and re-layouts: 4.55 us -> 7.58 us
    broadcast_in_dim x2 -> x3, local copies, waits for them, and re-layouts: 0.21 us -> 2.52 us  [gather(): spread = jnp.broadcast_to(x[None], (n,) + x.shape)]
    ppermute x7, waiting for transfers between devices: 2.36 us -> 4.43 us  [across_cores(): return lax.ppermute(x, 'c', [(0, 1), (1, 0)])]
    all_to_all x2, blocking collectives: 44.4 us -> 42.6 us  [gather(): return lax.all_to_all(spread, axes, 0, 0)]
  transfers between devices with their start and end apart: 9 -> 9, of which waited for: 5 -> 9; matrix products, arithmetic and copies ran while one was open for 3% -> 0% of each run, Pallas kernels for 8% -> 8%
where the time goes in v6:
time: 173 us
  blocking collectives  93.2 us (54%)
  Pallas kernels  34.2 us (20%)
  starting transfers between devices  22.1 us (13%)
  waiting for transfers between devices  12.2 us (7%)
  local copies, waits for them, and re-layouts  10.1 us (6%)
    all_to_all x2, blocking collectives, gather(): return lax.all_to_all(spread, axes, 0, 0)  42.6 us
    all_to_all x1, blocking collectives, per_device(): summed = jnp.sum(lax.all_to_all(packed, plane, 0, 0), axis=0)  30.5 us
    all_to_all x1, blocking collectives, per_device(): lax.all_to_all(partial.reshape(depth, share, rank), 'z', 0, 0)  20.1 us
    ppermute x7, starting transfers between devices, across_cores(): return lax.ppermute(x, 'c', [(0, 1), (1, 0)])  11.2 us
    pallas_call x1, Pallas kernels, factor(): pl.pallas_call(factor_kernel, out_shape=[jax.ShapeDtypeStruct((chips, pac...  10.5 us
    all_to_all x1, starting transfers between devices, gather(): return lax.all_to_all(spread, axes, 0, 0)  7.58 us
    unnamed x18, local copies, waits for them, and re-layouts  7.58 us
    all_to_all x1, waiting for transfers between devices, gather(): return lax.all_to_all(spread, axes, 0, 0)  7.18 us
  transfers between devices with their start and end apart: 9, of which 9 were waited for; matrix products, arithmetic and copies ran while one was open for 0% of the time, Pallas kernels for 8%

profile of v6, /device:TPU:1, one launch (start us, length us, event | category | flops | bytes accessed | tf_op | source)
XLA Modules:
  0.0 172.9 jit_solution(12730277501785264794)
XLA Ops:
  0.6 2.3 %broadcast_in_dim.6 = f32[16,112,256]{2,1,0:T(8,128)} broadcast(f32[112,256]{1,0:T(8,128)} %param.7), dimensions={1,2} | broadcast | bytes 1949696 | tf_op jit(solution)/shard_map/broadcast_in_dim | solution.py:438
  2.9 7.6 %all-to-all-start = ((f32[16,112,256]{2,1,0:T(8,128)}), f32[16,112,256]{2,1,0:T(8,128)S(1)}, u32[]{:S(2)}, u32[]{:S(2)}) async-start(f32[16,112,256]{2,1,0:T(8,128)} %broadcast_in_dim.6), calls=%async_computation | async-start | bytes 3670016 | tf_op jit(solution)/shard_map/all_to_all | solution.py:439
  10.5 0.0 copy-start
  10.5 2.0 %copy-done = f32[256,3584]{1,0:T(8,128)S(1)} copy-done((f32[256,3584]{1,0:T(8,128)S(1)}, f32[256,3584]{1,0:T(8,128)}, u32[]{:S(2)}) %copy-start) | copy-done | bytes 3670040
  12.6 0.0 copy-start.1
  12.6 1.5 copy-done.1
  14.1 6.8 %shard_map.67 = (f32[256,1792]{1,0:T(8,128)S(1)}, f32[64,1792]{1,0:T(8,128)S(1)}, f32[64,1792]{1,0:T(8,128)S(1)}, f32[64,1792]{1,0:T(8,128)S(1)}, f32[64,1792]{1,0:T(8,128)S(1)}) custom-call(s32[1]{0:T(128)} %bitcast.core_ref, f32[256,3584]{1,0:T(8,128)S(1)} %copy-done, bf16[256,3584]{1,0:T(8,128)(2,1)S(1)} %copy-done.1), custom_call_target="tpu_custom_call" | custom-call | flops 917504 | bytes 9175040 | tf_op jit(solution)/shard_map/pallas_call | solution.py:87
  20.9 0.0 copy-start.2
  20.9 1.2 copy-done.2
  22.1 0.9 collective-permute-start
  23.0 0.0 collective-permute-start.1
  23.0 0.5 collective-permute-start.2
  23.5 0.0 collective-permute-start.3
  23.5 0.9 collective-permute-done.refs_0_.refs_1_
  24.5 0.7 collective-permute-done.1.refs_1_.refs_2_
  25.1 0.7 collective-permute-done.2.refs_2_.refs_3_
  25.8 0.7 collective-permute-done.3.refs_3_.refs_4_
  26.4 0.0 copy-start.6
  26.4 0.8 copy-done.6
  27.2 7.2 %all-to-all-done = f32[16,112,256]{2,1,0:T(8,128)S(1)} async-done(((f32[16,112,256]{2,1,0:T(8,128)}), f32[16,112,256]{2,1,0:T(8,128)S(1)}, u32[]{:S(2)}, u32[]{:S(2)}) %all-to-all-start) | async-done | bytes 1835040 | tf_op jit(solution)/shard_map/all_to_all | solution.py:439
  34.4 0.0 copy-start.7
  34.4 1.0 copy-done.7
  35.4 0.0 copy-start.3
  35.4 2.0 %shard_map.69 = f32[256,256]{1,0:T(8,128)S(1)} custom-call(f32[1792,256]{1,0:T(8,128)S(1)} %bitcast.5, f32[64,1792]{1,0:T(8,128)S(1)} %collective-permute-done.refs_0_.refs_1_, f32[64,1792]{1,0:T(8,128)S(1)} %collective-permute-done.1.refs_1_.refs_2_, f32[64,1792]{1,0:T(8,128)S(1)} %collective-permute-done.2.refs_2_.refs_3_, f32[64,1792]{1,0:T(8,128)S(1)} %copy-done.7), custom_call_target="tpu_custom_call" | custom-call | flops 704643072 | bytes 3670016 | tf_op jit(solution)/shard_map/pallas_call | solution.py:382
  37.4 4.2 %collective-permute-start.4 = (f32[256,256]{1,0:T(8,128)S(1)}, f32[256,256]{1,0:T(8,128)S(1)}, u32[]{:S(2)}, u32[]{:S(2)}) collective-permute-start(f32[256,256]{1,0:T(8,128)S(1)} %shard_map.69), channel_id=1, source_target_pairs={{0,8},{8,0},{1,9},{9,1},{2,10},{10,2},{3,11},{11,3},{4,12},{12,4},... | collective-permute-start | bytes 786440 | tf_op jit(solution)/shard_map/ppermute | solution.py:434
  41.6 0.0 copy-done.3
  41.6 0.9 shard_map.68
  42.5 0.0 copy-start.4
  42.6 0.3 collective-permute-done.4
  42.8 20.1 %all_to_all.30 = f32[8,32,256]{2,1,0:T(8,128)S(1)} all-to-all(f32[8,32,256]{2,1,0:T(8,128)S(1)} %bitcast.10), channel_id=1, replica_groups=mesh['x'=4,'y'=4,'c'=2,'z'=8] {'z'}, dimensions={0} | all-to-all | bytes 524288 | tf_op jit(solution)/shard_map/all_to_all | solution.py:460
  63.0 13.0 %all_to_all.31 = f32[8,32,256]{2,1,0:T(8,128)S(1)} all-to-all(f32[8,32,256]{2,1,0:T(8,128)S(1)} %broadcast_in_dim.7), channel_id=1, replica_groups=mesh['x'=4,'y'=4,'c'=2,'z'=8] {'z'}, dimensions={0} | all-to-all | bytes 524288 | tf_op jit(solution)/shard_map/all_to_all | solution.py:439
  75.9 2.3 %collective-permute-start.5 = (f32[256,256]{1,0:T(8,128)S(1)}, f32[256,256]{1,0:T(8,128)S(1)}, u32[]{:S(2)}, u32[]{:S(2)}) collective-permute-start(f32[256,256]{1,0:T(8,128)S(1)} %bitcast.7), channel_id=1, source_target_pairs={{0,8},{8,0},{1,9},{9,1},{2,10},{10,2},{3,11},{11,3},{4,12},{12,4},... | collective-permute-start | bytes 786440 | tf_op jit(solution)/shard_map/ppermute | solution.py:434
  78.2 1.2 collective-permute-done.5.other_ref
  79.4 0.0 copy-done.4
  79.4 0.0 copy-start.8
  79.4 1.0 copy-done.8
  80.4 2.2 %shard_map.70 = f32[16,128,256]{2,1,0:T(8,128)S(1)} custom-call(f32[256,256]{1,0:T(8,128)S(1)} %bitcast.8, f32[256,256]{1,0:T(8,128)S(1)} %collective-permute-done.5.other_ref, f32[256,1792]{1,0:T(8,128)S(1)} %copy-done.4, f32[64,1792]{1,0:T(8,128)S(1)} %collective-permute-done.refs_0_.refs_1_, f32[64,1792]{1,0:T(8,128)S(1)} %collective-permute-done.1.refs_1_.refs_2_, ...), custom_call_target="tpu_custom_call" | custom-call | flops 1409286144 | bytes 3670016 | tf_op jit(solution)/shard_map/pallas_call | solution.py:421
  82.6 30.5 %all_to_all.32 = f32[16,128,256]{2,1,0:T(8,128)S(1)} all-to-all(f32[16,128,256]{2,1,0:T(8,128)S(1)} %shard_map.70), channel_id=1, replica_groups=mesh['x'=4,'y'=4,'c'=2,'z'=8] {'x','y'}, dimensions={0} | all-to-all | bytes 4194304 | tf_op jit(solution)/shard_map/all_to_all | solution.py:465
  113.1 0.1 reduce_sum.19
  113.2 0.2 broadcast_in_dim.8
  113.4 29.6 %all_to_all.33.got_ref = f32[16,128,256]{2,1,0:T(8,128)S(1)} all-to-all(f32[16,128,256]{2,1,0:T(8,128)S(1)} %broadcast_in_dim.8), channel_id=1, replica_groups=mesh['x'=4,'y'=4,'c'=2,'z'=8] {'x','y'}, dimensions={0} | all-to-all | bytes 4194304 | tf_op jit(solution)/shard_map/all_to_all | solution.py:439
  143.0 10.5 %shard_map.71 = (f32[16,112,256]{2,1,0:T(8,128)S(1)}, f32[256,256]{1,0:T(8,128)S(1)}, f32[16,8,256]{2,1,0:T(8,128)}) custom-call(f32[16,128,256]{2,1,0:T(8,128)S(1)} %all_to_all.33.got_ref, f32[256,256]{1,0:T(8,128)S(1)} %bitcast.9), custom_call_target="tpu_custom_call" | custom-call | flops 671088640 | bytes 1048576 | tf_op jit(solution)/shard_map/pallas_call | solution.py:219
  153.5 0.0 copy-start.5
  153.5 3.3 %collective-permute-start.6 = (f32[16,112,256]{2,1,0:T(8,128)S(1)}, f32[16,112,256]{2,1,0:T(8,128)}, u32[]{:S(2)}, u32[]{:S(2)}) collective-permute-start(f32[16,112,256]{2,1,0:T(8,128)S(1)} %get-tuple-element.25.own_ref.back_ref), channel_id=1, source_target_pairs={{0,8},{8,0},{1,9},{9,1},{2,10},{10,2},{3,11},{11,3},{4,12},{12,4},... | collective-permute-start | bytes 5505032 | tf_op jit(solution)/shard_map/ppermute | solution.py:434
  156.7 3.4 %all-to-all-start.5 = ((f32[16,8,256]{2,1,0:T(8,128)}), f32[16,8,256]{2,1,0:T(8,128)S(1)}, u32[]{:S(2)}, u32[]{:S(2)}) async-start(f32[16,8,256]{2,1,0:T(8,128)} %get-tuple-element.27), calls=%async_computation.5 | async-start | bytes 262144 | tf_op jit(solution)/shard_map/all_to_all | solution.py:469
  160.2 0.1 collective-permute-done.6.other_ref
  160.3 0.0 copy-done.5
  160.3 6.5 %shard_map.72 = (f32[256,3584]{1,0:T(8,128)}, bf16[3584,256]{1,0:T(8,128)(2,1)}, bf16[3584,256]{1,0:T(8,128)(2,1)}) custom-call(s32[1]{0:T(128)} %bitcast.core_ref, f32[256,3584]{1,0:T(8,128)} %mom_ref.3, bf16[256,3584]{1,0:T(8,128)(2,1)} %grad_ref.3, f32[256,256]{1,0:T(8,128)S(1)} %get-tuple-element.24.ortho_ref, f32[16,112,256]{2,1,0:T(8,128)} %copy-done.5, ...), custom_call_target="tpu_custom_call" | custom-call | flops 469762048 | bytes 16515072 | tf_op jit(solution)/shard_map/pallas_call | solution.py:289
  166.8 0.6 all-to-all-done.5.got_ref
  167.4 5.3 %shard_map.73 = (bf16[256,3584]{1,0:T(8,128)(2,1)}, f32[112,256]{1,0:T(8,128)}) custom-call(s32[1]{0:T(128)} %bitcast.4.chip_ref, bf16[256,3584]{1,0:T(8,128)(2,1)} %weight_ref.1, f32[16,8,256]{2,1,0:T(8,128)S(1)} %all-to-all-done.5.got_ref, f32[256,256]{1,0:T(8,128)S(1)} %get-tuple-element.24.ortho_ref, f32[16,112,256]{2,1,0:T(8,128)} %copy-done.5, ...), custom_call_target="tpu_custom_call" | custom-call | flops 1409286144 | bytes 7340032 | tf_op jit(solution)/shard_map/pallas_call | solution.py:350
  (3 shorter events, 0.1 us)
Async XLA Ops:
  2.9 31.4 %all-to-all-start = ((f32[16,112,256]{2,1,0:T(8,128)}), f32[16,112,256]{2,1,0:T(8,128)S(1)}, u32[]{:S(2)}, u32[]{:S(2)}) async-start(f32[16,112,256]{2,1,0:T(8,128)} %broadcast_in_dim.6), calls=%async_computation | async-start | bytes 3670016 | tf_op jit(solution)/shard_map/all_to_all | solution.py:439
  10.5 2.0 %copy-start = (f32[256,3584]{1,0:T(8,128)S(1)}, f32[256,3584]{1,0:T(8,128)}, u32[]{:S(2)}) copy-start(f32[256,3584]{1,0:T(8,128)} %mom_ref.3) | copy-start | bytes 11010052
  12.6 1.5 copy-start.1
  20.9 1.2 copy-start.2
  22.1 2.3 %collective-permute-start = (f32[64,1792]{1,0:T(8,128)S(1)}, f32[64,1792]{1,0:T(8,128)S(1)}, u32[]{:S(2)}, u32[]{:S(2)}) collective-permute-start(f32[64,1792]{1,0:T(8,128)S(1)} %get-tuple-element.20), channel_id=1, source_target_pairs={{0,8},{8,0},{1,9},{9,1},{2,10},{10,2},{3,11},{11,3},{4,12},{12,4},... | collective-permute-start | bytes 1376264 | tf_op jit(solution)/shard_map/ppermute | solution.py:434
  23.0 2.1 %collective-permute-start.1 = (f32[64,1792]{1,0:T(8,128)S(1)}, f32[64,1792]{1,0:T(8,128)S(1)}, u32[]{:S(2)}, u32[]{:S(2)}) collective-permute-start(f32[64,1792]{1,0:T(8,128)S(1)} %get-tuple-element.21), channel_id=1, source_target_pairs={{0,8},{8,0},{1,9},{9,1},{2,10},{10,2},{3,11},{11,3},{4,12},{12,4},... | collective-permute-start | bytes 1376264 | tf_op jit(solution)/shard_map/ppermute | solution.py:434
  23.0 2.8 %collective-permute-start.2 = (f32[64,1792]{1,0:T(8,128)S(1)}, f32[64,1792]{1,0:T(8,128)S(1)}, u32[]{:S(2)}, u32[]{:S(2)}) collective-permute-start(f32[64,1792]{1,0:T(8,128)S(1)} %get-tuple-element.22), channel_id=1, source_target_pairs={{0,8},{8,0},{1,9},{9,1},{2,10},{10,2},{3,11},{11,3},{4,12},{12,4},... | collective-permute-start | bytes 1376264 | tf_op jit(solution)/shard_map/ppermute | solution.py:434
  23.5 2.9 %collective-permute-start.3 = (f32[64,1792]{1,0:T(8,128)S(1)}, f32[64,1792]{1,0:T(8,128)S(1)}, u32[]{:S(2)}, u32[]{:S(2)}) collective-permute-start(f32[64,1792]{1,0:T(8,128)S(1)} %get-tuple-element.23), channel_id=1, source_target_pairs={{0,8},{8,0},{1,9},{9,1},{2,10},{10,2},{3,11},{11,3},{4,12},{12,4},... | collective-permute-start | bytes 1376264 | tf_op jit(solution)/shard_map/ppermute | solution.py:434
  26.4 0.8 copy-start.6
  34.4 1.0 copy-start.7
  35.4 6.3 %copy-start.3 = (f32[256,1792]{1,0:T(8,128)S(1)}, f32[256,1792]{1,0:T(8,128)}, u32[]{:S(2)}) copy-start(f32[256,1792]{1,0:T(8,128)} %copy-done.2) | copy-start | bytes 5505028
  37.4 5.4 %collective-permute-start.4 = (f32[256,256]{1,0:T(8,128)S(1)}, f32[256,256]{1,0:T(8,128)S(1)}, u32[]{:S(2)}, u32[]{:S(2)}) collective-permute-start(f32[256,256]{1,0:T(8,128)S(1)} %shard_map.69), channel_id=1, source_target_pairs={{0,8},{8,0},{1,9},{9,1},{2,10},{10,2},{3,11},{11,3},{4,12},{12,4},... | collective-permute-start | bytes 786440 | tf_op jit(solution)/shard_map/ppermute | solution.py:434
  42.5 36.8 %copy-start.4 = (f32[256,1792]{1,0:T(8,128)S(1)}, f32[256,1792]{1,0:T(8,128)}, u32[]{:S(2)}) copy-start(f32[256,1792]{1,0:T(8,128)} %copy-done.2) | copy-start | bytes 5505028
  75.9 3.4 %collective-permute-start.5 = (f32[256,256]{1,0:T(8,128)S(1)}, f32[256,256]{1,0:T(8,128)S(1)}, u32[]{:S(2)}, u32[]{:S(2)}) collective-permute-start(f32[256,256]{1,0:T(8,128)S(1)} %bitcast.7), channel_id=1, source_target_pairs={{0,8},{8,0},{1,9},{9,1},{2,10},{10,2},{3,11},{11,3},{4,12},{12,4},... | collective-permute-start | bytes 786440 | tf_op jit(solution)/shard_map/ppermute | solution.py:434
  79.4 1.0 copy-start.8
  153.5 6.8 %copy-start.5 = (f32[16,112,256]{2,1,0:T(8,128)}, f32[16,112,256]{2,1,0:T(8,128)S(1)}, u32[]{:S(2)}) copy-start(f32[16,112,256]{2,1,0:T(8,128)S(1)} %get-tuple-element.25.own_ref.back_ref) | copy-start | bytes 5505028
  153.5 6.8 %collective-permute-start.6 = (f32[16,112,256]{2,1,0:T(8,128)S(1)}, f32[16,112,256]{2,1,0:T(8,128)}, u32[]{:S(2)}, u32[]{:S(2)}) collective-permute-start(f32[16,112,256]{2,1,0:T(8,128)S(1)} %get-tuple-element.25.own_ref.back_ref), channel_id=1, source_target_pairs={{0,8},{8,0},{1,9},{9,1},{2,10},{10,2},{3,11},{11,3},{4,12},{12,4},... | collective-permute-start | bytes 5505032 | tf_op jit(solution)/shard_map/ppermute | solution.py:434
  156.7 10.7 %all-to-all-start.5 = ((f32[16,8,256]{2,1,0:T(8,128)}), f32[16,8,256]{2,1,0:T(8,128)S(1)}, u32[]{:S(2)}, u32[]{:S(2)}) async-start(f32[16,8,256]{2,1,0:T(8,128)} %get-tuple-element.27), calls=%async_computation.5 | async-start | bytes 262144 | tf_op jit(solution)/shard_map/all_to_all | solution.py:469

commit v7 on v6

--- a/solution.py
+++ b/solution.py
@@ -370,10 +370,9 @@
 def project_kernel(right_ref, *refs):
     left_refs, out_ref = refs[:-1], refs[-1]
     b_hi, b_lo = split(right_ref[...])
-    rows = left_refs[0].shape[0]
-    for i, left_ref in enumerate(left_refs):
-        a_hi, a_lo = split(left_ref[...])
-        out_ref[i * rows : (i + 1) * rows, :] = nn(a_hi, b_hi) + nn(a_hi, b_lo) + nn(a_lo, b_hi)
+    left = jnp.concatenate([left_ref[...] for left_ref in left_refs], axis=0)
+    a_hi, a_lo = split(left)
+    out_ref[...] = nn(a_hi, b_hi) + nn(a_hi, b_lo) + nn(a_lo, b_hi)
 
 
 def project(lefts, right):

time: 173 us -> 171 us (0.988)
  blocking collectives: 93.2 us -> 91.4 us
where the time goes in v7:
time: 171 us
  blocking collectives  91.4 us (53%)
  Pallas kernels  33 us (19%)
  starting transfers between devices  23 us (13%)
  waiting for transfers between devices  12.2 us (7%)
  local copies, waits for them, and re-layouts  10.1 us (6%)
    all_to_all x2, blocking collectives, gather(): return lax.all_to_all(spread, axes, 0, 0)  41.7 us
    all_to_all x1, blocking collectives, per_device(): summed = jnp.sum(lax.all_to_all(packed, plane, 0, 0), axis=0)  30.5 us
    all_to_all x1, blocking collectives, per_device(): lax.all_to_all(partial.reshape(depth, share, rank), 'z', 0, 0)  19.2 us
    ppermute x7, starting transfers between devices, across_cores(): return lax.ppermute(x, 'c', [(0, 1), (1, 0)])  12 us
    pallas_call x1, Pallas kernels, factor(): pl.pallas_call(factor_kernel, out_shape=[jax.ShapeDtypeStruct((chips, pac...  10.5 us
    all_to_all x1, starting transfers between devices, gather(): return lax.all_to_all(spread, axes, 0, 0)  7.58 us
    unnamed x18, local copies, waits for them, and re-layouts  7.58 us
    all_to_all x1, waiting for transfers between devices, gather(): return lax.all_to_all(spread, axes, 0, 0)  7.18 us
  transfers between devices with their start and end apart: 9, of which 9 were waited for; matrix products, arithmetic and copies ran while one was open for 0% of the time, Pallas kernels for 8%

profile of v7, /device:TPU:1, one launch (start us, length us, event | category | flops | bytes accessed | tf_op | source)
XLA Modules:
  0.0 170.9 jit_solution(7187160289624972791)
XLA Ops:
  0.6 2.3 %broadcast_in_dim.6 = f32[16,112,256]{2,1,0:T(8,128)} broadcast(f32[112,256]{1,0:T(8,128)} %param.7), dimensions={1,2} | broadcast | bytes 1949696 | tf_op jit(solution)/shard_map/broadcast_in_dim | solution.py:437
  2.9 7.6 %all-to-all-start = ((f32[16,112,256]{2,1,0:T(8,128)}), f32[16,112,256]{2,1,0:T(8,128)S(1)}, u32[]{:S(2)}, u32[]{:S(2)}) async-start(f32[16,112,256]{2,1,0:T(8,128)} %broadcast_in_dim.6), calls=%async_computation | async-start | bytes 3670016 | tf_op jit(solution)/shard_map/all_to_all | solution.py:438
  10.5 0.0 copy-start
  10.5 2.0 %copy-done = f32[256,3584]{1,0:T(8,128)S(1)} copy-done((f32[256,3584]{1,0:T(8,128)S(1)}, f32[256,3584]{1,0:T(8,128)}, u32[]{:S(2)}) %copy-start) | copy-done | bytes 3670040
  12.6 0.0 copy-start.1
  12.6 1.5 copy-done.1
  14.1 6.8 %shard_map.67 = (f32[256,1792]{1,0:T(8,128)S(1)}, f32[64,1792]{1,0:T(8,128)S(1)}, f32[64,1792]{1,0:T(8,128)S(1)}, f32[64,1792]{1,0:T(8,128)S(1)}, f32[64,1792]{1,0:T(8,128)S(1)}) custom-call(s32[1]{0:T(128)} %bitcast.core_ref, f32[256,3584]{1,0:T(8,128)S(1)} %copy-done, bf16[256,3584]{1,0:T(8,128)(2,1)S(1)} %copy-done.1), custom_call_target="tpu_custom_call" | custom-call | flops 917504 | bytes 9175040 | tf_op jit(solution)/shard_map/pallas_call | solution.py:87
  20.9 0.0 copy-start.2
  20.9 1.2 copy-done.2
  22.1 0.9 collective-permute-start
  23.0 0.0 collective-permute-start.1
  23.0 0.5 collective-permute-start.2
  23.5 0.0 collective-permute-start.3
  23.5 0.9 collective-permute-done.refs_0_.refs_1_
  24.5 0.7 collective-permute-done.1.refs_1_.refs_2_
  25.1 0.7 collective-permute-done.2.refs_2_.refs_3_
  25.8 0.7 collective-permute-done.3.refs_3_.refs_4_
  26.4 0.0 copy-start.6
  26.4 0.8 copy-done.6
  27.2 7.2 %all-to-all-done = f32[16,112,256]{2,1,0:T(8,128)S(1)} async-done(((f32[16,112,256]{2,1,0:T(8,128)}), f32[16,112,256]{2,1,0:T(8,128)S(1)}, u32[]{:S(2)}, u32[]{:S(2)}) %all-to-all-start) | async-done | bytes 1835040 | tf_op jit(solution)/shard_map/all_to_all | solution.py:438
  34.4 0.0 copy-start.7
  34.4 1.0 copy-done.7
  35.4 0.0 copy-start.3
  35.4 0.9 shard_map.69
  36.3 4.2 %collective-permute-start.4 = (f32[256,256]{1,0:T(8,128)S(1)}, f32[256,256]{1,0:T(8,128)S(1)}, u32[]{:S(2)}, u32[]{:S(2)}) collective-permute-start(f32[256,256]{1,0:T(8,128)S(1)} %shard_map.69), channel_id=1, source_target_pairs={{0,8},{8,0},{1,9},{9,1},{2,10},{10,2},{3,11},{11,3},{4,12},{12,4},... | collective-permute-start | bytes 786440 | tf_op jit(solution)/shard_map/ppermute | solution.py:433
  40.5 0.0 copy-done.3
  40.5 0.9 shard_map.68
  41.4 0.0 copy-start.4
  41.4 0.3 collective-permute-done.4
  41.7 19.2 %all_to_all.30 = f32[8,32,256]{2,1,0:T(8,128)S(1)} all-to-all(f32[8,32,256]{2,1,0:T(8,128)S(1)} %bitcast.10), channel_id=1, replica_groups=mesh['x'=4,'y'=4,'c'=2,'z'=8] {'z'}, dimensions={0} | all-to-all | bytes 524288 | tf_op jit(solution)/shard_map/all_to_all | solution.py:459
  61.0 12.1 %all_to_all.31 = f32[8,32,256]{2,1,0:T(8,128)S(1)} all-to-all(f32[8,32,256]{2,1,0:T(8,128)S(1)} %broadcast_in_dim.7), channel_id=1, replica_groups=mesh['x'=4,'y'=4,'c'=2,'z'=8] {'z'}, dimensions={0} | all-to-all | bytes 524288 | tf_op jit(solution)/shard_map/all_to_all | solution.py:438
  73.0 3.2 %collective-permute-start.5 = (f32[256,256]{1,0:T(8,128)S(1)}, f32[256,256]{1,0:T(8,128)S(1)}, u32[]{:S(2)}, u32[]{:S(2)}) collective-permute-start(f32[256,256]{1,0:T(8,128)S(1)} %bitcast.7), channel_id=1, source_target_pairs={{0,8},{8,0},{1,9},{9,1},{2,10},{10,2},{3,11},{11,3},{4,12},{12,4},... | collective-permute-start | bytes 786440 | tf_op jit(solution)/shard_map/ppermute | solution.py:433
  76.2 1.2 collective-permute-done.5.other_ref
  77.4 0.0 copy-done.4
  77.4 0.0 copy-start.8
  77.4 1.0 copy-done.8
  78.4 2.2 %shard_map.70 = f32[16,128,256]{2,1,0:T(8,128)S(1)} custom-call(f32[256,256]{1,0:T(8,128)S(1)} %bitcast.8, f32[256,256]{1,0:T(8,128)S(1)} %collective-permute-done.5.other_ref, f32[256,1792]{1,0:T(8,128)S(1)} %copy-done.4, f32[64,1792]{1,0:T(8,128)S(1)} %collective-permute-done.refs_0_.refs_1_, f32[64,1792]{1,0:T(8,128)S(1)} %collective-permute-done.1.refs_1_.refs_2_, ...), custom_call_target="tpu_custom_call" | custom-call | flops 1409286144 | bytes 3670016 | tf_op jit(solution)/shard_map/pallas_call | solution.py:420
  80.6 30.5 %all_to_all.32 = f32[16,128,256]{2,1,0:T(8,128)S(1)} all-to-all(f32[16,128,256]{2,1,0:T(8,128)S(1)} %shard_map.70), channel_id=1, replica_groups=mesh['x'=4,'y'=4,'c'=2,'z'=8] {'x','y'}, dimensions={0} | all-to-all | bytes 4194304 | tf_op jit(solution)/shard_map/all_to_all | solution.py:464
  111.1 0.1 reduce_sum.19
  111.2 0.2 broadcast_in_dim.8
  111.4 29.6 %all_to_all.33.got_ref = f32[16,128,256]{2,1,0:T(8,128)S(1)} all-to-all(f32[16,128,256]{2,1,0:T(8,128)S(1)} %broadcast_in_dim.8), channel_id=1, replica_groups=mesh['x'=4,'y'=4,'c'=2,'z'=8] {'x','y'}, dimensions={0} | all-to-all | bytes 4194304 | tf_op jit(solution)/shard_map/all_to_all | solution.py:438
  141.0 10.5 %shard_map.71 = (f32[16,112,256]{2,1,0:T(8,128)S(1)}, f32[256,256]{1,0:T(8,128)S(1)}, f32[16,8,256]{2,1,0:T(8,128)}) custom-call(f32[16,128,256]{2,1,0:T(8,128)S(1)} %all_to_all.33.got_ref, f32[256,256]{1,0:T(8,128)S(1)} %bitcast.9), custom_call_target="tpu_custom_call" | custom-call | flops 671088640 | bytes 1048576 | tf_op jit(solution)/shard_map/pallas_call | solution.py:219
  151.5 0.0 copy-start.5
  151.5 3.2 %collective-permute-start.6 = (f32[16,112,256]{2,1,0:T(8,128)S(1)}, f32[16,112,256]{2,1,0:T(8,128)}, u32[]{:S(2)}, u32[]{:S(2)}) collective-permute-start(f32[16,112,256]{2,1,0:T(8,128)S(1)} %get-tuple-element.25.own_ref.back_ref), channel_id=1, source_target_pairs={{0,8},{8,0},{1,9},{9,1},{2,10},{10,2},{3,11},{11,3},{4,12},{12,4},... | collective-permute-start | bytes 5505032 | tf_op jit(solution)/shard_map/ppermute | solution.py:433
  154.7 3.4 %all-to-all-start.5 = ((f32[16,8,256]{2,1,0:T(8,128)}), f32[16,8,256]{2,1,0:T(8,128)S(1)}, u32[]{:S(2)}, u32[]{:S(2)}) async-start(f32[16,8,256]{2,1,0:T(8,128)} %get-tuple-element.27), calls=%async_computation.5 | async-start | bytes 262144 | tf_op jit(solution)/shard_map/all_to_all | solution.py:468
  158.1 0.1 collective-permute-done.6.other_ref
  158.3 0.0 copy-done.5
  158.3 6.5 %shard_map.72 = (f32[256,3584]{1,0:T(8,128)}, bf16[3584,256]{1,0:T(8,128)(2,1)}, bf16[3584,256]{1,0:T(8,128)(2,1)}) custom-call(s32[1]{0:T(128)} %bitcast.core_ref, f32[256,3584]{1,0:T(8,128)} %mom_ref.3, bf16[256,3584]{1,0:T(8,128)(2,1)} %grad_ref.3, f32[256,256]{1,0:T(8,128)S(1)} %get-tuple-element.24.ortho_ref, f32[16,112,256]{2,1,0:T(8,128)} %copy-done.5, ...), custom_call_target="tpu_custom_call" | custom-call | flops 469762048 | bytes 16515072 | tf_op jit(solution)/shard_map/pallas_call | solution.py:289
  164.8 0.6 all-to-all-done.5.got_ref
  165.4 5.3 %shard_map.73 = (bf16[256,3584]{1,0:T(8,128)(2,1)}, f32[112,256]{1,0:T(8,128)}) custom-call(s32[1]{0:T(128)} %bitcast.4.chip_ref, bf16[256,3584]{1,0:T(8,128)(2,1)} %weight_ref.1, f32[16,8,256]{2,1,0:T(8,128)S(1)} %all-to-all-done.5.got_ref, f32[256,256]{1,0:T(8,128)S(1)} %get-tuple-element.24.ortho_ref, f32[16,112,256]{2,1,0:T(8,128)} %copy-done.5, ...), custom_call_target="tpu_custom_call" | custom-call | flops 1409286144 | bytes 7340032 | tf_op jit(solution)/shard_map/pallas_call | solution.py:350
  (3 shorter events, 0.1 us)
Async XLA Ops:
  2.9 31.4 %all-to-all-start = ((f32[16,112,256]{2,1,0:T(8,128)}), f32[16,112,256]{2,1,0:T(8,128)S(1)}, u32[]{:S(2)}, u32[]{:S(2)}) async-start(f32[16,112,256]{2,1,0:T(8,128)} %broadcast_in_dim.6), calls=%async_computation | async-start | bytes 3670016 | tf_op jit(solution)/shard_map/all_to_all | solution.py:438
  10.5 2.0 %copy-start = (f32[256,3584]{1,0:T(8,128)S(1)}, f32[256,3584]{1,0:T(8,128)}, u32[]{:S(2)}) copy-start(f32[256,3584]{1,0:T(8,128)} %mom_ref.3) | copy-start | bytes 11010052
  12.6 1.5 copy-start.1
  20.9 1.2 copy-start.2
  22.1 2.3 %collective-permute-start = (f32[64,1792]{1,0:T(8,128)S(1)}, f32[64,1792]{1,0:T(8,128)S(1)}, u32[]{:S(2)}, u32[]{:S(2)}) collective-permute-start(f32[64,1792]{1,0:T(8,128)S(1)} %get-tuple-element.20), channel_id=1, source_target_pairs={{0,8},{8,0},{1,9},{9,1},{2,10},{10,2},{3,11},{11,3},{4,12},{12,4},... | collective-permute-start | bytes 1376264 | tf_op jit(solution)/shard_map/ppermute | solution.py:433
  23.0 2.1 %collective-permute-start.1 = (f32[64,1792]{1,0:T(8,128)S(1)}, f32[64,1792]{1,0:T(8,128)S(1)}, u32[]{:S(2)}, u32[]{:S(2)}) collective-permute-start(f32[64,1792]{1,0:T(8,128)S(1)} %get-tuple-element.21), channel_id=1, source_target_pairs={{0,8},{8,0},{1,9},{9,1},{2,10},{10,2},{3,11},{11,3},{4,12},{12,4},... | collective-permute-start | bytes 1376264 | tf_op jit(solution)/shard_map/ppermute | solution.py:433
  23.0 2.8 %collective-permute-start.2 = (f32[64,1792]{1,0:T(8,128)S(1)}, f32[64,1792]{1,0:T(8,128)S(1)}, u32[]{:S(2)}, u32[]{:S(2)}) collective-permute-start(f32[64,1792]{1,0:T(8,128)S(1)} %get-tuple-element.22), channel_id=1, source_target_pairs={{0,8},{8,0},{1,9},{9,1},{2,10},{10,2},{3,11},{11,3},{4,12},{12,4},... | collective-permute-start | bytes 1376264 | tf_op jit(solution)/shard_map/ppermute | solution.py:433
  23.5 2.9 %collective-permute-start.3 = (f32[64,1792]{1,0:T(8,128)S(1)}, f32[64,1792]{1,0:T(8,128)S(1)}, u32[]{:S(2)}, u32[]{:S(2)}) collective-permute-start(f32[64,1792]{1,0:T(8,128)S(1)} %get-tuple-element.23), channel_id=1, source_target_pairs={{0,8},{8,0},{1,9},{9,1},{2,10},{10,2},{3,11},{11,3},{4,12},{12,4},... | collective-permute-start | bytes 1376264 | tf_op jit(solution)/shard_map/ppermute | solution.py:433
  26.4 0.8 copy-start.6
  34.4 1.0 copy-start.7
  35.4 5.1 %copy-start.3 = (f32[256,1792]{1,0:T(8,128)S(1)}, f32[256,1792]{1,0:T(8,128)}, u32[]{:S(2)}) copy-start(f32[256,1792]{1,0:T(8,128)} %copy-done.2) | copy-start | bytes 5505028
  36.3 5.4 %collective-permute-start.4 = (f32[256,256]{1,0:T(8,128)S(1)}, f32[256,256]{1,0:T(8,128)S(1)}, u32[]{:S(2)}, u32[]{:S(2)}) collective-permute-start(f32[256,256]{1,0:T(8,128)S(1)} %shard_map.69), channel_id=1, source_target_pairs={{0,8},{8,0},{1,9},{9,1},{2,10},{10,2},{3,11},{11,3},{4,12},{12,4},... | collective-permute-start | bytes 786440 | tf_op jit(solution)/shard_map/ppermute | solution.py:433
  41.4 36.0 %copy-start.4 = (f32[256,1792]{1,0:T(8,128)S(1)}, f32[256,1792]{1,0:T(8,128)}, u32[]{:S(2)}) copy-start(f32[256,1792]{1,0:T(8,128)} %copy-done.2) | copy-start | bytes 5505028
  73.0 4.3 %collective-permute-start.5 = (f32[256,256]{1,0:T(8,128)S(1)}, f32[256,256]{1,0:T(8,128)S(1)}, u32[]{:S(2)}, u32[]{:S(2)}) collective-permute-start(f32[256,256]{1,0:T(8,128)S(1)} %bitcast.7), channel_id=1, source_target_pairs={{0,8},{8,0},{1,9},{9,1},{2,10},{10,2},{3,11},{11,3},{4,12},{12,4},... | collective-permute-start | bytes 786440 | tf_op jit(solution)/shard_map/ppermute | solution.py:433
  77.4 1.0 copy-start.8
  151.5 6.8 %copy-start.5 = (f32[16,112,256]{2,1,0:T(8,128)}, f32[16,112,256]{2,1,0:T(8,128)S(1)}, u32[]{:S(2)}) copy-start(f32[16,112,256]{2,1,0:T(8,128)S(1)} %get-tuple-element.25.own_ref.back_ref) | copy-start | bytes 5505028
  151.5 6.8 %collective-permute-start.6 = (f32[16,112,256]{2,1,0:T(8,128)S(1)}, f32[16,112,256]{2,1,0:T(8,128)}, u32[]{:S(2)}, u32[]{:S(2)}) collective-permute-start(f32[16,112,256]{2,1,0:T(8,128)S(1)} %get-tuple-element.25.own_ref.back_ref), channel_id=1, source_target_pairs={{0,8},{8,0},{1,9},{9,1},{2,10},{10,2},{3,11},{11,3},{4,12},{12,4},... | collective-permute-start | bytes 5505032 | tf_op jit(solution)/shard_map/ppermute | solution.py:433
  154.7 10.7 %all-to-all-start.5 = ((f32[16,8,256]{2,1,0:T(8,128)}), f32[16,8,256]{2,1,0:T(8,128)S(1)}, u32[]{:S(2)}, u32[]{:S(2)}) async-start(f32[16,8,256]{2,1,0:T(8,128)} %get-tuple-element.27), calls=%async_computation.5 | async-start | bytes 262144 | tf_op jit(solution)/shard_map/all_to_all | solution.py:468
